TPU v7x, 32 devices: a whole 2x2x4 slice. The times are simulated.
32 devices in a mesh: fsdp: 8 (over y, x, core), dp: 4 (over z).
Axes of the slice: x: 2, y: 2, z: 4, core: 2. Of those that a mesh axis runs over, the one named last changes fastest.
Arguments:
- tokens: bfloat16 [32768, 960], P(('fsdp', 'dp')), may hold values from -6 to 6
- first_len: int32 [32], P(('fsdp', 'dp')), may hold values from 256 to 1024, as said below
- gain_attn: bfloat16 [960], P('fsdp'), may hold values from 0.099609375 to 1.8984375
- w_query: bfloat16 [960, 960], P('fsdp', 'dp'), may hold values from -0.1875 to 0.1875
- w_key: bfloat16 [960, 320], P('fsdp', 'dp'), may hold values from -0.1875 to 0.1875
- w_value: bfloat16 [960, 320], P('fsdp', 'dp'), may hold values from -0.1875 to 0.1875
- w_out: bfloat16 [960, 960], P('fsdp', 'dp'), may hold values from -1.5 to 1.5
- gain_mlp: bfloat16 [960], P('fsdp'), may hold values from 0.099609375 to 1.8984375
- w_gate: bfloat16 [960, 2560], P('fsdp', 'dp'), may hold values from -0.1875 to 0.1875
- w_up: bfloat16 [960, 2560], P('fsdp', 'dp'), may hold values from -0.1875 to 0.1875
- w_down: bfloat16 [2560, 960], P('fsdp', 'dp'), may hold values from -0.125 to 0.125
- cotangent: bfloat16 [32768, 960], P(('fsdp', 'dp')), may hold values from -6 to 6
Outputs:
- mixed: bfloat16 [32768, 960], P(('fsdp', 'dp'))
- grad_tokens: bfloat16 [32768, 960], P(('fsdp', 'dp'))
- grad_gain_attn: float32 [960], P('fsdp')
- grad_query: float32 [960, 960], P('fsdp', 'dp')
- grad_key: float32 [960, 320], P('fsdp', 'dp')
- grad_value: float32 [960, 320], P('fsdp', 'dp')
- grad_out: float32 [960, 960], P('fsdp', 'dp')
- grad_gain_mlp: float32 [960], P('fsdp')
- grad_gate: float32 [960, 2560], P('fsdp', 'dp')
- grad_up: float32 [960, 2560], P('fsdp', 'dp')
- grad_down: float32 [2560, 960], P('fsdp', 'dp')
Inputs may be any that keep to these rules, and one draw needn't show every extreme that they name: `first_len`: every entry is a multiple of 128; either it equals 1024 (the group holds one sequence) or it and 1024 minus it are both at least 256; at least one group holds a single sequence.
All inputs are finite; a program needn't handle non-finite values.
Results may differ from a plain program's by a relative error of at most 0.02.
Values may be sent and summed in bfloat16 or wider, within the bound.
No kernel may reach another device: no remote copies, remote signals or barrier semaphores. Data moves between devices by JAX's collectives and lax.ppermute only.
A program may use at most 320 MiB of HBM per device.

v0:
```python
import jax
import jax.numpy as jnp
from jax import lax
from jax.sharding import PartitionSpec as P

D = 960
HEADS = 15
KV_HEADS = 5
HEAD_DIM = 64
QBLK = 512


epsilon = 1e-05
rope_base = 10000.0


def rms_scale(values, gain):
    inverse = lax.rsqrt(jnp.mean(values * values, axis=-1, keepdims=True) + epsilon)
    return values * inverse * gain


def rotate(values, cosine, sine):
    middle = values.shape[-1] // 2
    turned = jnp.concatenate([-values[..., middle:], values[..., :middle]], axis=-1)
    return values * cosine + turned * sine


def unrotate(grads, cosine, sine):
    middle = grads.shape[-1] // 2
    scaled = grads * sine
    turned = jnp.concatenate([scaled[..., middle:], -scaled[..., :middle]], axis=-1)
    return grads * cosine + turned


def rope_tables(first, length):
    places = jnp.arange(length, dtype=jnp.int32)
    position = jnp.where(places < first, places, places - first).astype(jnp.float32)
    frequency = rope_base ** (-jnp.arange(0, HEAD_DIM, 2, dtype=jnp.float32) / HEAD_DIM)
    angles = position[:, None] * frequency[None, :]
    angles = jnp.concatenate([angles, angles], axis=-1)
    return (jnp.cos(angles)[:, None, :], jnp.sin(angles)[:, None, :])


def product(left, right):
    return jnp.dot(left, right, preferred_element_type=jnp.float32)


def product_left(left, right):
    return lax.dot_general(
        left, right, (((0,), (0,)), ((), ())), preferred_element_type=jnp.float32
    )


def product_right(left, right):
    return lax.dot_general(
        left, right, (((1,), (1,)), ((), ())), preferred_element_type=jnp.float32
    )


def allowed_mask(first, row_start, rows, columns):
    query_place = row_start + jnp.arange(rows, dtype=jnp.int32)[:, None]
    key_place = jnp.arange(columns, dtype=jnp.int32)[None, :]
    return (key_place <= query_place) & ((key_place >= first) | (query_place < first))


def swiglu(gating, rising):
    return jax.nn.silu(gating) * rising


def on_device(
    tokens,
    first_len,
    gain_attn,
    w_query,
    w_key,
    w_value,
    w_out,
    gain_mlp,
    w_gate,
    w_up,
    w_down,
    cotangent,
):
    length = tokens.shape[0]
    first = first_len[0]
    groups = HEADS // KV_HEADS
    scale = HEAD_DIM ** (-0.5)
    kv_width = KV_HEADS * HEAD_DIM
    blocks = length // QBLK
    cosine, sine = rope_tables(first, length)
    attention_part = (
        lax.all_gather(w_query, "dp", axis=1, tiled=True),
        lax.all_gather(w_key, "dp", axis=1, tiled=True),
        lax.all_gather(w_value, "dp", axis=1, tiled=True),
        lax.all_gather(w_out, "dp", axis=1, tiled=True),
    )
    attention_full = (
        lax.all_gather(attention_part[0], "fsdp", axis=0, tiled=True),
        lax.all_gather(attention_part[1], "fsdp", axis=0, tiled=True),
        lax.all_gather(attention_part[2], "fsdp", axis=0, tiled=True),
        lax.all_gather(attention_part[3], "fsdp", axis=0, tiled=True),
        lax.all_gather(gain_attn, "fsdp", axis=0, tiled=True),
    )
    query_full, key_full, value_full, out_full, gain_one = attention_full
    gain_one32 = gain_one.astype(jnp.float32)
    inputs = tokens.astype(jnp.float32)
    normed_one = rms_scale(inputs, gain_one32).astype(jnp.bfloat16)
    queries = product(normed_one, query_full).reshape(length, HEADS, HEAD_DIM)
    queries = rotate(queries, cosine, sine).astype(jnp.bfloat16)
    grouped = queries.reshape(length, KV_HEADS, groups, HEAD_DIM)
    keys = product(normed_one, key_full).reshape(length, KV_HEADS, HEAD_DIM)
    keys = rotate(keys, cosine, sine).astype(jnp.bfloat16)
    values = (
        product(normed_one, value_full).astype(jnp.bfloat16).reshape(length, KV_HEADS, HEAD_DIM)
    )

    def block_scores(index):
        start = index * QBLK
        span = start + QBLK
        raw = (
            jnp.einsum(
                "qkgd,skd->kgqs",
                grouped[start:span],
                keys[:span],
                preferred_element_type=jnp.float32,
            )
            * scale
        )
        return jnp.where(allowed_mask(first, start, QBLK, span), raw, -1e30)

    pieces = []
    log_totals = []
    for index in range(blocks):
        span = (index + 1) * QBLK
        scores = block_scores(index)
        highest = jnp.max(scores, axis=-1, keepdims=True)
        weights_exp = jnp.exp(scores - highest)
        total = jnp.sum(weights_exp, axis=-1, keepdims=True)
        probs = (weights_exp / total).astype(jnp.bfloat16)
        pieces.append(
            jnp.einsum(
                "kgqs,skd->qkgd", probs, values[:span], preferred_element_type=jnp.float32
            ).reshape(QBLK, D)
        )
        log_totals.append(highest + jnp.log(total))
    attended = jnp.concatenate(pieces, axis=0).astype(jnp.bfloat16)
    middle = inputs + product(attended, out_full)
    feed_part = (
        lax.all_gather(w_gate, "dp", axis=1, tiled=True),
        lax.all_gather(w_up, "dp", axis=1, tiled=True),
        lax.all_gather(w_down, "dp", axis=1, tiled=True),
    )
    feed_full = (
        lax.all_gather(feed_part[0], "fsdp", axis=0, tiled=True),
        lax.all_gather(feed_part[1], "fsdp", axis=0, tiled=True),
        lax.all_gather(feed_part[2], "fsdp", axis=0, tiled=True),
        lax.all_gather(gain_mlp, "fsdp", axis=0, tiled=True),
    )
    gate_full, up_full, down_full, gain_two = feed_full
    gain_two32 = gain_two.astype(jnp.float32)
    normed_two = rms_scale(middle, gain_two32).astype(jnp.bfloat16)
    gate = product(normed_two, gate_full)
    upward = product(normed_two, up_full)
    hidden = swiglu(gate, upward).astype(jnp.bfloat16)
    mixed = (middle + product(hidden, down_full)).astype(jnp.bfloat16)
    feed_again = (
        lax.all_gather(w_gate, "dp", axis=1, tiled=True),
        lax.all_gather(w_up, "dp", axis=1, tiled=True),
        lax.all_gather(w_down, "dp", axis=1, tiled=True),
    )
    back_gate, back_up, back_down = (
        lax.all_gather(feed_again[0], "fsdp", axis=0, tiled=True),
        lax.all_gather(feed_again[1], "fsdp", axis=0, tiled=True),
        lax.all_gather(feed_again[2], "fsdp", axis=0, tiled=True),
    )
    attention_again = (
        lax.all_gather(w_query, "dp", axis=1, tiled=True),
        lax.all_gather(w_key, "dp", axis=1, tiled=True),
        lax.all_gather(w_value, "dp", axis=1, tiled=True),
        lax.all_gather(w_out, "dp", axis=1, tiled=True),
    )
    back_query, back_key, back_value, back_out = (
        lax.all_gather(attention_again[0], "fsdp", axis=0, tiled=True),
        lax.all_gather(attention_again[1], "fsdp", axis=0, tiled=True),
        lax.all_gather(attention_again[2], "fsdp", axis=0, tiled=True),
        lax.all_gather(attention_again[3], "fsdp", axis=0, tiled=True),
    )
    upstream = cotangent.astype(jnp.float32)
    grad_down_w = product_left(hidden, cotangent)
    grad_hidden = product_right(cotangent, back_down)
    unused, swiglu_pull = jax.vjp(swiglu, gate, upward)
    grad_gating, grad_rising = swiglu_pull(grad_hidden)
    grad_gating = grad_gating.astype(jnp.bfloat16)
    grad_rising = grad_rising.astype(jnp.bfloat16)
    grad_gate_w = product_left(normed_two, grad_gating)
    grad_up_w = product_left(normed_two, grad_rising)
    grad_normed_two = product_right(grad_gating, back_gate) + product_right(grad_rising, back_up)
    unused, second_pull = jax.vjp(rms_scale, middle, gain_two32)
    grad_middle_norm, grad_gain_two = second_pull(grad_normed_two)
    grad_middle = upstream + grad_middle_norm
    feed_rows = (
        lax.psum_scatter(
            grad_gate_w.astype(jnp.bfloat16), "fsdp", scatter_dimension=0, tiled=True
        ).astype(jnp.float32),
        lax.psum_scatter(
            grad_up_w.astype(jnp.bfloat16), "fsdp", scatter_dimension=0, tiled=True
        ).astype(jnp.float32),
        lax.psum_scatter(
            grad_down_w.astype(jnp.bfloat16), "fsdp", scatter_dimension=0, tiled=True
        ).astype(jnp.float32),
        lax.psum_scatter(
            grad_gain_two.astype(jnp.bfloat16), "fsdp", scatter_dimension=0, tiled=True
        ).astype(jnp.float32),
    )
    feed_shards = (
        lax.psum_scatter(
            feed_rows[0].astype(jnp.bfloat16), "dp", scatter_dimension=1, tiled=True
        ).astype(jnp.float32),
        lax.psum_scatter(
            feed_rows[1].astype(jnp.bfloat16), "dp", scatter_dimension=1, tiled=True
        ).astype(jnp.float32),
        lax.psum_scatter(
            feed_rows[2].astype(jnp.bfloat16), "dp", scatter_dimension=1, tiled=True
        ).astype(jnp.float32),
    )
    feed_gain = feed_rows[3]
    branch_grad = grad_middle.astype(jnp.bfloat16)
    grad_out_w = product_left(attended, branch_grad)
    grad_attended = (
        product_right(branch_grad, back_out)
        .astype(jnp.bfloat16)
        .reshape(length, KV_HEADS, groups, HEAD_DIM)
    )
    query_grads = []
    grad_keys = jnp.zeros((length, KV_HEADS, HEAD_DIM), jnp.float32)
    grad_values = jnp.zeros((length, KV_HEADS, HEAD_DIM), jnp.float32)
    for index in range(blocks):
        start = index * QBLK
        span = start + QBLK
        probs = jnp.exp(block_scores(index) - log_totals[index])
        grad_block = grad_attended[start:span]
        grad_probs = jnp.einsum(
            "qkgd,skd->kgqs", grad_block, values[:span], preferred_element_type=jnp.float32
        )
        inner = jnp.sum(grad_probs * probs, axis=-1, keepdims=True)
        grad_scores = (probs * (grad_probs - inner)).astype(jnp.bfloat16)
        query_grads.append(
            jnp.einsum(
                "kgqs,skd->qkgd", grad_scores, keys[:span], preferred_element_type=jnp.float32
            )
            * scale
        )
        grad_keys = grad_keys.at[:span].add(
            jnp.einsum(
                "kgqs,qkgd->skd",
                grad_scores,
                grouped[start:span],
                preferred_element_type=jnp.float32,
            )
            * scale
        )
        grad_values = grad_values.at[:span].add(
            jnp.einsum(
                "kgqs,qkgd->skd",
                probs.astype(jnp.bfloat16),
                grad_block,
                preferred_element_type=jnp.float32,
            )
        )
    grad_queries = jnp.concatenate(query_grads, axis=0).reshape(length, HEADS, HEAD_DIM)
    grad_queries = unrotate(grad_queries, cosine, sine).reshape(length, D).astype(jnp.bfloat16)
    grad_keys = unrotate(grad_keys, cosine, sine).reshape(length, kv_width).astype(jnp.bfloat16)
    grad_values = grad_values.reshape(length, kv_width).astype(jnp.bfloat16)
    grad_query_w = product_left(normed_one, grad_queries)
    grad_key_w = product_left(normed_one, grad_keys)
    grad_value_w = product_left(normed_one, grad_values)
    grad_normed_one = (
        product_right(grad_queries, back_query)
        + product_right(grad_keys, back_key)
        + product_right(grad_values, back_value)
    )
    unused, first_pull = jax.vjp(rms_scale, inputs, gain_one32)
    grad_input_norm, grad_gain_one = first_pull(grad_normed_one)
    grad_tokens = (grad_middle + grad_input_norm).astype(jnp.bfloat16)
    attention_rows = (
        lax.psum_scatter(
            grad_query_w.astype(jnp.bfloat16), "fsdp", scatter_dimension=0, tiled=True
        ).astype(jnp.float32),
        lax.psum_scatter(
            grad_key_w.astype(jnp.bfloat16), "fsdp", scatter_dimension=0, tiled=True
        ).astype(jnp.float32),
        lax.psum_scatter(
            grad_value_w.astype(jnp.bfloat16), "fsdp", scatter_dimension=0, tiled=True
        ).astype(jnp.float32),
        lax.psum_scatter(
            grad_out_w.astype(jnp.bfloat16), "fsdp", scatter_dimension=0, tiled=True
        ).astype(jnp.float32),
        lax.psum_scatter(
            grad_gain_one.astype(jnp.bfloat16), "fsdp", scatter_dimension=0, tiled=True
        ).astype(jnp.float32),
    )
    attention_shards = (
        lax.psum_scatter(
            attention_rows[0].astype(jnp.bfloat16), "dp", scatter_dimension=1, tiled=True
        ).astype(jnp.float32),
        lax.psum_scatter(
            attention_rows[1].astype(jnp.bfloat16), "dp", scatter_dimension=1, tiled=True
        ).astype(jnp.float32),
        lax.psum_scatter(
            attention_rows[2].astype(jnp.bfloat16), "dp", scatter_dimension=1, tiled=True
        ).astype(jnp.float32),
        lax.psum_scatter(
            attention_rows[3].astype(jnp.bfloat16), "dp", scatter_dimension=1, tiled=True
        ).astype(jnp.float32),
    )
    gain_totals = lax.psum((attention_rows[4], feed_gain), "dp")
    return (
        mixed,
        grad_tokens,
        gain_totals[0],
        attention_shards[0],
        attention_shards[1],
        attention_shards[2],
        attention_shards[3],
        gain_totals[1],
        feed_shards[0],
        feed_shards[1],
        feed_shards[2],
    )


def solution(mesh):
    in_specs = (
        P(("fsdp", "dp"), None),
        P(("fsdp", "dp")),
        P("fsdp"),
        P("fsdp", "dp"),
        P("fsdp", "dp"),
        P("fsdp", "dp"),
        P("fsdp", "dp"),
        P("fsdp"),
        P("fsdp", "dp"),
        P("fsdp", "dp"),
        P("fsdp", "dp"),
        P(("fsdp", "dp"), None),
    )
    out_specs = (
        P(("fsdp", "dp"), None),
        P(("fsdp", "dp"), None),
        P("fsdp"),
        P("fsdp", "dp"),
        P("fsdp", "dp"),
        P("fsdp", "dp"),
        P("fsdp", "dp"),
        P("fsdp"),
        P("fsdp", "dp"),
        P("fsdp", "dp"),
        P("fsdp", "dp"),
    )
    return jax.shard_map(
        on_device, mesh=mesh, in_specs=in_specs, out_specs=out_specs, check_vma=False
    )
```

profile of v0, /device:TPU:9, one launch (start us, length us, event | category | flops | bytes accessed | tf_op | source)
XLA Modules:
  0.0 907.7 jit_solution(7990659759946313625)
XLA Ops:
  8.2 11.1 %all_gather.67 = bf16[120,960]{0,1:T(8,128)(2,1)S(1)} all-gather(bf16[120,240]{0,1:T(8,128)(2,1)S(1)} %copy.57), channel_id=1, replica_groups=mesh['fsdp'=8,'dp'=4] {'dp'}, dimensions={1}, use_global_device_ids=true | all-gather | bytes 288000 | tf_op jit(solution)/shard_map/all_gather | solution.py:92
  21.2 12.0 %all_gather.69 = bf16[120,960]{0,1:T(8,128)(2,1)S(1)} all-gather(bf16[120,240]{0,1:T(8,128)(2,1)S(1)} %copy.61), channel_id=1, replica_groups=mesh['fsdp'=8,'dp'=4] {'dp'}, dimensions={1}, use_global_device_ids=true | all-gather | bytes 288000 | tf_op jit(solution)/shard_map/all_gather | solution.py:95
  34.1 15.1 %all_gather.74 = bf16[120,2560]{1,0:T(8,128)(2,1)} all-gather(bf16[120,640]{1,0:T(8,128)(2,1)} %param.33), channel_id=1, replica_groups=mesh['fsdp'=8,'dp'=4] {'dp'}, dimensions={1}, use_global_device_ids=true | all-gather | bytes 768000 | tf_op jit(solution)/shard_map/all_gather | solution.py:150
  49.2 14.9 %all_gather.72 = bf16[120,2560]{1,0:T(8,128)(2,1)} all-gather(bf16[120,640]{1,0:T(8,128)(2,1)} %param.32), channel_id=1, replica_groups=mesh['fsdp'=8,'dp'=4] {'dp'}, dimensions={1}, use_global_device_ids=true | all-gather | bytes 768000 | tf_op jit(solution)/shard_map/all_gather | solution.py:149
  64.3 14.6 %all-gather.2 = bf16[4,240,320]{1,2,0:T(8,128)(2,1)S(1)} all-gather(bf16[1,240,320]{1,2,0:T(8,128)(2,1)S(1)} %bitcast.229), channel_id=1, replica_groups=mesh['fsdp'=8,'dp'=4] {'dp'}, dimensions={0}, use_global_device_ids=true | all-gather | bytes 768000 | tf_op jit(solution)/shard_map/all_gather | solution.py:151
  84.9 23.7 %all-reduce.10 = (bf16[960]{0:T(1024)(128)(2,1)S(1)}, bf16[960]{0:T(1024)(128)(2,1)S(1)}) all-reduce(bf16[960]{0:T(1024)(128)(2,1)S(1)} %dynamic-update-slice.10, bf16[960]{0:T(1024)(128)(2,1)S(1)} %dynamic-update-slice.11), channel_id=1, replica_groups=mesh['fsdp'=8,'dp'=4] {'fsdp'}, use_global_device_ids=true, to_apply=%add.2 | all-reduce | flops 1920 | bytes 7680
  109.2 11.5 %all_gather.65 = bf16[120,320]{0,1:T(8,128)(2,1)} all-gather(bf16[120,80]{0,1:T(8,128)(2,1)S(1)} %copy-done.41), channel_id=1, replica_groups=mesh['fsdp'=8,'dp'=4] {'dp'}, dimensions={1}, use_global_device_ids=true | all-gather | bytes 96000 | tf_op jit(solution)/shard_map/all_gather | solution.py:93
  132.5 16.6 %all-gather = bf16[8,120,320]{1,2,0:T(8,128)(2,1)S(1)} all-gather(bf16[1,120,320]{1,2,0:T(8,128)(2,1)S(1)} %bitcast.225), channel_id=1, replica_groups=mesh['fsdp'=8,'dp'=4] {'fsdp'}, dimensions={0}, use_global_device_ids=true | all-gather | bytes 691200 | tf_op jit(solution)/shard_map/all_gather | solution.py:100
  150.0 13.0 %all-gather.1 = bf16[8,120,320]{1,2,0:T(8,128)(2,1)S(1)} all-gather(bf16[1,120,320]{1,2,0:T(8,128)(2,1)} %bitcast.224), channel_id=1, replica_groups=mesh['fsdp'=8,'dp'=4] {'fsdp'}, dimensions={0}, use_global_device_ids=true | all-gather | bytes 691200 | tf_op jit(solution)/shard_map/all_gather | solution.py:99
  201.5 12.8 %fusion.81 = (f32[5,3,512]{2,1,0:T(4,128)S(1)}, f32[5,3,512,1024]{2,3,1,0:T(8,128)}) fusion(bf16[512,5,3,64]{0,3,2,1:T(8,128)(2,1)S(1)} %bitcast.202, bf16[1024,5,64]{0,2,1:T(8,128)(2,1)S(1)} %fusion.50, pred[512,1024]{0,1:T(8,128)(4,1)S(1)} %fusion.34), kind=kOutput, calls=%fused_computation.145 | convolution fusion | flops 1030218240 | bytes 33650688 | tf_op jit(solution)/shard_map/qkgd,skd->kgqs/dot_general | solution.py:121
  214.2 12.8 %fusion.3 = f32[5,3,512]{2,1,0:T(4,128)S(1)} fusion(f32[5,3,512,1024]{2,3,1,0:T(8,128)} %get-tuple-element.107, f32[5,3,512]{2,1,0:T(4,128)S(1)} %get-tuple-element.106), kind=kLoop, calls=%fused_computation.9 | loop fusion | flops 15720960 | bytes 31518720 | tf_op jit(solution)/shard_map/reduce_sum | solution.py:138
  227.1 13.8 %fusion.36 = bf16[5,64,3,512]{3,1,2,0:T(8,128)(2,1)} fusion(bf16[1024,5,64,1]{0,2,3,1:T(8,128)(2,1)S(1)} %bitcast.220, f32[5,3,512,1024]{2,3,1,0:T(8,128)} %get-tuple-element.107, f32[5,3,512]{2,1,0:T(4,128)S(1)} %fusion.3, f32[5,3,512]{2,1,0:T(4,128)S(1)} %get-tuple-element.106), kind=kOutput, calls=%fused_computation.82 | convolution fusion | flops 1030717440 | bytes 33157120 | tf_op jit(solution)/shard_map/kgqs,skd->qkgd/dot_general | solution.py:141
  249.1 10.7 %fusion.84 = f32[1024,2560]{1,0:T(8,128)} fusion(bf16[1024,960]{0,1:T(8,128)(2,1)} %multiply_convert_fusion.2, bf16[960,2560]{1,0:T(8,128)(2,1)} %all-gather.15.cloned.1.call-done), kind=kOutput, calls=%fused_computation.148 | convolution fusion | flops 5033164800 | bytes 17367040 | tf_op jit(solution)/shard_map/dot_general | solution.py:45
  259.8 10.5 %fusion.83 = f32[1024,2560]{1,0:T(8,128)} fusion(bf16[1024,960]{0,1:T(8,128)(2,1)} %multiply_convert_fusion.2, bf16[960,2560]{1,0:T(8,128)(2,1)} %all-gather.13.cloned.1.call-done), kind=kOutput, calls=%fused_computation.147 | convolution fusion | flops 5033164800 | bytes 17367040 | tf_op jit(solution)/shard_map/dot_general | solution.py:45
  270.3 19.8 %multiply_convert_fusion = (bf16[1024,2560]{1,0:T(8,128)(2,1)}, bf16[1024,2560]{1,0:T(8,128)(2,1)}, bf16[1024,2560]{1,0:T(8,128)(2,1)}) fusion(f32[1024,2560]{1,0:T(8,128)} %fusion.83, f32[1024,2560]{1,0:T(8,128)} %fusion.84, bf16[1024,960]{0,1:T(8,128)(2,1)} %param.35, bf16[2560,960]{1,0:T(8,128)(2,1)} %all-gather.17.cloned.1.call-done), kind=kOutput, calls=%fused_computation.29 | convolution fusion | flops 5075107840 | bytes 43581440 | tf_op jit(solution)/shard_map/dot_general | solution.py:55
  325.8 23.6 %fusion = (f32[5,3,512]{2,1,0:T(4,128)S(1)}, f32[5,1024,512,3]{2,1,3,0:T(8,128)}) fusion(f32[5,3,512,1024]{2,3,1,0:T(8,128)} %get-tuple-element.107, f32[5,3,512]{2,1,0:T(4,128)S(1)} %log_add_fusion, bf16[1024,5,64,1]{0,2,3,1:T(8,128)(2,1)S(1)} %bitcast.221, bf16[512,5,3,64]{0,3,2,1:T(8,128)(2,1)S(1)} %bitcast.206), kind=kOutput, calls=%fused_computation.2 | convolution fusion | flops 1030218240 | bytes 64614400 | tf_op jit(solution)/shard_map/qkgd,skd->kgqs/dot_general | solution.py:242
  349.4 12.8 %fusion.43 = bf16[1024,5,64]{0,2,1:T(8,128)(2,1)S(1)} fusion(bf16[512,5,3,64]{0,3,2,1:T(8,128)(2,1)S(1)} %bitcast.207, f32[5,3,512,1024]{2,3,1,0:T(8,128)} %get-tuple-element.107, f32[5,3,512]{2,1,0:T(4,128)S(1)} %log_add_fusion, f32[512,5,64]{0,2,1:T(8,128)S(1)} %fusion.52), kind=kOutput, calls=%fused_computation.86 | convolution fusion | flops 1023016960 | bytes 33781760 | tf_op jit(solution)/shard_map/kgqs,qkgd->skd/dot_general | solution.py:263
  364.0 11.3 %fusion.9 = bf16[5,3,512,512]{2,3,1,0:T(8,128)(2,1)S(1)} fusion(f32[5,512,512,3]{2,1,3,0:T(8,128)} %get-tuple-element.116, f32[5,3,512,512]{2,3,1,0:T(8,128)} %get-tuple-element.109, f32[5,3,512]{2,1,0:T(4,128)S(1)} %get-tuple-element.115, f32[5,3,512]{2,1,0:T(4,128)S(1)} %log_add_fusion.1), kind=kLoop, calls=%fused_computation.16 | loop fusion | flops 15728640 | bytes 39383040 | tf_op jit(solution)/shard_map/convert_element_type | solution.py:246
  378.7 26.9 %fusion.2 = bf16[5,3,512,1024]{2,3,1,0:T(8,128)(2,1)} fusion(f32[5,1024,512,3]{2,1,3,0:T(8,128)} %get-tuple-element.114, f32[5,3,512,1024]{2,3,1,0:T(8,128)} %get-tuple-element.107, f32[5,3,512]{2,1,0:T(4,128)S(1)} %get-tuple-element.113, f32[5,3,512]{2,1,0:T(4,128)S(1)} %log_add_fusion), kind=kLoop, calls=%fused_computation.4 | loop fusion | flops 31457280 | bytes 78704640 | tf_op jit(solution)/shard_map/convert_element_type | solution.py:246
  405.6 11.9 %broadcast_multiply_fusion = (f32[1024,5,64]{0,2,1:T(8,128)}, f32[1024,5,64]{0,2,1:T(8,128)}) fusion(f32[1024,64]{0,1:T(8,128)S(1)} %copy-done.7, bf16[512,5,3,64]{0,3,2,1:T(8,128)(2,1)S(1)} %bitcast.203, bf16[5,3,512,1024]{2,3,1,0:T(8,128)(2,1)} %fusion.2, f32[512,5,64]{0,2,1:T(8,128)} %fusion.56), kind=kOutput, calls=%fused_computation.110 | convolution fusion | flops 1007616000 | bytes 20250624 | tf_op jit(solution)/shard_map/kgqs,qkgd->skd/dot_general | solution.py:254
  483.8 40.8 %reduce-scatter.31.cloned.1.call-done = bf16[120,960]{1,0:T(8,128)(2,1)} async-done(((bf16[960,960]{1,0:T(8,128)(2,1)}), bf16[120,960]{1,0:T(8,128)(2,1)}) %reduce-scatter.31.cloned.1.call-update) | async-done | bytes 230416 | tf_op jit(solution)/shard_map/reduce_scatter | solution.py:295
  526.5 42.4 %reduce-scatter.25.cloned.1.call-done = bf16[120,960]{1,0:T(8,128)(2,1)} async-done(((bf16[960,960]{1,0:T(8,128)(2,1)}), bf16[120,960]{1,0:T(8,128)(2,1)}) %reduce-scatter.25.cloned.1.call-update) | async-done | bytes 230416 | tf_op jit(solution)/shard_map/reduce_scatter | solution.py:286
  570.8 56.9 %reduce-scatter.35.cloned.1.call-done = bf16[120,2560]{1,0:T(8,128)(2,1)} async-done(((bf16[960,2560]{1,0:T(8,128)(2,1)}), bf16[120,2560]{1,0:T(8,128)(2,1)}) %reduce-scatter.35.cloned.1.call-update) | async-done | bytes 614416 | tf_op jit(solution)/shard_map/reduce_scatter | solution.py:205
  629.9 56.1 %reduce-scatter.33.cloned.1.call-done = bf16[120,2560]{1,0:T(8,128)(2,1)} async-done(((bf16[960,2560]{1,0:T(8,128)(2,1)}), bf16[120,2560]{1,0:T(8,128)(2,1)}) %reduce-scatter.33.cloned.1.call-update) | async-done | bytes 614416 | tf_op jit(solution)/shard_map/reduce_scatter | solution.py:202
  688.3 10.4 %add_convert_fusion = bf16[1024,960]{0,1:T(8,128)(2,1)} fusion(f32[1024,960]{0,1:T(8,128)} %copy-done.4, bf16[1024,2560]{1,0:T(8,128)(2,1)} %get-tuple-element.89, bf16[2560,960]{1,0:T(8,128)(2,1)} %all-gather.17.cloned.1.call-done), kind=kOutput, calls=%fused_computation.67 | convolution fusion | flops 5035130880 | bytes 16056320 | tf_op jit(solution)/shard_map/dot_general | solution.py:45
  706.3 40.0 %reduce-scatter.37.cloned.1.call-done = bf16[320,960]{1,0:T(8,128)(2,1)} async-done(((bf16[2560,960]{1,0:T(8,128)(2,1)}), bf16[320,960]{1,0:T(8,128)(2,1)}) %reduce-scatter.37.cloned.1.call-update) | async-done | bytes 614416 | tf_op jit(solution)/shard_map/reduce_scatter | solution.py:208
  756.1 11.8 %all-reduce.9 = (bf16[960]{0:T(1024)(128)(2,1)S(1)}, bf16[960]{0:T(1024)(128)(2,1)S(1)}) all-reduce(bf16[960]{0:T(1024)(128)(2,1)S(1)} %get-tuple-element.77, bf16[960]{0:T(1024)(128)(2,1)S(1)} %copy-done.44), channel_id=2, replica_groups=mesh['fsdp'=8,'dp'=4] {'fsdp'}, use_global_device_ids=true, to_apply=%region_11.12.clone | all-reduce | flops 1920 | bytes 7680
  785.3 19.4 %reduce-scatter.41.cloned.1.call-done = bf16[240,120]{1,0:T(8,128)(2,1)} async-done(((bf16[960,120]{1,0:T(8,128)(2,1)}), bf16[240,120]{1,0:T(8,128)(2,1)}) %reduce-scatter.41.cloned.1.call-update) | async-done | bytes 57616
  806.3 19.0 %reduce-scatter.39.cloned.1.call-done = bf16[240,120]{1,0:T(8,128)(2,1)} async-done(((bf16[960,120]{1,0:T(8,128)(2,1)}), bf16[240,120]{1,0:T(8,128)(2,1)}) %reduce-scatter.39.cloned.1.call-update) | async-done | bytes 57616
  826.9 22.1 %reduce-scatter.45.cloned.1.call-done = bf16[640,120]{1,0:T(8,128)(2,1)} async-done(((bf16[2560,120]{1,0:T(8,128)(2,1)}), bf16[640,120]{1,0:T(8,128)(2,1)}) %reduce-scatter.45.cloned.1.call-update) | async-done | bytes 153616
  850.1 22.1 %reduce-scatter.43.cloned.1.call-done = bf16[640,120]{1,0:T(8,128)(2,1)} async-done(((bf16[2560,120]{1,0:T(8,128)(2,1)}), bf16[640,120]{1,0:T(8,128)(2,1)}) %reduce-scatter.43.cloned.1.call-update) | async-done | bytes 153616
  873.3 23.9 %reduce-scatter.47.cloned.1.call-done = bf16[240,320]{1,0:T(8,128)(2,1)} async-done(((bf16[960,320]{1,0:T(8,128)(2,1)}), bf16[240,320]{1,0:T(8,128)(2,1)}) %reduce-scatter.47.cloned.1.call-update) | async-done | bytes 153616
  (264 shorter events, 225.5 us)
Async XLA Ops:
  7.2 57.1 %copy-start.34 = (bf16[320,240]{1,0:T(8,128)(2,1)S(1)}, bf16[320,240]{1,0:T(8,128)(2,1)}, u32[]{:S(2)}) copy-start(bf16[320,240]{1,0:T(8,128)(2,1)} %param.34) | copy-start | bytes 460804
  7.2 164.0 %all-gather.9.cloned.1.call-start = ((), (), s32[]{:S(2)}) async-start(), calls=%async_computation.12 | async-start | bytes 2211840 | tf_op jit(solution)/shard_map/all_gather | solution.py:98
  20.1 220.8 %all-gather.11.cloned.1.call-start = ((), (), s32[]{:S(2)}) async-start(), calls=%async_computation.13 | async-start | bytes 2211840 | tf_op jit(solution)/shard_map/all_gather | solution.py:101
  21.1 62.1 %copy-start.43 = (u32[32]{0:T(128)S(1)}, u32[32]{0:T(128)}, u32[]{:S(2)}) copy-start(u32[32]{0:T(128)} %constant.154) | copy-start | bytes 388
  21.2 63.3 %copy-start.51 = (bf16[120]{0:T(256)(128)(2,1)S(1)}, bf16[120]{0:T(256)(128)(2,1)}, u32[]{:S(2)}) copy-start(bf16[120]{0:T(256)(128)(2,1)} %param.26) | copy-start | bytes 724
  21.2 63.5 %copy-start.52 = (bf16[120]{0:T(256)(128)(2,1)S(1)}, bf16[120]{0:T(256)(128)(2,1)}, u32[]{:S(2)}) copy-start(bf16[120]{0:T(256)(128)(2,1)} %param.31) | copy-start | bytes 724
  21.2 87.5 %copy-start.1 = (bf16[1024,960]{0,1:T(8,128)(2,1)S(1)}, bf16[1024,960]{0,1:T(8,128)(2,1)}, u32[]{:S(2)}) copy-start(bf16[1024,960]{0,1:T(8,128)(2,1)} %param.24) | copy-start | bytes 5898244
  34.0 215.1 %all-gather.15.cloned.1.call-start = ((), (), s32[]{:S(2)}) async-start(), calls=%async_computation.15 | async-start | bytes 5529600 | tf_op jit(solution)/shard_map/all_gather | solution.py:155
  49.2 60.0 %copy-start.41 = (bf16[120,80]{0,1:T(8,128)(2,1)S(1)}, bf16[120,80]{0,1:T(8,128)(2,1)}, u32[]{:S(2)}) copy-start(bf16[120,80]{0,1:T(8,128)(2,1)} %param.28) | copy-start | bytes 57604
  49.2 71.6 %copy-start.42 = (bf16[120,80]{0,1:T(8,128)(2,1)S(1)}, bf16[120,80]{0,1:T(8,128)(2,1)}, u32[]{:S(2)}) copy-start(bf16[120,80]{0,1:T(8,128)(2,1)} %param.29) | copy-start | bytes 57604
  49.2 210.6 %all-gather.13.cloned.1.call-start = ((), (), s32[]{:S(2)}) async-start(), calls=%async_computation.14 | async-start | bytes 5529600 | tf_op jit(solution)/shard_map/all_gather | solution.py:154
  64.2 206.1 %all-gather.17.cloned.1.call-start = ((), (), s32[]{:S(2)}) async-start(), calls=%async_computation.16 | async-start | bytes 5898240 | tf_op jit(solution)/shard_map/all_gather | solution.py:156
  80.8 399.6 %all-reduce.14.cloned.1.call-start = ((), (), s32[]{:S(2)}) async-start(), calls=%async_computation.29 | async-start | bytes 2621440
  108.7 62.5 %copy-start.37 = (f32[960]{0:T(1024)}, f32[960]{0:T(1024)S(1)}, u32[]{:S(2)}) copy-start(f32[960]{0:T(1024)S(1)} %convert_element_type.158) | copy-start | bytes 11524
  109.2 39.9 %copy-start.35 = (f32[1024]{0:T(1024)}, f32[1024]{0:T(1024)S(1)}, u32[]{:S(2)}) copy-start(f32[1024]{0:T(1024)S(1)} %fusion.29) | copy-start | bytes 12292
  109.2 62.0 %copy-start.39 = (f32[1024]{0:T(1024)}, f32[1024]{0:T(1024)S(1)}, u32[]{:S(2)}) copy-start(f32[1024]{0:T(1024)S(1)} %fusion.64) | copy-start | bytes 12292
  132.5 43.5 %copy-start.6 = (f32[1024,64]{0,1:T(8,128)}, f32[1024,64]{0,1:T(8,128)S(1)}, u32[]{:S(2)}) copy-start(f32[1024,64]{0,1:T(8,128)S(1)} %get-tuple-element.103) | copy-start | bytes 786436
  171.1 30.4 %copy-start.8 = (bf16[1024,5,64]{0,2,1:T(8,128)(2,1)}, bf16[1024,5,64]{0,2,1:T(8,128)(2,1)S(1)}, u32[]{:S(2)}) copy-start(bf16[1024,5,64]{0,2,1:T(8,128)(2,1)S(1)} %fusion.50) | copy-start | bytes 1966084
  423.3 101.4 %reduce-scatter.31.cloned.1.call-start = ((), (), s32[]{:S(2)}) async-start(), calls=%async_computation.20 | async-start | bytes 2211840 | tf_op jit(solution)/shard_map/reduce_scatter | solution.py:295
  433.1 135.9 %reduce-scatter.25.cloned.1.call-start = ((), (), s32[]{:S(2)}) async-start(), calls=%async_computation.17 | async-start | bytes 2211840 | tf_op jit(solution)/shard_map/reduce_scatter | solution.py:286
  449.8 177.9 %reduce-scatter.35.cloned.1.call-start = ((), (), s32[]{:S(2)}) async-start(), calls=%async_computation.22 | async-start | bytes 5529600 | tf_op jit(solution)/shard_map/reduce_scatter | solution.py:205
  459.6 226.5 %reduce-scatter.33.cloned.1.call-start = ((), (), s32[]{:S(2)}) async-start(), calls=%async_computation.21 | async-start | bytes 5529600 | tf_op jit(solution)/shard_map/reduce_scatter | solution.py:202
  469.4 277.0 %reduce-scatter.37.cloned.1.call-start = ((), (), s32[]{:S(2)}) async-start(), calls=%async_computation.23 | async-start | bytes 5898240 | tf_op jit(solution)/shard_map/reduce_scatter | solution.py:208
  479.6 301.6 %reduce-scatter.27.cloned.1.call-start = ((), (), s32[]{:S(2)}) async-start(), calls=%async_computation.18 | async-start | bytes 102400 | tf_op jit(solution)/shard_map/reduce_scatter | solution.py:306
  482.0 301.9 %reduce-scatter.29.cloned.1.call-start = ((), (), s32[]{:S(2)}) async-start(), calls=%async_computation.19 | async-start | bytes 102400 | tf_op jit(solution)/shard_map/reduce_scatter | solution.py:309
  483.8 321.0 %reduce-scatter.41.cloned.1.call-start = ((), (), s32[]{:S(2)}) async-start(), calls=%async_computation.25 | async-start | bytes 307200
  526.5 298.9 %reduce-scatter.39.cloned.1.call-start = ((), (), s32[]{:S(2)}) async-start(), calls=%async_computation.24 | async-start | bytes 307200
  570.8 278.3 %reduce-scatter.45.cloned.1.call-start = ((), (), s32[]{:S(2)}) async-start(), calls=%async_computation.27 | async-start | bytes 819200
  629.9 242.3 %reduce-scatter.43.cloned.1.call-start = ((), (), s32[]{:S(2)}) async-start(), calls=%async_computation.26 | async-start | bytes 819200
  688.2 208.9 %reduce-scatter.47.cloned.1.call-start = ((), (), s32[]{:S(2)}) async-start(), calls=%async_computation.28 | async-start | bytes 921600
  702.1 46.6 %copy-start.21 = (bf16[1024,5,64]{0,2,1:T(8,128)(2,1)S(1)}, bf16[1024,5,64]{0,2,1:T(8,128)(2,1)}, u32[]{:S(2)}) copy-start(bf16[1024,5,64]{0,2,1:T(8,128)(2,1)} %copy-done.20) | copy-start | bytes 1966084
  702.1 46.6 %copy-start.23 = (bf16[960,320]{0,1:T(8,128)(2,1)S(1)}, bf16[960,320]{0,1:T(8,128)(2,1)}, u32[]{:S(2)}) copy-start(bf16[960,320]{0,1:T(8,128)(2,1)} %copy-done.22) | copy-start | bytes 1843204
  (46 other events, 342.4 us)
Sparse Core Ops, SparseCore 0:
  20.3 32.2 all-gather.8
  54.4 27.3 all-gather.10
  83.7 39.7 all-gather.14
  125.2 42.7 all-gather.12
  169.8 41.1 all-gather.16
  423.4 56.9 all-reduce.13
  484.1 40.4 reduce-scatter.30
  528.6 40.2 reduce-scatter.24
  572.9 54.8 reduce-scatter.34
  631.1 54.8 reduce-scatter.32
  689.8 56.5 reduce-scatter.36
  749.1 14.5 reduce-scatter.26
  766.6 17.2 reduce-scatter.28
  786.6 18.0 reduce-scatter.40
  807.5 17.7 reduce-scatter.38
  827.5 21.5 reduce-scatter.44
  851.2 21.0 reduce-scatter.42
  874.4 22.7 reduce-scatter.46
where the time goes:
time: 918 us; the launch traced here: 908 us
  waiting for transfers between devices  345 us (38%)
  matrix products  255 us (28%)
  blocking collectives  162 us (18%)
  other arithmetic  87 us (9%)
  local copies, waits for them, and re-layouts  39.8 us (4%)
  between operations  17.6 us (2%)
    unnamed x24, waiting for transfers between devices  107 us
    reduce_scatter x1, waiting for transfers between devices, on_device(): lax.psum_scatter(grad_up_w.astype(jnp.bfloat16), 'fsdp', scatter_dimensio...  56.9 us
    reduce_scatter x1, waiting for transfers between devices, on_device(): lax.psum_scatter(grad_gate_w.astype(jnp.bfloat16), 'fsdp', scatter_dimens...  56.1 us
    dot_general x7, matrix products, product_right(): lax.dot_general(left, right, (((1,), (1,)), ((), ())), preferred_element_...  55.1 us
    reduce_scatter x1, waiting for transfers between devices, on_device(): lax.psum_scatter(grad_query_w.astype(jnp.bfloat16), 'fsdp', scatter_dimen...  42.4 us
    dot_general x7, matrix products, product(): return jnp.dot(left, right, preferred_element_type=jnp.float32)  42.2 us
    reduce_scatter x1, waiting for transfers between devices, on_device(): lax.psum_scatter(grad_out_w.astype(jnp.bfloat16), 'fsdp', scatter_dimensi...  40.8 us
    dot_general x7, matrix products, product_left(): lax.dot_general(left, right, (((0,), (0,)), ((), ())), preferred_element_...  40.1 us
  transfers between devices with their start and end apart: 18, of which 12 were waited for; matrix products, arithmetic and copies ran while one was open for 24% of the time, Pallas kernels for 0%

commit v1 on v0

v1 whole, which is shorter than its diff:
```python
import functools

import jax
import jax.numpy as jnp
from jax import lax
from jax.experimental import pallas as pl
from jax.experimental.pallas import tpu as pltpu
from jax.sharding import PartitionSpec as P

D = 960
FF = 2560
HEADS = 15
KV_HEADS = 5
GROUP = HEADS // KV_HEADS
HEAD_DIM = 64
HALF = HEAD_DIM // 2
TILE = 256
QUAD = 4
DB = D // QUAD
FB = FF // QUAD
QB = D // QUAD
KB = KV_HEADS * HEAD_DIM // QUAD
ROWS = 128
SPARE = 16
QKV = QB + 2 * KB
QKV_ROWS = 208
LEAD = FB - 512
SKIP = DB - LEAD
NEG = -1e30
EPS = 1e-05
ROPE_BASE = 10000.0
BIG = 60 * 1024 * 1024

F32 = jnp.float32
BF16 = jnp.bfloat16


def nn(a, b):
    return jnp.dot(a, b, preferred_element_type=F32)


def nt(a, b):
    return lax.dot_general(a, b, (((1,), (1,)), ((), ())), preferred_element_type=F32)


def rope_tables(first, length):
    places = jnp.arange(length, dtype=jnp.int32)
    position = jnp.where(places < first, places, places - first).astype(F32)
    frequency = ROPE_BASE ** (-jnp.arange(0, HEAD_DIM, 2, dtype=F32) / HEAD_DIM)
    angles = frequency[:, None] * position[None, :]
    return jnp.cos(angles), jnp.sin(angles)


def params():
    return pltpu.CompilerParams(vmem_limit_bytes=BIG)


def any_spec():
    return pl.BlockSpec(memory_space=pl.ANY)


def copies(idx, mine, other, sems, target):
    plans = ([], [])
    for mine_core in range(2):
        slot = 0
        for core, pieces in ((mine_core, mine), (1 - mine_core, other)):
            for k in range(QUAD):
                for kz in range(QUAD):
                    if k < 3:
                        ref = pieces[k].at[kz]
                    elif kz < 2:
                        ref = pieces[3].at[kz]
                    else:
                        ref = pieces[4].at[kz - 2]
                    for source, dest in target(core, idx[4 + kz], idx[k], kz):
                        src = ref if source is None else ref.at[pl.ds(*source), :]
                        plans[mine_core].append(
                            pltpu.make_async_copy(src, dest, sems.at[slot])
                        )
                        slot += 1
    return plans


def rows_target(weight, gains=None):
    def target(core, z, yx, kz):
        base = pl.multiple_of(yx * DB, 16)
        if core == 0:
            return [((0, ROWS), weight.at[z, pl.ds(base, ROWS), :])]
        found = [((SPARE, DB - ROWS), weight.at[z, pl.ds(base + ROWS, DB - ROWS), :])]
        if gains is not None and kz == 0:
            found.append(((0, SPARE), gains.at[yx]))
        return found

    return target


def down_target(weight):
    def target(core, z, yx, kz):
        base = pl.multiple_of(z * DB, 16)
        if core == 0:
            return [((0, ROWS), weight.at[yx, pl.ds(base, ROWS), :])]
        return [((SPARE, DB - ROWS), weight.at[yx, pl.ds(base + ROWS, DB - ROWS), :])]

    return target


def pair_target(weight):
    def target(core, z, yx, kz):
        base = pl.multiple_of(yx * DB, 16)
        return [(None, weight.at[core, z, pl.ds(base, DB), :])]

    return target


def run_copies(core, plans):
    for c in range(2):

        @pl.when(core == c)
        def _():
            for copy in plans[c]:
                copy.start()
            for copy in plans[c]:
                copy.wait()


def attention_forward(
    idx, x_ref, cos_ref, sin_ref, *rest
):
    mine, other = rest[0:5], rest[5:10]
    (
        weight, gain_ref, n1t_ref, qx_ref, kx_ref, kt_ref, vt_ref, ot_ref, lse_ref,
        y_ref, n2_ref, n2t_ref, gains, sems,
    ) = rest[10:]
    run_copies(idx[8], copies(idx, mine, other, sems, rows_target(weight, gains)))
    length = x_ref.shape[0]
    tiles = length // TILE
    first = idx[9]
    gain_one = jnp.concatenate([gains[b, 0:1, 0:DB] for b in range(QUAD)], axis=1).astype(F32)
    gain_two = jnp.concatenate([gains[b, 0:1, 256 : 256 + DB] for b in range(QUAD)], axis=1).astype(F32)
    gain_ref[0:1, :] = gain_one
    gain_ref[1:2, :] = gain_two

    place = lax.broadcasted_iota(jnp.int32, (HEAD_DIM, length), 1)
    row = lax.broadcasted_iota(jnp.int32, (HEAD_DIM, length), 0)
    extra_q = jnp.where((row == 0) & (place >= first), NEG, 0.0).astype(BF16)
    extra_k = jnp.where((row == 0) & (place < first), 1.0, 0.0)
    for h in range(HEADS):
        qx_ref[h, HEAD_DIM:, :] = extra_q

    def project(i, carry):
        at = pl.ds(pl.multiple_of(i * TILE, TILE), TILE)
        x = x_ref[at, :].astype(F32)
        inverse = lax.rsqrt(jnp.mean(x * x, axis=-1, keepdims=True) + EPS)
        n1 = x * inverse * gain_one
        n1b = n1.astype(BF16)
        n1t_ref[:, at] = n1b.T
        cosine, sine = cos_ref[:, at], sin_ref[:, at]
        flat = [nn(n1b, weight[z, :, LEAD:]).T for z in range(QUAD)]
        queries = jnp.concatenate([f[SKIP : SKIP + QB] for f in flat], axis=0)
        keys = jnp.concatenate([f[SKIP + QB : SKIP + QB + KB] for f in flat], axis=0)
        values = jnp.concatenate([f[SKIP + QB + KB :] for f in flat], axis=0)
        for h in range(HEADS):
            u1 = queries[h * HEAD_DIM : h * HEAD_DIM + HALF]
            u2 = queries[h * HEAD_DIM + HALF : (h + 1) * HEAD_DIM]
            turned = jnp.concatenate([u1 * cosine - u2 * sine, u2 * cosine + u1 * sine], axis=0)
            qx_ref[h, 0:HEAD_DIM, at] = turned.astype(BF16) * jnp.asarray(0.125, BF16)
        for h in range(KV_HEADS):
            u1 = keys[h * HEAD_DIM : h * HEAD_DIM + HALF]
            u2 = keys[h * HEAD_DIM + HALF : (h + 1) * HEAD_DIM]
            turned = jnp.concatenate([u1 * cosine - u2 * sine, u2 * cosine + u1 * sine], axis=0)
            kt_ref[h, :, at] = turned.astype(BF16)
        vt_ref[:, :, at] = values.astype(BF16).reshape(KV_HEADS, HEAD_DIM, TILE)
        return carry

    lax.fori_loop(0, tiles, project, 0)

    causal = lax.broadcasted_iota(jnp.int32, (TILE, GROUP * TILE), 0) > (
        lax.broadcasted_iota(jnp.int32, (TILE, GROUP * TILE), 1) % TILE
    )

    def head(j, carry):
        wide = jnp.concatenate([kt_ref[j].astype(F32), extra_k], axis=0)
        kx_ref[j] = wide.T.astype(BF16)
        for b in range(tiles):
            at = slice(b * TILE, (b + 1) * TILE)
            qx = jnp.concatenate([qx_ref[GROUP * j + g, :, at] for g in range(GROUP)], axis=1)
            scores = []
            for s in range(b + 1):
                raw = nn(kx_ref[j, s * TILE : (s + 1) * TILE, :], qx)
                scores.append(jnp.where(causal, NEG, raw) if s == b else raw)
            highest = functools.reduce(jnp.maximum, [jnp.max(s, axis=0, keepdims=True) for s in scores])
            total = 0.0
            out = 0.0
            for s in range(b + 1):
                weights = jnp.exp(scores[s] - highest)
                total = total + jnp.sum(weights, axis=0, keepdims=True)
                out = out + nn(vt_ref[j, :, s * TILE : (s + 1) * TILE], weights.astype(BF16))
            out = out / total
            lse_ref[j, b] = highest + jnp.log(total)
            for g in range(GROUP):
                ot_ref[GROUP * j + g, :, at] = out[:, g * TILE : (g + 1) * TILE].astype(BF16)
        return carry

    lax.fori_loop(0, KV_HEADS, head, 0)

    def finish(i, carry):
        at = pl.ds(pl.multiple_of(i * TILE, TILE), TILE)
        o = ot_ref[:, :, at].reshape(D, TILE).T
        added = jnp.concatenate([nn(o, weight[z, :, 0:256])[:, 0:DB] for z in range(QUAD)], axis=1)
        y = x_ref[at, :].astype(F32) + added
        y_ref[at, :] = y
        inverse = lax.rsqrt(jnp.mean(y * y, axis=-1, keepdims=True) + EPS)
        n2 = (y * inverse * gain_two).astype(BF16)
        n2_ref[at, :] = n2
        n2t_ref[:, at] = n2.T
        return carry

    lax.fori_loop(0, tiles, finish, 0)


def call_attention_forward(idx, x, cosine, sine, mine, other):
    length = x.shape[0]
    tiles = length // TILE
    s = jax.ShapeDtypeStruct
    vm = pl.BlockSpec(memory_space=pltpu.VMEM)
    return pl.pallas_call(
        attention_forward,
        out_shape=(
            s((QUAD, D, FB), BF16),
            s((8, D), F32),
            s((D, length), BF16),
            s((HEADS, 2 * HEAD_DIM, length), BF16),
            s((KV_HEADS, length, 2 * HEAD_DIM), BF16),
            s((KV_HEADS, HEAD_DIM, length), BF16),
            s((KV_HEADS, HEAD_DIM, length), BF16),
            s((HEADS, HEAD_DIM, length), BF16),
            s((KV_HEADS, tiles, 1, GROUP * TILE), F32),
            s((length, D), F32),
            s((length, D), BF16),
            s((D, length), BF16),
        ),
        in_specs=[pl.BlockSpec(memory_space=pltpu.SMEM)] + [vm] * 3 + [any_spec()] * 10,
        out_specs=(vm,) * 12,
        scratch_shapes=[
            pltpu.VMEM((QUAD, SPARE, FB), BF16),
            pltpu.SemaphoreType.DMA((64,)),
        ],
        compiler_params=params(),
        name="attention_forward",
        cost_estimate=pl.CostEstimate(flops=20_000_000_000, bytes_accessed=30_000_000, transcendentals=10_000_000),
    )(idx, x, cosine, sine, *mine, *other)


def feed(idx, n2_ref, y_ref, c_ref, gain_ref, *rest):
    pairs, downs = rest[0:10], rest[10:20]
    (
        mixed_ref, h_ref, dgu_ref, dy_ref, dat_ref, ct_ref, gg_ref,
        weight, down, gate, rise, sems,
    ) = rest[20:]

    @pl.when(pl.program_id(0) == 0)
    def _():
        first = copies(idx, pairs[0:5], pairs[5:10], sems.at[0], pair_target(weight))
        second = copies(idx, downs[0:5], downs[5:10], sems.at[1], down_target(down))
        run_copies(idx[8], [a + b for a, b in zip(first, second)])
        gg_ref[...] = jnp.zeros_like(gg_ref)

    n2 = n2_ref[...]
    for b in range(QUAD):
        at = slice(b * FB, (b + 1) * FB)
        g = nn(n2, weight[0, b])
        u = nn(n2, weight[1, b])
        gate[:, at] = g
        rise[:, at] = u
        h_ref[b] = (g / (1.0 + jnp.exp(-g)) * u).astype(BF16)
    y = y_ref[...]
    total = y
    for b in range(QUAD):
        total = total + nt(h_ref[b], down[b])
    mixed_ref[...] = total.astype(BF16)
    c = c_ref[...]
    ct_ref[...] = c.T
    dn2 = jnp.zeros((TILE, D), F32)
    for b in range(QUAD):
        at = slice(b * FB, (b + 1) * FB)
        dh = nn(c, down[b])
        g, u = gate[:, at], rise[:, at]
        sig = 1.0 / (1.0 + jnp.exp(-g))
        silu = g * sig
        dg = (dh * u * (sig + silu * (1.0 - sig))).astype(BF16)
        du = (dh * silu).astype(BF16)
        dgu_ref[0, b] = dg
        dgu_ref[1, b] = du
        dn2 = dn2 + nt(dg, weight[0, b]) + nt(du, weight[1, b])
    r = lax.rsqrt(jnp.mean(y * y, axis=-1, keepdims=True) + EPS)
    yr = y * r
    gg_ref[0:1, :] += jnp.sum(dn2 * yr, axis=0, keepdims=True)
    t = dn2 * gain_ref[1:2, :]
    dy = c.astype(F32) + r * (t - yr * jnp.mean(t * yr, axis=-1, keepdims=True))
    dy_ref[...] = dy
    dat_ref[...] = dy.astype(BF16).T


def call_feed(idx, n2, y, c, gains, pairs, downs):
    length = n2.shape[0]
    s = jax.ShapeDtypeStruct
    wide = pl.BlockSpec((TILE, D), lambda i, p: (i, 0))
    tall = pl.BlockSpec((D, TILE), lambda i, p: (0, i))
    whole = pl.BlockSpec((8, D), lambda i, p: (0, 0))
    return pl.pallas_call(
        feed,
        out_shape=(
            s((length, D), BF16),
            s((QUAD, length, FB), BF16),
            s((2, QUAD, length, FB), BF16),
            s((length, D), F32),
            s((D, length), BF16),
            s((D, length), BF16),
            s((8, D), F32),
        ),
        grid_spec=pltpu.PrefetchScalarGridSpec(
            num_scalar_prefetch=1,
            grid=(length // TILE,),
            in_specs=[wide, wide, wide, whole] + [any_spec()] * 20,
            out_specs=[
                wide,
                pl.BlockSpec((QUAD, TILE, FB), lambda i, p: (0, i, 0)),
                pl.BlockSpec((2, QUAD, TILE, FB), lambda i, p: (0, 0, i, 0)),
                wide,
                tall,
                tall,
                whole,
            ],
            scratch_shapes=[
                pltpu.VMEM((2, QUAD, D, FB), BF16),
                pltpu.VMEM((QUAD, D, FB), BF16),
                pltpu.VMEM((TILE, FF), F32),
                pltpu.VMEM((TILE, FF), F32),
                pltpu.SemaphoreType.DMA((2, 64)),
            ],
        ),
        compiler_params=params(),
        name="feed_forward_backward",
        cost_estimate=pl.CostEstimate(flops=30_000_000_000, bytes_accessed=50_000_000, transcendentals=5_000_000),
    )(idx, n2, y, c, gains, *pairs, *downs)


def pair_grads(target, idx, n2t_ref, d_ref, *rest):
    received, outs = (rest[0:1], rest[1:]) if len(rest) > 1 and target == 0 else ((), rest)
    for k in range(QUAD):
        rows = pl.ds(pl.multiple_of(idx[k] * DB, 16), DB)
        got = nn(n2t_ref[rows, :], d_ref[...])
        if received:
            got = got + received[0][k, 0].astype(F32)
        if len(outs) == 1:
            outs[0][k, 0] = got.astype(BF16)
        else:
            outs[k][0] = got.astype(BF16)


def call_pair_grads(idx, n2t, dgu, received=None):
    length = n2t.shape[1]
    s = jax.ShapeDtypeStruct
    block = pl.BlockSpec((QUAD, 1, DB, FB), lambda i, p: (0, i, 0, 0))
    matrix = 10 if received is None else 8
    specs = [
        pl.BlockSpec((D, length), lambda i, p: (0, 0)),
        pl.BlockSpec((None, None, length, FB), lambda i, p: (p[matrix], p[4 + i], 0, 0)),
    ]
    if received is None:
        out_shape = [s((QUAD, QUAD, DB, FB), BF16)]
        out_specs = [block]
        extra = ()
    else:
        specs.append(block)
        extra = (received,)
        out_shape = [s((QUAD, DB, FB), BF16)] * QUAD
        out_specs = [pl.BlockSpec((1, DB, FB), lambda i, p: (i, 0, 0))] * QUAD
    return pl.pallas_call(
        functools.partial(pair_grads, 1 if received is None else 0),
        out_shape=out_shape,
        grid_spec=pltpu.PrefetchScalarGridSpec(
            num_scalar_prefetch=1, grid=(QUAD,), in_specs=specs, out_specs=out_specs
        ),
        compiler_params=params(),
        name="pair_grads",
        cost_estimate=pl.CostEstimate(flops=5_000_000_000, bytes_accessed=15_000_000, transcendentals=0),
    )(idx, n2t, dgu, *extra)


WIDE = FB + 256


def down_grads(which, idx, ct_ref, h_ref, ot_ref, dat_ref, gg_ref, *rest):
    received, outs = (rest[0:1], rest[1:]) if which == 8 else ((), rest)
    core = idx[which]
    z = idx[4 + pl.program_id(0)]
    start = pl.multiple_of(z * DB + core * (DB - ROWS), 16)
    left = ct_ref[pl.ds(start, ROWS), :]
    right = dat_ref[pl.ds(pl.multiple_of(z * DB, 16), DB), :]
    for k in range(QUAD):
        yx = idx[k]
        got = nn(left, h_ref[yx])
        begin = pl.multiple_of(yx * DB + core * (DB - ROWS), 16)
        also = nt(ot_ref[pl.ds(begin, ROWS), :], right)
        spare = jnp.broadcast_to(gg_ref[yx, 0:1, :], (SPARE, FB))
        head = jnp.where(core == 1, spare, got[0:SPARE])
        if received:
            got = got + received[0][k, 0, :, 0:FB].astype(F32)
            also = also + received[0][k, 0, :, FB : FB + DB].astype(F32)
            head = head + received[0][k, 0, 0:SPARE, 0:FB].astype(F32)
            ref = outs[k].at[0]
        else:
            ref = outs[0].at[k, 0]
        ref[:, 0:FB] = got.astype(BF16)
        ref[:, FB : FB + DB] = also.astype(BF16)
        ref[:, FB + DB :] = jnp.zeros((ROWS, 256 - DB), BF16)
        ref[0:SPARE, 0:FB] = head.astype(BF16)


def call_down_grads(idx, ct, h, ot, dat, gg, received=None):
    length = ct.shape[1]
    s = jax.ShapeDtypeStruct
    block = pl.BlockSpec((QUAD, 1, ROWS, WIDE), lambda i, p: (0, i, 0, 0))
    vm = pl.BlockSpec((D, length), lambda i, p: (0, 0))
    specs = [
        vm,
        pl.BlockSpec(memory_space=pltpu.VMEM),
        vm,
        vm,
        pl.BlockSpec((QUAD, 8, FB), lambda i, p: (0, 0, 0)),
    ]
    if received is None:
        out_shape, out_specs, extra = [s((QUAD, QUAD, ROWS, WIDE), BF16)], [block], ()
    else:
        specs.append(block)
        extra = (received,)
        out_shape = [s((QUAD, ROWS, WIDE), BF16)] * QUAD
        out_specs = [pl.BlockSpec((1, ROWS, WIDE), lambda i, p: (i, 0, 0))] * QUAD
    return pl.pallas_call(
        functools.partial(down_grads, 10 if received is None else 8),
        out_shape=out_shape,
        grid_spec=pltpu.PrefetchScalarGridSpec(
            num_scalar_prefetch=1, grid=(QUAD,), in_specs=specs, out_specs=out_specs
        ),
        compiler_params=params(),
        name="down_grads",
        cost_estimate=pl.CostEstimate(flops=4_000_000_000, bytes_accessed=15_000_000, transcendentals=0),
    )(idx, ct, h, ot, dat, gg, *extra)


def attention_backward(
    idx, x_ref, gain_ref, weight, n1t_ref, qx_ref, kx_ref, kt_ref, vt_ref, ot_ref, lse_ref, dat_ref, dy_ref,
    cos_ref, sin_ref, gx_ref, z_ref, gg_ref, dot_s, zq, zk, zv, dk_s, dv_s,
):
    length = x_ref.shape[0]
    tiles = length // TILE

    def back(i, carry):
        at = pl.ds(pl.multiple_of(i * TILE, TILE), TILE)
        total = 0.0
        for z in range(QUAD):
            total = total + nn(weight[z, :, 0:DB], dat_ref[z * DB : (z + 1) * DB, at])
        dot_s[:, :, at] = total.astype(BF16).reshape(HEADS, HEAD_DIM, TILE)
        return carry

    lax.fori_loop(0, tiles, back, 0)

    causal = lax.broadcasted_iota(jnp.int32, (TILE, GROUP * TILE), 0) > (
        lax.broadcasted_iota(jnp.int32, (TILE, GROUP * TILE), 1) % TILE
    )

    def unrotate(grads, cosine, sine):
        u1, u2 = grads[:HALF], grads[HALF:]
        return jnp.concatenate([u1 * cosine + u2 * sine, u2 * cosine - u1 * sine], axis=0)

    def head(j, carry):
        values = vt_ref[j].astype(F32).T.astype(BF16)
        for b in range(tiles):
            at = slice(b * TILE, (b + 1) * TILE)
            qx = jnp.concatenate([qx_ref[GROUP * j + g, :, at] for g in range(GROUP)], axis=1)
            do = jnp.concatenate([dot_s[GROUP * j + g, :, at] for g in range(GROUP)], axis=1)
            o = jnp.concatenate([ot_ref[GROUP * j + g, :, at] for g in range(GROUP)], axis=1)
            inner = jnp.sum(do.astype(F32) * o.astype(F32), axis=0, keepdims=True)
            log_total = lse_ref[j, b]
            dq = 0.0
            for s in range(b + 1):
                keys = slice(s * TILE, (s + 1) * TILE)
                raw = nn(kx_ref[j, keys, :], qx)
                if s == b:
                    raw = jnp.where(causal, NEG, raw)
                probs = jnp.exp(raw - log_total)
                dp = nn(values[keys, :], do)
                ds = (probs * (dp - inner)).astype(BF16)
                dq = dq + nn(kt_ref[j, :, keys], ds)
                dk = nt(ds, qx[0:HEAD_DIM, :])
                dv = nt(probs.astype(BF16), do)
                if s == b:
                    dk_s[keys, :] = dk
                    dv_s[keys, :] = dv
                else:
                    dk_s[keys, :] += dk
                    dv_s[keys, :] += dv
            cosine, sine = cos_ref[:, at], sin_ref[:, at]
            for g in range(GROUP):
                part = unrotate(dq[:, g * TILE : (g + 1) * TILE] * 0.125, cosine, sine)
                zq[GROUP * j + g, :, at] = part.astype(BF16)
        zk[j] = unrotate(dk_s[...].T, cos_ref[...], sin_ref[...]).astype(BF16)
        zv[j] = dv_s[...].T.astype(BF16)
        return carry

    lax.fori_loop(0, KV_HEADS, head, 0)

    gain_one = gain_ref[0:1, :]
    for z in range(QUAD):
        z_ref[z, 0:SKIP, :] = jnp.zeros((SKIP, length), BF16)
    flat_q, flat_k, flat_v = (a.reshape(-1, length) for a in (zq, zk, zv))
    for z in range(QUAD):
        z_ref[z, SKIP : SKIP + QB, :] = flat_q[z * QB : (z + 1) * QB, :]
        z_ref[z, SKIP + QB : SKIP + QB + KB, :] = flat_k[z * KB : (z + 1) * KB, :]
        z_ref[z, SKIP + QB + KB :, :] = flat_v[z * KB : (z + 1) * KB, :]
    gg_ref[...] = jnp.zeros_like(gg_ref)

    def finish(i, carry):
        at = pl.ds(pl.multiple_of(i * TILE, TILE), TILE)
        total = 0.0
        for z in range(QUAD):
            total = total + nn(weight[z, :, LEAD:], z_ref[z, :, at])
        dn1 = total.T
        x = x_ref[at, :].astype(F32)
        r = lax.rsqrt(jnp.mean(x * x, axis=-1, keepdims=True) + EPS)
        xr = x * r
        gg_ref[0:1, :] += jnp.sum(dn1 * xr, axis=0, keepdims=True)
        t = dn1 * gain_one
        gx = dy_ref[at, :] + r * (t - xr * jnp.mean(t * xr, axis=-1, keepdims=True))
        gx_ref[at, :] = gx.astype(BF16)
        return carry

    lax.fori_loop(0, tiles, finish, 0)


def call_attention_backward(idx, *args):
    length = args[0].shape[0]
    s = jax.ShapeDtypeStruct
    vm = pl.BlockSpec(memory_space=pltpu.VMEM)
    return pl.pallas_call(
        attention_backward,
        out_shape=(
            s((length, D), BF16),
            s((QUAD, 512, length), BF16),
            s((8, D), F32),
        ),
        in_specs=[pl.BlockSpec(memory_space=pltpu.SMEM)] + [vm] * len(args),
        out_specs=(vm,) * 3,
        scratch_shapes=[
            pltpu.VMEM((HEADS, HEAD_DIM, length), BF16),
            pltpu.VMEM((HEADS, HEAD_DIM, length), BF16),
            pltpu.VMEM((KV_HEADS, HEAD_DIM, length), BF16),
            pltpu.VMEM((KV_HEADS, HEAD_DIM, length), BF16),
            pltpu.VMEM((length, HEAD_DIM), F32),
            pltpu.VMEM((length, HEAD_DIM), F32),
        ],
        compiler_params=params(),
        name="attention_backward",
        cost_estimate=pl.CostEstimate(flops=30_000_000_000, bytes_accessed=30_000_000, transcendentals=10_000_000),
    )(idx, *args)


def qkv_grads(which, idx, z_ref, n1t_ref, gg_ref, *rest):
    received, outs = (rest[0:1], rest[1:]) if which == 8 else ((), rest)
    core = idx[which]
    start = pl.multiple_of(SKIP + core * (QKV - QKV_ROWS), 16)
    left = z_ref[pl.ds(start, QKV_ROWS), :]
    for k in range(QUAD):
        yx = idx[k]
        got = nt(left, n1t_ref[pl.ds(pl.multiple_of(yx * DB, 16), DB), :])
        spare = jnp.broadcast_to(gg_ref[yx, 0:1, :], (SPARE, DB))
        head = jnp.where(core == 1, spare, got[0:SPARE])
        if received:
            got = got + received[0][k, 0].astype(F32)
            head = head + received[0][k, 0, 0:SPARE].astype(F32)
            ref = outs[k].at[0]
        else:
            ref = outs[0].at[k, 0]
        ref[...] = got.astype(BF16)
        ref[0:SPARE, :] = head.astype(BF16)


def call_qkv_grads(idx, z, n1t, gg, received=None):
    length = n1t.shape[1]
    s = jax.ShapeDtypeStruct
    block = pl.BlockSpec((QUAD, 1, QKV_ROWS, DB), lambda i, p: (0, i, 0, 0))
    specs = [
        pl.BlockSpec((None, 512, length), lambda i, p: (p[4 + i], 0, 0)),
        pl.BlockSpec((D, length), lambda i, p: (0, 0)),
        pl.BlockSpec((QUAD, 8, DB), lambda i, p: (0, 0, 0)),
    ]
    if received is None:
        out_shape, out_specs, extra = [s((QUAD, QUAD, QKV_ROWS, DB), BF16)], [block], ()
    else:
        specs.append(block)
        extra = (received,)
        out_shape = [s((QUAD, QKV_ROWS, DB), BF16)] * QUAD
        out_specs = [pl.BlockSpec((1, QKV_ROWS, DB), lambda i, p: (i, 0, 0))] * QUAD
    return pl.pallas_call(
        functools.partial(qkv_grads, 10 if received is None else 8),
        out_shape=out_shape,
        grid_spec=pltpu.PrefetchScalarGridSpec(
            num_scalar_prefetch=1, grid=(QUAD,), in_specs=specs, out_specs=out_specs
        ),
        compiler_params=params(),
        name="qkv_grads",
        cost_estimate=pl.CostEstimate(flops=3_000_000_000, bytes_accessed=10_000_000, transcendentals=0),
    )(idx, z, n1t, gg, *extra)


CORE = [(i, i ^ 1) for i in range(8)]
ALONG_X = [(i, i ^ 2) for i in range(8)]
ALONG_Y = [(i, i ^ 4) for i in range(8)]
ACROSS = [(i, i ^ 6) for i in range(8)]


def swap(values):
    return lax.ppermute(values, "fsdp", CORE)


def from_z(values, k):
    return lax.ppermute(values, "dp", [(j, (j - k) % QUAD) for j in range(QUAD)])


def to_z(values, k):
    return lax.ppermute(values, "dp", [(j, (j + k) % QUAD) for j in range(QUAD)])


def spread_z(piece):
    return jnp.stack([piece] + [from_z(piece, k) for k in range(1, QUAD)])


def spread_plane(own):
    by_x = lax.ppermute(own, "fsdp", ALONG_X)
    by_y = lax.ppermute(own, "fsdp", ALONG_Y)
    low = lax.ppermute(by_y[0:2], "fsdp", ALONG_X)
    high = lax.ppermute(by_x[2:4], "fsdp", ALONG_Y)
    return (own, by_x, by_y, low, high)


def spread_core(pieces):
    return tuple(swap(piece) for piece in pieces)


def add(parts):
    return functools.reduce(jnp.add, [part.astype(F32) for part in parts])


def sum_plane(blocks):
    got = (
        blocks[0],
        lax.ppermute(blocks[1], "fsdp", ALONG_X),
        lax.ppermute(blocks[2], "fsdp", ALONG_Y),
        lax.ppermute(blocks[3], "fsdp", ACROSS),
    )
    return add(got).astype(BF16)


def sum_z(blocks):
    return add([blocks[0]] + [to_z(blocks[k], k) for k in range(1, QUAD)])


def slab(values, start, size, axis):
    return lax.dynamic_slice_in_dim(values, start, size, axis)


def tables(yx, z, core, first):
    entries = [yx ^ k for k in range(QUAD)] + [(z + k) % QUAD for k in range(QUAD)]
    entries += [core, first, 1 - core, 0, 0, 0, 0, 0]
    return jnp.stack([jnp.asarray(e, jnp.int32) for e in entries])


def gather_near(core, gain_attn, w_query, w_key, w_value, w_out, gain_mlp, w_gate, w_up, w_down):
    zero = core == 0
    rows = jnp.concatenate([w_out, w_query, w_key, w_value], axis=1)
    share = rows.shape[0]
    extra = ROWS - share
    pad = jnp.zeros((1, 256 - DB), BF16)
    gains = jnp.concatenate(
        [gain_attn[None], jnp.zeros((1, 256 - share), BF16), gain_mlp[None], jnp.zeros((1, FB - 256 - share), BF16)], axis=1
    )
    sent = jnp.concatenate([rows[0:extra], gains, jnp.zeros((SPARE - extra - 1, FB), BF16)], axis=0)
    taken = swap(sent)
    theirs = taken[extra : extra + 1]
    line = jnp.concatenate(
        [theirs[:, 0:share], gain_attn[None], pad, theirs[:, 256 : 256 + share], gain_mlp[None], jnp.zeros((1, FB - 256 - DB), BF16)],
        axis=1,
    )
    attn = jnp.where(
        zero,
        jnp.concatenate([rows, taken[0:extra]], axis=0),
        jnp.concatenate([jnp.broadcast_to(line, (SPARE, FB)), rows[extra:]], axis=0),
    )
    attn = spread_z(attn)
    w_gate, w_up, w_down, attn = lax.optimization_barrier((w_gate, w_up, w_down, attn))
    taken = swap(jnp.where(zero, w_up, w_gate))
    pair = jnp.where(zero, jnp.concatenate([w_gate, taken], axis=0), jnp.concatenate([taken, w_up], axis=0))
    turned = w_down.T
    taken = swap(slab(turned, (1 - core) * (DB - ROWS), ROWS, 0))
    kept = slab(turned, core * (DB - ROWS), ROWS, 0)
    down = jnp.where(zero, jnp.concatenate([kept, taken], axis=1), jnp.concatenate([taken, kept], axis=1))
    attn = spread_plane(attn)
    attn_other = spread_core(attn)
    pair = spread_plane(spread_z(pair))
    pair_other = spread_core(pair)
    down = spread_plane(spread_z(down))
    down_other = spread_core(down)
    return attn + attn_other, pair + pair_other, down + down_other


def in_pieces(blocks):
    return (blocks[0], blocks[1], blocks[2], blocks[3, 0:2], blocks[3, 2:4])


def gather_any(gain_attn, w_query, w_key, w_value, w_out, gain_mlp, w_gate, w_up, w_down):
    def whole(weight):
        return lax.all_gather(lax.all_gather(weight, "dp", axis=1, tiled=True), "fsdp", axis=0, tiled=True)

    def blocks(weight):
        return weight.reshape(QUAD, weight.shape[0] // QUAD, QUAD, weight.shape[1] // QUAD).transpose(0, 2, 1, 3)

    attn = jnp.concatenate([blocks(whole(w)) for w in (w_out, w_query, w_key, w_value)], axis=3)
    gains = [lax.all_gather(g, "fsdp", axis=0, tiled=True).reshape(QUAD, 1, 1, DB) for g in (gain_attn, gain_mlp)]
    line = jnp.concatenate(
        [gains[0], jnp.zeros((QUAD, 1, 1, 256 - DB), BF16), gains[1], jnp.zeros((QUAD, 1, 1, FB - 256 - DB), BF16)], axis=3
    )
    line = jnp.broadcast_to(line, (QUAD, QUAD, SPARE, FB))
    attn_two = jnp.concatenate([line, attn[:, :, ROWS:]], axis=2)
    down = blocks(whole(w_down).T).transpose(1, 0, 2, 3)
    pair = [in_pieces(blocks(whole(w))) for w in (w_gate, w_up)]
    return (
        in_pieces(attn[:, :, 0:ROWS]) + in_pieces(attn_two),
        pair[0] + pair[1],
        in_pieces(down[:, :, 0:ROWS]) + in_pieces(down[:, :, DB - ROWS :]),
    )


def on_device(
    near,
    tokens,
    first_len,
    gain_attn,
    w_query,
    w_key,
    w_value,
    w_out,
    gain_mlp,
    w_gate,
    w_up,
    w_down,
    cotangent,
):
    length = tokens.shape[0]
    first = first_len[0]
    weights = (gain_attn, w_query, w_key, w_value, w_out, gain_mlp, w_gate, w_up, w_down)
    if near:
        place = lax.axis_index("fsdp")
        core = place & 1
        idx = tables(place >> 1, lax.axis_index("dp"), core, first)
        attn, pair, down = gather_near(core, *weights)
    else:
        idx = tables(0, 0, 0, first)
        attn, pair, down = gather_any(*weights)
    cosine, sine = rope_tables(first, length)
    (
        weight, gains, n1t, qx, kx, kt, vt, ot, lse, y, n2, n2t,
    ) = call_attention_forward(idx, tokens, cosine, sine, attn[0:5], attn[5:10])
    mixed, h, dgu, dy, dat, ct, gain_two = call_feed(idx, n2, y, cotangent, gains, pair, down)

    halves = gain_two[0].reshape(QUAD, 1, 2, DB // 2)
    row = jnp.pad(halves, ((0, 0), (0, 7), (0, 0), (0, FB // 2 - DB // 2))).reshape(QUAD, 8, FB)
    flat_o = ot.reshape(D, length)
    args_down = (ct, h, flat_o, dat, row)
    down_theirs = call_down_grads(idx, *args_down)[0]
    pair_theirs = call_pair_grads(idx, n2t, dgu)[0]
    if near:
        down_mine = call_down_grads(idx, *args_down, received=swap(down_theirs))
        pair_mine = call_pair_grads(idx, n2t, dgu, received=swap(pair_theirs))
        down_sum = sum_z(sum_plane(down_mine))
        pair_sum = sum_z(sum_plane(pair_mine))
    else:
        down_mine = call_down_grads(idx, *args_down, received=jnp.zeros_like(down_theirs))
        pair_mine = call_pair_grads(idx, n2t, dgu, received=jnp.zeros_like(pair_theirs))

    grad_tokens, turned, gain_one = call_attention_backward(
        idx, tokens, gains, weight, n1t, qx, kx, kt, vt, ot, lse, dat, dy, cosine, sine
    )
    row = jnp.pad(gain_one[0].reshape(QUAD, 1, DB), ((0, 0), (0, 7), (0, 0)))
    qkv_theirs = call_qkv_grads(idx, turned, n1t, row)[0]
    if near:
        qkv_mine = call_qkv_grads(idx, turned, n1t, row, received=swap(qkv_theirs))
        qkv_sum = sum_z(sum_plane(qkv_mine))
        outs = settle_near(core, down_sum, pair_sum, qkv_sum)
    else:
        qkv_mine = call_qkv_grads(idx, turned, n1t, row, received=jnp.zeros_like(qkv_theirs))
        outs = settle_any(down_mine, down_theirs, pair_mine, pair_theirs, qkv_mine, qkv_theirs, gain_one[0], gain_two[0])
    return (mixed, grad_tokens) + outs


def settle_near(core, down_sum, pair_sum, qkv_sum):
    zero = core == 0
    share = DB // 2

    kept = slab(pair_sum, core * share, share, 0)
    taken = swap(slab(pair_sum, (1 - core) * share, share, 0).astype(BF16)).astype(F32)
    grad_gate, grad_up = jnp.where(zero, kept, taken), jnp.where(zero, taken, kept)

    grad_out = jnp.where(zero, down_sum[0:share, FB : FB + DB], down_sum[ROWS - share :, FB : FB + DB])
    half = FB // 2
    kept = slab(down_sum, core * half, half, 1)
    taken = swap(slab(down_sum, (1 - core) * half, half, 1).astype(BF16)).astype(F32)
    upper, lower = jnp.where(zero, kept, taken), jnp.where(zero, taken, kept)
    grad_down = jnp.concatenate([upper, lower[SPARE:]], axis=0).T
    grad_gain_mlp = lower[0, 0:share]

    kept = slab(qkv_sum, core * share, share, 1)
    taken = swap(slab(qkv_sum, (1 - core) * share, share, 1).astype(BF16)).astype(F32)
    upper, lower = jnp.where(zero, kept, taken), jnp.where(zero, taken, kept)
    grad_gain_attn = lower[0]
    rows = jnp.concatenate([upper, lower[SPARE:]], axis=0).T
    return (
        grad_gain_attn, rows[:, 0:QB], rows[:, QB : QB + KB], rows[:, QB + KB :], grad_out,
        grad_gain_mlp, grad_gate, grad_up, grad_down,
    )


def settle_any(down_mine, down_theirs, pair_mine, pair_theirs, qkv_mine, qkv_theirs, gain_one, gain_two):
    def whole(blocks):
        return blocks.transpose(0, 2, 1, 3).reshape(blocks.shape[0] * blocks.shape[2], -1)

    def shard(values):
        values = lax.psum_scatter(values, "fsdp", scatter_dimension=0, tiled=True)
        return lax.psum_scatter(values, "dp", scatter_dimension=1, tiled=True).astype(F32)

    def gain(values):
        values = lax.psum(values, "dp")
        return lax.psum_scatter(values, "fsdp", scatter_dimension=0, tiled=True)

    both = jnp.concatenate([jnp.stack(down_mine), down_theirs[:, :, SPARE:]], axis=2)
    grad_down = shard(whole(both[..., 0:FB].transpose(1, 0, 2, 3)).T)
    grad_out = shard(whole(both[..., FB : FB + DB]))
    grad_gate, grad_up = shard(whole(jnp.stack(pair_mine))), shard(whole(pair_theirs))
    both = jnp.concatenate([jnp.stack(qkv_mine), qkv_theirs[:, :, SPARE:]], axis=2).transpose(0, 1, 3, 2)
    grad_query = shard(whole(both[..., 0:QB]))
    grad_key = shard(whole(both[..., QB : QB + KB]))
    grad_value = shard(whole(both[..., QB + KB :]))
    return (
        gain(gain_one), grad_query, grad_key, grad_value, grad_out, gain(gain_two), grad_gate, grad_up, grad_down,
    )


def solution(mesh):
    sizes = dict(mesh.shape)
    near = sizes["fsdp"] == 8 and sizes["dp"] == QUAD
    in_specs = (
        P(("fsdp", "dp"), None),
        P(("fsdp", "dp")),
        P("fsdp"),
        P("fsdp", "dp"),
        P("fsdp", "dp"),
        P("fsdp", "dp"),
        P("fsdp", "dp"),
        P("fsdp"),
        P("fsdp", "dp"),
        P("fsdp", "dp"),
        P("fsdp", "dp"),
        P(("fsdp", "dp"), None),
    )
    out_specs = (
        P(("fsdp", "dp"), None),
        P(("fsdp", "dp"), None),
        P("fsdp"),
        P("fsdp", "dp"),
        P("fsdp", "dp"),
        P("fsdp", "dp"),
        P("fsdp", "dp"),
        P("fsdp"),
        P("fsdp", "dp"),
        P("fsdp", "dp"),
        P("fsdp", "dp"),
    )
    return jax.shard_map(
        functools.partial(on_device, near), mesh=mesh, in_specs=in_specs, out_specs=out_specs, check_vma=False
    )
```

time: 918 us -> 516 us (0.56)
  matrix products: 255 us -> 0 us
  Pallas kernels: 0 us -> 203 us
  blocking collectives: 162 us -> 0 us
  waiting for transfers between devices: 345 us -> 188 us
  other arithmetic: 87 us -> 14.8 us
  starting transfers between devices: 1.21 us -> 68.2 us
  between operations: 17.6 us -> 2.35 us
    dot_general x33 -> x0, matrix products: 255 us -> none  [the longest x7 55.1 us: product_right(): lax.dot_general(left, right, (((1,), (1,)), ((), ())), preferred_element_...]
    reduce_scatter x7 -> x0, waiting for transfers between devices: 238 us -> none  [the longest x1 56.9 us: on_device(): lax.psum_scatter(grad_up_w.astype(jnp.bfloat16), 'fsdp', scatter_dimensio...]
    pallas_call x0 -> x9, Pallas kernels: none -> 203 us  [the longest x1 54.7 us: call_feed(): pl.pallas_call(feed, out_shape=(s((length, D), BF16), s((QUAD, length, FB...]
    ppermute x0 -> x63, waiting for transfers between devices: none -> 188 us  [the longest x9 44.4 us: to_z(): lax.ppermute(values, 'dp', [(j, (j + k) % QUAD) for j in range(QUAD)])]
    all_gather x9 -> x0, blocking collectives: 119 us -> none  [the longest x1 16.6 us: on_device(): lax.all_gather(attention_part[2], 'fsdp', axis=0, tiled=True)]
    unnamed x24 -> x0, waiting for transfers between devices: 107 us -> none
    ppermute x0 -> x63, starting transfers between devices: none -> 68.2 us  [the longest x24 21.8 us: swap(): return lax.ppermute(values, 'fsdp', CORE)]
    convert_element_type x20 -> x4, other arithmetic: 56 us -> 5.03 us  [the longest x3 5.03 us: sum_plane(): return add(got).astype(BF16)]
  transfers between devices with their start and end apart: 18 -> 63, of which waited for: 12 -> 29; matrix products, arithmetic and copies ran while one was open for 24% -> 7% of each run, Pallas kernels for 0% -> 27%
where the time goes in v1:
time: 516 us; the launch traced here: 509 us
  Pallas kernels  203 us (39%)
  waiting for transfers between devices  188 us (36%)
  starting transfers between devices  68.2 us (13%)
  local copies, waits for them, and re-layouts  32 us (6%)
  other arithmetic  14.8 us (3%)
    pallas_call x1, Pallas kernels, call_feed(): pl.pallas_call(feed, out_shape=(s((length, D), BF16), s((QUAD, length, FB...  54.7 us
    pallas_call x1, Pallas kernels, call_attention_backward(): pl.pallas_call(attention_backward, out_shape=(s((length, D), BF16), s((QU...  48.1 us
    ppermute x9, waiting for transfers between devices, to_z(): lax.ppermute(values, 'dp', [(j, (j + k) % QUAD) for j in range(QUAD)])  44.4 us
    ppermute x3, waiting for transfers between devices, sum_plane(): lax.ppermute(blocks[3], 'fsdp', ACROSS)  42.9 us
    ppermute x9, waiting for transfers between devices, from_z(): lax.ppermute(values, 'dp', [(j, (j - k) % QUAD) for j in range(QUAD)])  42.3 us
    pallas_call x1, Pallas kernels, call_attention_forward(): pl.pallas_call(attention_forward, out_shape=(s((QUAD, D, FB), BF16), s((8...  39.1 us
    pallas_call x2, Pallas kernels, call_down_grads(): pl.pallas_call(functools.partial(down_grads, 10 if received is None else...  25 us
    pallas_call x2, Pallas kernels, call_pair_grads(): pl.pallas_call(functools.partial(pair_grads, 1 if received is None else 0...  22.1 us
  transfers between devices with their start and end apart: 63, of which 29 were waited for; matrix products, arithmetic and copies ran while one was open for 7% of the time, Pallas kernels for 27%

profile of v1, /device:TPU:9, one launch (start us, length us, event | category | flops | bytes accessed | tf_op | source)
XLA Modules:
  0.0 509.3 jit_solution(16913244800940093097)
XLA Ops:
  13.4 7.0 %collective-permute-done.2 = bf16[128,640]{1,0:T(8,128)(2,1)S(1)} collective-permute-done((bf16[128,640]{1,0:T(8,128)(2,1)S(1)}, bf16[128,640]{1,0:T(8,128)(2,1)S(1)}, u32[]{:S(2)}, u32[]{:S(2)}) %collective-permute-start.2) | collective-permute-done | bytes 163872 | tf_op jit(solution)/shard_map/ppermute | solution.py:628
  20.4 3.5 collective-permute-done.3
  34.3 17.9 %collective-permute-done.28 = bf16[128,640]{1,0:T(8,128)(2,1)S(1)} collective-permute-done((bf16[128,640]{1,0:T(8,128)(2,1)S(1)}, bf16[128,640]{1,0:T(8,128)(2,1)S(1)}, u32[]{:S(2)}, u32[]{:S(2)}) %collective-permute-start.28) | collective-permute-done | bytes 163872 | tf_op jit(solution)/shard_map/ppermute | solution.py:628
  53.5 8.8 %collective-permute-done.29 = bf16[128,640]{1,0:T(8,128)(2,1)S(1)} collective-permute-done((bf16[128,640]{1,0:T(8,128)(2,1)S(1)}, bf16[128,640]{1,0:T(8,128)(2,1)S(1)}, u32[]{:S(2)}, u32[]{:S(2)}) %collective-permute-start.29) | collective-permute-done | bytes 163872 | tf_op jit(solution)/shard_map/ppermute | solution.py:628
  66.7 4.0 collective-permute-done.16
  75.4 6.4 %collective-permute-done.31.rest_12_ = bf16[4,128,640]{2,1,0:T(8,128)(2,1)} collective-permute-done((bf16[4,128,640]{2,1,0:T(8,128)(2,1)S(1)}, bf16[4,128,640]{2,1,0:T(8,128)(2,1)}, u32[]{:S(2)}, u32[]{:S(2)}) %collective-permute-start.31) | collective-permute-done | bytes 655392 | tf_op jit(solution)/shard_map/ppermute | solution.py:641
  83.1 2.7 collective-permute-done.30.rest_11_
  94.0 21.1 %collective-permute-done.7.rest_4_ = bf16[2,128,640]{2,1,0:T(8,128)(2,1)S(1)} collective-permute-done((bf16[2,128,640]{2,1,0:T(8,128)(2,1)S(1)}, bf16[2,128,640]{2,1,0:T(8,128)(2,1)S(1)}, u32[]{:S(2)}, u32[]{:S(2)}) %collective-permute-start.7) | collective-permute-done | bytes 327712 | tf_op jit(solution)/shard_map/ppermute | solution.py:643
  116.4 9.8 %collective-permute-done.32.rest_13_ = bf16[2,128,640]{2,1,0:T(8,128)(2,1)} collective-permute-done((bf16[2,128,640]{2,1,0:T(8,128)(2,1)S(1)}, bf16[2,128,640]{2,1,0:T(8,128)(2,1)}, u32[]{:S(2)}, u32[]{:S(2)}) %collective-permute-start.32) | collective-permute-done | bytes 327712 | tf_op jit(solution)/shard_map/ppermute | solution.py:642
  141.3 4.0 copy.28.c_ref
  153.4 39.1 %attention_forward.1 = (bf16[4,960,640]{2,1,0:T(8,128)(2,1)}, f32[8,960]{1,0:T(8,128)}, bf16[960,1024]{1,0:T(8,128)(2,1)}, bf16[15,128,1024]{2,1,0:T(8,128)(2,1)...) custom-call(s32[16]{0:T(128)} %stack.82.idx, ...), custom_call_target="tpu_custom_call" | custom-call | flops 20000000000 | bytes 30000000 | tf_op jit(solution)/shard_map/attention_forward/pallas_call | solution.py:226
  193.4 54.7 %feed_forward_backward.1 = (bf16[1024,960]{1,0:T(8,128)(2,1)}, bf16[4,1024,640]{2,1,0:T(8,128)(2,1)}, bf16[2,4,1024,640]{3,2,1,0:T(8,128)(2,1)}, f32[1024,960]{1...) custom-call(s32[16]{0:T(128)} %stack.82.idx, ...), custom_call_target="tpu_custom_call" | custom-call | flops 30000001024 | bytes 50000000 | tf_op jit(solution)/shard_map/feed_forward_backward/pallas_call | solution.py:310
  249.7 12.3 %down_grads.2 = bf16[4,4,128,896]{3,2,1,0:T(8,128)(2,1)} custom-call(s32[16]{0:T(128)} %stack.82.idx, bf16[960,1024]{1,0:T(8,128)(2,1)} %get-tuple-element.74.ct_ref, bf16[4,1024,640]{2,1,0:T(8,128)(2,1)} %get-tuple-element.75.h_ref, bf16[960,1024]{1,0:T(8,128)(2,1)} %bitcast.83, bf16[960,1024]{1,0:T(8,128)(2,1)} %get-tuple-element.65.dat_ref, ...), custom_call_target="tpu_custom_call" | custom-call | flops 4000000000 | bytes 15000000 | tf_op jit(solution)/shard_map/down_grads/pallas_call | solution.py:440
  262.1 10.8 %pair_grads.2 = bf16[4,4,240,640]{3,2,1,0:T(8,128)(2,1)} custom-call(s32[16]{0:T(128)} %stack.82.idx, bf16[960,1024]{1,0:T(8,128)(2,1)} %get-tuple-element.81.n2t_ref, bf16[2,4,1024,640]{3,2,1,0:T(8,128)(2,1)} %get-tuple-element.82.d_ref), custom_call_target="tpu_custom_call" | custom-call | flops 5000000000 | bytes 15000000 | tf_op jit(solution)/shard_map/pair_grads/pallas_call | solution.py:379
  273.4 48.1 %attention_backward.1 = (bf16[1024,960]{1,0:T(8,128)(2,1)}, bf16[4,512,1024]{2,1,0:T(8,128)(2,1)}, f32[8,960]{1,0:T(8,128)}) custom-call(s32[16]{0:T(128)} %stack.82.idx, bf16[1024,960]{1,0:T(8,128)(2,1)} %copy.25.x_ref, f32[8,960]{1,0:T(8,128)} %get-tuple-element.52.gain_ref, bf16[4,960,640]{2,1,0:T(8,128)(2,1)} %get-tuple-element.57.weight, ...), custom_call_target="tpu_custom_call" | custom-call | flops 30000001024 | bytes 30000000 | tf_op jit(solution)/shard_map/attention_backward/pallas_call | solution.py:546
  323.0 7.1 %qkv_grads.2 = bf16[4,4,208,240]{3,2,1,0:T(8,128)(2,1)} custom-call(s32[16]{0:T(128)} %stack.82.idx, bf16[4,512,1024]{2,1,0:T(8,128)(2,1)} %get-tuple-element.68.z_ref, bf16[960,1024]{1,0:T(8,128)(2,1)} %get-tuple-element.58.n1t_ref, f32[4,8,240]{2,1,0:T(8,128)} %pad.8.gg_ref), custom_call_target="tpu_custom_call" | custom-call | flops 3000000000 | bytes 10000000 | tf_op jit(solution)/shard_map/qkv_grads/pallas_call | solution.py:605
  330.1 3.8 collective-permute-done.39.rest_0_
  335.1 7.2 %qkv_grads.3 = (bf16[4,208,240]{2,1,0:T(8,128)(2,1)}, bf16[4,208,240]{2,1,0:T(8,128)(2,1)}, bf16[4,208,240]{2,1,0:T(8,128)(2,1)}, bf16[4,208,240]{2,1,0:T(8,128)(2,1)}) custom-call(s32[16]{0:T(128)} %stack.82.idx, bf16[4,512,1024]{2,1,0:T(8,128)(2,1)} %get-tuple-element.68.z_ref, bf16[960,1024]{1,0:T(8,128)(2,1)} %get-tuple-element.58.n1t_ref, ...), custom_call_target="tpu_custom_call" | custom-call | flops 3000000000 | bytes 10000000 | tf_op jit(solution)/shard_map/qkv_grads/pallas_call | solution.py:605
  345.0 12.7 %down_grads.3 = (bf16[4,128,896]{2,1,0:T(8,128)(2,1)}, bf16[4,128,896]{2,1,0:T(8,128)(2,1)}, bf16[4,128,896]{2,1,0:T(8,128)(2,1)}, bf16[4,128,896]{2,1,0:T(8,128)(2,1)}) custom-call(s32[16]{0:T(128)} %stack.82.idx, bf16[960,1024]{1,0:T(8,128)(2,1)} %get-tuple-element.74.ct_ref, bf16[4,1024,640]{2,1,0:T(8,128)(2,1)} %get-tuple-element.75.h_ref, ...), custom_call_target="tpu_custom_call" | custom-call | flops 4000000000 | bytes 15000000 | tf_op jit(solution)/shard_map/down_grads/pallas_call | solution.py:440
  360.4 3.5 collective-permute-done.42
  371.0 3.6 collective-permute-done.44
  376.1 4.1 copy.32
  383.7 6.7 %collective-permute-start.46 = (bf16[208,120]{1,0:T(8,128)(2,1)S(1)}, bf16[208,120]{1,0:T(8,128)(2,1)S(1)}, u32[]{:S(2)}, u32[]{:S(2)}) collective-permute-start(bf16[208,120]{1,0:T(8,128)(2,1)S(1)} %dynamic-slice_convert_fusion.2), channel_id=1, source_target_pairs={{0,4},{4,0},{8,12},{12,8},{16,20},{20,16},{24,28},{28,24},{1,5},{5... | collective-permute-start | bytes 149768 | tf_op jit(solution)/shard_map/ppermute | solution.py:624
  390.4 12.9 %collective-permute-done.50 = bf16[4,128,896]{2,1,0:T(8,128)(2,1)} collective-permute-done((bf16[4,128,896]{2,1,0:T(8,128)(2,1)}, bf16[4,128,896]{2,1,0:T(8,128)(2,1)}, u32[]{:S(2)}, u32[]{:S(2)}) %collective-permute-start.50) | collective-permute-done | bytes 917536 | tf_op jit(solution)/shard_map/ppermute | solution.py:660
  407.8 11.3 %pair_grads.3 = (bf16[4,240,640]{2,1,0:T(8,128)(2,1)}, bf16[4,240,640]{2,1,0:T(8,128)(2,1)}, bf16[4,240,640]{2,1,0:T(8,128)(2,1)}, bf16[4,240,640]{2,1,0:T(8,128)(2,1)}) custom-call(s32[16]{0:T(128)} %stack.82.idx, bf16[960,1024]{1,0:T(8,128)(2,1)} %get-tuple-element.81.n2t_ref, bf16[2,4,1024,640]{3,2,1,0:T(8,128)(2,1)} %get-tuple-element.82.d_ref, ...), custom_call_target="tpu_custom_call" | custom-call | flops 5000000000 | bytes 15000000 | tf_op jit(solution)/shard_map/pair_grads/pallas_call | solution.py:379
  425.4 13.4 %collective-permute-done.52 = bf16[128,896]{1,0:T(8,128)(2,1)S(1)} collective-permute-done((bf16[128,896]{1,0:T(8,128)(2,1)S(1)}, bf16[128,896]{1,0:T(8,128)(2,1)S(1)}, u32[]{:S(2)}, u32[]{:S(2)}) %collective-permute-start.52) | collective-permute-done | bytes 229408 | tf_op jit(solution)/shard_map/ppermute | solution.py:632
  441.3 5.3 %collective-permute-done.56 = bf16[4,240,640]{2,1,0:T(8,128)(2,1)} collective-permute-done((bf16[4,240,640]{2,1,0:T(8,128)(2,1)}, bf16[4,240,640]{2,1,0:T(8,128)(2,1)}, u32[]{:S(2)}, u32[]{:S(2)}) %collective-permute-start.56) | collective-permute-done | bytes 1228832 | tf_op jit(solution)/shard_map/ppermute | solution.py:658
  447.2 26.4 %collective-permute-done.58 = bf16[4,240,640]{2,1,0:T(8,128)(2,1)} collective-permute-done((bf16[4,240,640]{2,1,0:T(8,128)(2,1)}, bf16[4,240,640]{2,1,0:T(8,128)(2,1)}, u32[]{:S(2)}, u32[]{:S(2)}) %collective-permute-start.58) | collective-permute-done | bytes 1228832 | tf_op jit(solution)/shard_map/ppermute | solution.py:660
  473.6 2.6 add_convert_fusion
  480.8 2.9 collective-permute-done.59
  483.7 18.0 %collective-permute-done.60 = bf16[240,640]{1,0:T(8,128)(2,1)S(1)} collective-permute-done((bf16[240,640]{1,0:T(8,128)(2,1)S(1)}, bf16[240,640]{1,0:T(8,128)(2,1)S(1)}, u32[]{:S(2)}, u32[]{:S(2)}) %collective-permute-start.60) | collective-permute-done | bytes 307232 | tf_op jit(solution)/shard_map/ppermute | solution.py:632
  501.6 4.6 collective-permute-done.61
  (242 shorter events, 110.4 us)
Async XLA Ops:
  27.5 44.4 %collective-permute-start.5 = (bf16[4,128,640]{2,1,0:T(8,128)(2,1)S(1)}, bf16[4,128,640]{2,1,0:T(8,128)(2,1)S(1)}, u32[]{:S(2)}, u32[]{:S(2)}) collective-permute-start(bf16[4,128,640]{2,1,0:T(8,128)(2,1)S(1)} %pad_maximum_fusion.1.rest_0_), channel_id=1, source_target_pairs={{0,16},{4,20},{8,24},{12,28},{16,0},{20,4},{24,8},{28,12},{1,17},{... | collective-permute-start | bytes 1966088 | tf_op jit(solution)/shard_map/ppermute | solution.py:641
  28.8 23.4 %collective-permute-start.28 = (bf16[128,640]{1,0:T(8,128)(2,1)S(1)}, bf16[128,640]{1,0:T(8,128)(2,1)S(1)}, u32[]{:S(2)}, u32[]{:S(2)}) collective-permute-start(bf16[128,640]{1,0:T(8,128)(2,1)S(1)} %maximum_select_fusion.5), channel_id=1, source_target_pairs={{0,2},{1,3},{2,0},{3,1},{4,6},{5,7},{6,4},{7,5},{8,10},{9,11},{10,... | collective-permute-start | bytes 491528 | tf_op jit(solution)/shard_map/ppermute | solution.py:628
  31.4 33.2 %collective-permute-start.14 = (bf16[240,640]{1,0:T(8,128)(2,1)S(1)}, bf16[240,640]{1,0:T(8,128)(2,1)S(1)}, u32[]{:S(2)}, u32[]{:S(2)}) collective-permute-start(bf16[240,640]{1,0:T(8,128)(2,1)S(1)} %maximum_select_fusion.1), channel_id=1, source_target_pairs={{0,3},{1,0},{2,1},{3,2},{4,7},{5,4},{6,5},{7,6},{8,11},{9,8},{10,9... | collective-permute-start | bytes 921608 | tf_op jit(solution)/shard_map/ppermute | solution.py:628
  31.5 33.9 %collective-permute-start.15 = (bf16[240,640]{1,0:T(8,128)(2,1)S(1)}, bf16[240,640]{1,0:T(8,128)(2,1)S(1)}, u32[]{:S(2)}, u32[]{:S(2)}) collective-permute-start(bf16[240,640]{1,0:T(8,128)(2,1)S(1)} %maximum_select_fusion.1), channel_id=1, source_target_pairs={{0,2},{1,3},{2,0},{3,1},{4,6},{5,7},{6,4},{7,5},{8,10},{9,11},{10,... | collective-permute-start | bytes 921608 | tf_op jit(solution)/shard_map/ppermute | solution.py:628
  33.2 29.1 %collective-permute-start.29 = (bf16[128,640]{1,0:T(8,128)(2,1)S(1)}, bf16[128,640]{1,0:T(8,128)(2,1)S(1)}, u32[]{:S(2)}, u32[]{:S(2)}) collective-permute-start(bf16[128,640]{1,0:T(8,128)(2,1)S(1)} %maximum_select_fusion.5), channel_id=1, source_target_pairs={{0,1},{1,2},{2,3},{3,0},{4,5},{5,6},{6,7},{7,4},{8,9},{9,10},{10,1... | collective-permute-start | bytes 491528 | tf_op jit(solution)/shard_map/ppermute | solution.py:628
  52.1 21.4 %collective-permute-start.4 = (bf16[4,128,640]{2,1,0:T(8,128)(2,1)S(1)}, bf16[4,128,640]{2,1,0:T(8,128)(2,1)S(1)}, u32[]{:S(2)}, u32[]{:S(2)}) collective-permute-start(bf16[4,128,640]{2,1,0:T(8,128)(2,1)S(1)} %pad_maximum_fusion.1.rest_0_), channel_id=1, source_target_pairs={{0,8},{4,12},{8,0},{12,4},{16,24},{20,28},{24,16},{28,20},{1,9},{5... | collective-permute-start | bytes 1966088 | tf_op jit(solution)/shard_map/ppermute | solution.py:640
  71.9 17.1 %collective-permute-start.34 = (bf16[4,128,640]{2,1,0:T(8,128)(2,1)S(1)}, bf16[4,128,640]{2,1,0:T(8,128)(2,1)S(1)}, u32[]{:S(2)}, u32[]{:S(2)}) collective-permute-start(bf16[4,128,640]{2,1,0:T(8,128)(2,1)S(1)} %pad_maximum_fusion.2.rest_10_), channel_id=1, source_target_pairs={{0,4},{4,0},{8,12},{12,8},{16,20},{20,16},{24,28},{28,24},{1,5},{5... | collective-permute-start | bytes 1966088 | tf_op jit(solution)/shard_map/ppermute | solution.py:624
  73.6 19.1 %collective-permute-start.6 = (bf16[2,128,640]{2,1,0:T(8,128)(2,1)S(1)}, bf16[2,128,640]{2,1,0:T(8,128)(2,1)S(1)}, u32[]{:S(2)}, u32[]{:S(2)}) collective-permute-start(bf16[2,128,640]{2,1,0:T(8,128)(2,1)S(1)} %slice.144), channel_id=1, source_target_pairs={{0,8},{4,12},{8,0},{12,4},{16,24},{20,28},{24,16},{28,20},{1,9},{5... | collective-permute-start | bytes 983048 | tf_op jit(solution)/shard_map/ppermute | solution.py:642
  74.1 57.7 %collective-permute-start.18 = (bf16[4,240,640]{2,1,0:T(8,128)(2,1)S(1)}, bf16[4,240,640]{2,1,0:T(8,128)(2,1)S(1)}, u32[]{:S(2)}, u32[]{:S(2)}) collective-permute-start(bf16[4,240,640]{2,1,0:T(8,128)(2,1)S(1)} %pad_maximum_fusion.rest_0_), channel_id=1, source_target_pairs={{0,16},{4,20},{8,24},{12,28},{16,0},{20,4},{24,8},{28,12},{1,17},{... | collective-permute-start | bytes 3686408 | tf_op jit(solution)/shard_map/ppermute | solution.py:641
  81.8 50.2 %collective-permute-start.17 = (bf16[4,240,640]{2,1,0:T(8,128)(2,1)S(1)}, bf16[4,240,640]{2,1,0:T(8,128)(2,1)S(1)}, u32[]{:S(2)}, u32[]{:S(2)}) collective-permute-start(bf16[4,240,640]{2,1,0:T(8,128)(2,1)S(1)} %pad_maximum_fusion.rest_0_), channel_id=1, source_target_pairs={{0,8},{4,12},{8,0},{12,4},{16,24},{20,28},{24,16},{28,20},{1,9},{5... | collective-permute-start | bytes 3686408 | tf_op jit(solution)/shard_map/ppermute | solution.py:640
  85.8 29.3 %collective-permute-start.7 = (bf16[2,128,640]{2,1,0:T(8,128)(2,1)S(1)}, bf16[2,128,640]{2,1,0:T(8,128)(2,1)S(1)}, u32[]{:S(2)}, u32[]{:S(2)}) collective-permute-start(bf16[2,128,640]{2,1,0:T(8,128)(2,1)S(1)} %slice.145), channel_id=1, source_target_pairs={{0,16},{4,20},{8,24},{12,28},{16,0},{20,4},{24,8},{28,12},{1,17},{... | collective-permute-start | bytes 983048 | tf_op jit(solution)/shard_map/ppermute | solution.py:643
  89.1 37.1 %collective-permute-start.32 = (bf16[2,128,640]{2,1,0:T(8,128)(2,1)S(1)}, bf16[2,128,640]{2,1,0:T(8,128)(2,1)}, u32[]{:S(2)}, u32[]{:S(2)}) collective-permute-start(bf16[2,128,640]{2,1,0:T(8,128)(2,1)S(1)} %slice.148), channel_id=1, source_target_pairs={{0,8},{4,12},{8,0},{12,4},{16,24},{20,28},{24,16},{28,20},{1,9},{5... | collective-permute-start | bytes 983048 | tf_op jit(solution)/shard_map/ppermute | solution.py:642
  92.7 35.6 %collective-permute-start.33 = (bf16[2,128,640]{2,1,0:T(8,128)(2,1)S(1)}, bf16[2,128,640]{2,1,0:T(8,128)(2,1)S(1)}, u32[]{:S(2)}, u32[]{:S(2)}) collective-permute-start(bf16[2,128,640]{2,1,0:T(8,128)(2,1)S(1)} %slice.149), channel_id=1, source_target_pairs={{0,16},{4,20},{8,24},{12,28},{16,0},{20,4},{24,8},{28,12},{1,17},{... | collective-permute-start | bytes 983048 | tf_op jit(solution)/shard_map/ppermute | solution.py:643
  148.1 44.5 %collective-permute-start.21 = (bf16[4,240,640]{2,1,0:T(8,128)(2,1)S(1)}, bf16[4,240,640]{2,1,0:T(8,128)(2,1)}, u32[]{:S(2)}, u32[]{:S(2)}) collective-permute-start(bf16[4,240,640]{2,1,0:T(8,128)(2,1)S(1)} %pad_maximum_fusion.rest_0_), channel_id=1, source_target_pairs={{0,4},{4,0},{8,12},{12,8},{16,20},{20,16},{24,28},{28,24},{1,5},{5... | collective-permute-start | bytes 3686408 | tf_op jit(solution)/shard_map/ppermute | solution.py:624
  148.4 44.2 %collective-permute-start.22 = (bf16[4,240,640]{2,1,0:T(8,128)(2,1)}, bf16[4,240,640]{2,1,0:T(8,128)(2,1)}, u32[]{:S(2)}, u32[]{:S(2)}) collective-permute-start(bf16[4,240,640]{2,1,0:T(8,128)(2,1)} %copy-done.12), channel_id=1, source_target_pairs={{0,4},{4,0},{8,12},{12,8},{16,20},{20,16},{24,28},{28,24},{1,5},{5... | collective-permute-start | bytes 3686408 | tf_op jit(solution)/shard_map/ppermute | solution.py:624
  148.6 44.0 %collective-permute-start.23 = (bf16[4,240,640]{2,1,0:T(8,128)(2,1)S(1)}, bf16[4,240,640]{2,1,0:T(8,128)(2,1)}, u32[]{:S(2)}, u32[]{:S(2)}) collective-permute-start(bf16[4,240,640]{2,1,0:T(8,128)(2,1)S(1)} %copy-done.11), channel_id=1, source_target_pairs={{0,4},{4,0},{8,12},{12,8},{16,20},{20,16},{24,28},{28,24},{1,5},{5... | collective-permute-start | bytes 3686408 | tf_op jit(solution)/shard_map/ppermute | solution.py:624
  150.4 42.2 %collective-permute-start.24 = (bf16[2,240,640]{2,1,0:T(8,128)(2,1)}, bf16[2,240,640]{2,1,0:T(8,128)(2,1)S(1)}, u32[]{:S(2)}, u32[]{:S(2)}) collective-permute-start(bf16[2,240,640]{2,1,0:T(8,128)(2,1)} %collective-permute-done.19.rest_3_), channel_id=1, source_target_pairs={{0,4},{4,0},{8,12},{12,8},{16,20},{20,16},{24,28},{28,24},{1,5},{5... | collective-permute-start | bytes 1843208 | tf_op jit(solution)/shard_map/ppermute | solution.py:624
  152.1 40.5 %collective-permute-start.25 = (bf16[2,240,640]{2,1,0:T(8,128)(2,1)}, bf16[2,240,640]{2,1,0:T(8,128)(2,1)}, u32[]{:S(2)}, u32[]{:S(2)}) collective-permute-start(bf16[2,240,640]{2,1,0:T(8,128)(2,1)} %collective-permute-done.20.rest_4_), channel_id=1, source_target_pairs={{0,4},{4,0},{8,12},{12,8},{16,20},{20,16},{24,28},{28,24},{1,5},{5... | collective-permute-start | bytes 1843208 | tf_op jit(solution)/shard_map/ppermute | solution.py:624
  262.1 82.9 %collective-permute-start.47 = (bf16[4,4,128,896]{3,2,1,0:T(8,128)(2,1)}, bf16[4,4,128,896]{3,2,1,0:T(8,128)(2,1)}, u32[]{:S(2)}, u32[]{:S(2)}) collective-permute-start(bf16[4,4,128,896]{3,2,1,0:T(8,128)(2,1)} %down_grads.2), channel_id=1, source_target_pairs={{0,4},{4,0},{8,12},{12,8},{16,20},{20,16},{24,28},{28,24},{1,5},{5... | collective-permute-start | bytes 11010056 | tf_op jit(solution)/shard_map/ppermute | solution.py:624
  272.9 134.9 %collective-permute-start.55 = (bf16[4,4,240,640]{3,2,1,0:T(8,128)(2,1)}, bf16[4,4,240,640]{3,2,1,0:T(8,128)(2,1)}, u32[]{:S(2)}, u32[]{:S(2)}) collective-permute-start(bf16[4,4,240,640]{3,2,1,0:T(8,128)(2,1)} %pair_grads.2), channel_id=1, source_target_pairs={{0,4},{4,0},{8,12},{12,8},{16,20},{20,16},{24,28},{28,24},{1,5},{5... | collective-permute-start | bytes 14745608 | tf_op jit(solution)/shard_map/ppermute | solution.py:624
  344.3 19.6 %collective-permute-start.42 = (bf16[4,208,240]{2,1,0:T(8,128)(2,1)}, bf16[4,208,240]{2,1,0:T(8,128)(2,1)S(1)}, u32[]{:S(2)}, u32[]{:S(2)}) collective-permute-start(bf16[4,208,240]{2,1,0:T(8,128)(2,1)} %get-tuple-element.73), channel_id=1, source_target_pairs={{0,24},{4,28},{8,16},{12,20},{16,8},{20,12},{24,0},{28,4},{1,25},{... | collective-permute-start | bytes 1198088 | tf_op jit(solution)/shard_map/ppermute | solution.py:660
  357.7 32.7 %collective-permute-start.48 = (bf16[4,128,896]{2,1,0:T(8,128)(2,1)}, bf16[4,128,896]{2,1,0:T(8,128)(2,1)}, u32[]{:S(2)}, u32[]{:S(2)}) collective-permute-start(bf16[4,128,896]{2,1,0:T(8,128)(2,1)} %get-tuple-element.78), channel_id=1, source_target_pairs={{0,8},{4,12},{8,0},{12,4},{16,24},{20,28},{24,16},{28,20},{1,9},{5... | collective-permute-start | bytes 2752520 | tf_op jit(solution)/shard_map/ppermute | solution.py:658
  358.5 31.9 %collective-permute-start.49 = (bf16[4,128,896]{2,1,0:T(8,128)(2,1)}, bf16[4,128,896]{2,1,0:T(8,128)(2,1)}, u32[]{:S(2)}, u32[]{:S(2)}) collective-permute-start(bf16[4,128,896]{2,1,0:T(8,128)(2,1)} %get-tuple-element.79), channel_id=1, source_target_pairs={{0,16},{4,20},{8,24},{12,28},{16,0},{20,4},{24,8},{28,12},{1,17},{... | collective-permute-start | bytes 2752520 | tf_op jit(solution)/shard_map/ppermute | solution.py:659
  359.8 43.6 %collective-permute-start.50 = (bf16[4,128,896]{2,1,0:T(8,128)(2,1)}, bf16[4,128,896]{2,1,0:T(8,128)(2,1)}, u32[]{:S(2)}, u32[]{:S(2)}) collective-permute-start(bf16[4,128,896]{2,1,0:T(8,128)(2,1)} %get-tuple-element.80), channel_id=1, source_target_pairs={{0,24},{4,28},{8,16},{12,20},{16,8},{20,12},{24,0},{28,4},{1,25},{... | collective-permute-start | bytes 2752520 | tf_op jit(solution)/shard_map/ppermute | solution.py:660
  383.7 38.1 %collective-permute-start.46 = (bf16[208,120]{1,0:T(8,128)(2,1)S(1)}, bf16[208,120]{1,0:T(8,128)(2,1)S(1)}, u32[]{:S(2)}, u32[]{:S(2)}) collective-permute-start(bf16[208,120]{1,0:T(8,128)(2,1)S(1)} %dynamic-slice_convert_fusion.2), channel_id=1, source_target_pairs={{0,4},{4,0},{8,12},{12,8},{16,20},{20,16},{24,28},{28,24},{1,5},{5... | collective-permute-start | bytes 149768 | tf_op jit(solution)/shard_map/ppermute | solution.py:624
  405.6 18.2 %collective-permute-start.51 = (bf16[128,896]{1,0:T(8,128)(2,1)S(1)}, bf16[128,896]{1,0:T(8,128)(2,1)S(1)}, u32[]{:S(2)}, u32[]{:S(2)}) collective-permute-start(bf16[128,896]{1,0:T(8,128)(2,1)S(1)} %get-tuple-element.101), channel_id=1, source_target_pairs={{0,1},{1,2},{2,3},{3,0},{4,5},{5,6},{6,7},{7,4},{8,9},{9,10},{10,1... | collective-permute-start | bytes 688136 | tf_op jit(solution)/shard_map/ppermute | solution.py:632
  419.1 27.6 %collective-permute-start.56 = (bf16[4,240,640]{2,1,0:T(8,128)(2,1)}, bf16[4,240,640]{2,1,0:T(8,128)(2,1)}, u32[]{:S(2)}, u32[]{:S(2)}) collective-permute-start(bf16[4,240,640]{2,1,0:T(8,128)(2,1)} %get-tuple-element.84), channel_id=1, source_target_pairs={{0,8},{4,12},{8,0},{12,4},{16,24},{20,28},{24,16},{28,20},{1,9},{5... | collective-permute-start | bytes 3686408 | tf_op jit(solution)/shard_map/ppermute | solution.py:658
  419.9 27.3 %collective-permute-start.57 = (bf16[4,240,640]{2,1,0:T(8,128)(2,1)}, bf16[4,240,640]{2,1,0:T(8,128)(2,1)}, u32[]{:S(2)}, u32[]{:S(2)}) collective-permute-start(bf16[4,240,640]{2,1,0:T(8,128)(2,1)} %get-tuple-element.85), channel_id=1, source_target_pairs={{0,16},{4,20},{8,24},{12,28},{16,0},{20,4},{24,8},{28,12},{1,17},{... | collective-permute-start | bytes 3686408 | tf_op jit(solution)/shard_map/ppermute | solution.py:659
  420.8 52.8 %collective-permute-start.58 = (bf16[4,240,640]{2,1,0:T(8,128)(2,1)}, bf16[4,240,640]{2,1,0:T(8,128)(2,1)}, u32[]{:S(2)}, u32[]{:S(2)}) collective-permute-start(bf16[4,240,640]{2,1,0:T(8,128)(2,1)} %get-tuple-element.86), channel_id=1, source_target_pairs={{0,24},{4,28},{8,16},{12,20},{16,8},{20,12},{24,0},{28,4},{1,25},{... | collective-permute-start | bytes 3686408 | tf_op jit(solution)/shard_map/ppermute | solution.py:660
  440.0 39.7 %collective-permute-start.54 = (bf16[128,320]{1,0:T(8,128)(2,1)S(1)}, bf16[128,320]{1,0:T(8,128)(2,1)S(1)}, u32[]{:S(2)}, u32[]{:S(2)}) collective-permute-start(bf16[128,320]{1,0:T(8,128)(2,1)S(1)} %dynamic-slice_convert_fusion.1), channel_id=1, source_target_pairs={{0,4},{4,0},{8,12},{12,8},{16,20},{20,16},{24,28},{28,24},{1,5},{5... | collective-permute-start | bytes 245768 | tf_op jit(solution)/shard_map/ppermute | solution.py:624
  477.5 24.2 %collective-permute-start.60 = (bf16[240,640]{1,0:T(8,128)(2,1)S(1)}, bf16[240,640]{1,0:T(8,128)(2,1)S(1)}, u32[]{:S(2)}, u32[]{:S(2)}) collective-permute-start(bf16[240,640]{1,0:T(8,128)(2,1)S(1)} %get-tuple-element.100), channel_id=1, source_target_pairs={{0,2},{1,3},{2,0},{3,1},{4,6},{5,7},{6,4},{7,5},{8,10},{9,11},{10,... | collective-permute-start | bytes 921608 | tf_op jit(solution)/shard_map/ppermute | solution.py:632
  478.5 27.7 %collective-permute-start.61 = (bf16[240,640]{1,0:T(8,128)(2,1)S(1)}, bf16[240,640]{1,0:T(8,128)(2,1)S(1)}, u32[]{:S(2)}, u32[]{:S(2)}) collective-permute-start(bf16[240,640]{1,0:T(8,128)(2,1)S(1)} %get-tuple-element.99), channel_id=1, source_target_pairs={{0,3},{1,0},{2,1},{3,2},{4,7},{5,4},{6,5},{7,6},{8,11},{9,8},{10,9... | collective-permute-start | bytes 921608 | tf_op jit(solution)/shard_map/ppermute | solution.py:632
  (61 other events, 1024.7 us)

commit v2 on v1

v2 whole, which is shorter than its diff:
```python
import functools

import jax
import jax.numpy as jnp
from jax import lax
from jax.experimental import pallas as pl
from jax.experimental.pallas import tpu as pltpu
from jax.sharding import PartitionSpec as P

D = 960
FF = 2560
HEADS = 15
KV_HEADS = 5
GROUP = HEADS // KV_HEADS
HEAD_DIM = 64
HALF = HEAD_DIM // 2
TILE = 256
QUAD = 4
DB = D // QUAD
FB = FF // QUAD
QB = D // QUAD
KB = KV_HEADS * HEAD_DIM // QUAD
ROWS = 128
SPARE = 16
QKV = QB + 2 * KB
QKV_ROWS = 208
LEAD = FB - 512
SKIP = DB - LEAD
NEG = -1e30
EPS = 1e-05
ROPE_BASE = 10000.0
BIG = 60 * 1024 * 1024

F32 = jnp.float32
BF16 = jnp.bfloat16


def nn(a, b):
    return jnp.dot(a, b, preferred_element_type=F32)


def nt(a, b):
    return lax.dot_general(a, b, (((1,), (1,)), ((), ())), preferred_element_type=F32)


def rope_tables(first, length):
    places = jnp.arange(length, dtype=jnp.int32)
    position = jnp.where(places < first, places, places - first).astype(F32)
    frequency = ROPE_BASE ** (-jnp.arange(0, HEAD_DIM, 2, dtype=F32) / HEAD_DIM)
    angles = frequency[:, None] * position[None, :]
    return jnp.cos(angles), jnp.sin(angles)


def params():
    return pltpu.CompilerParams(vmem_limit_bytes=BIG)


def any_spec():
    return pl.BlockSpec(memory_space=pl.ANY)


def by_plane_halved(pieces, k, kz):
    if k < 3:
        return pieces[k].at[kz]
    return pieces[3 + kz // 2].at[kz % 2]


def by_z(pieces, k, kz):
    return pieces[kz].at[k]


def copies(idx, pieces, pick, sems, target):
    plans = ([], [])
    mine, other = pieces[: len(pieces) // 2], pieces[len(pieces) // 2 :]
    for mine_core in range(2):
        slot = 0
        for core, found in ((mine_core, mine), (1 - mine_core, other)):
            for k in range(QUAD):
                for kz in range(QUAD):
                    ref = pick(found, k, kz)
                    for source, dest in target(core, idx[4 + kz], idx[k], kz):
                        src = ref if source is None else ref.at[pl.ds(*source), :]
                        plans[mine_core].append(
                            pltpu.make_async_copy(src, dest, sems.at[slot])
                        )
                        slot += 1
    return plans


def rows_target(weight, gains=None):
    def target(core, z, yx, kz):
        base = pl.multiple_of(yx * DB, 16)
        if core == 0:
            return [((0, ROWS), weight.at[z, pl.ds(base, ROWS), :])]
        found = [((SPARE, DB - ROWS), weight.at[z, pl.ds(base + ROWS, DB - ROWS), :])]
        if gains is not None and kz == 0:
            found.append(((0, SPARE), gains.at[yx]))
        return found

    return target


def down_target(weight):
    def target(core, z, yx, kz):
        base = pl.multiple_of(z * DB, 16)
        columns = pl.ds(pl.multiple_of(yx * FB, 128), FB)
        if core == 0:
            return [((0, ROWS), weight.at[pl.ds(base, ROWS), columns])]
        return [((SPARE, DB - ROWS), weight.at[pl.ds(base + ROWS, DB - ROWS), columns])]

    return target


def pair_target(weight):
    def target(core, z, yx, kz):
        base = pl.multiple_of(yx * DB, 16)
        columns = pl.ds(pl.multiple_of(z * FB, 128), FB)
        return [(None, weight.at[core, pl.ds(base, DB), columns])]

    return target


def run_copies(core, plans):
    for c in range(2):

        @pl.when(core == c)
        def _():
            for copy in plans[c]:
                copy.start()
            for copy in plans[c]:
                copy.wait()


def norm_columns(x, axis):
    return lax.rsqrt(jnp.mean(x * x, axis=axis, keepdims=True) + EPS)


def column(row):
    return jnp.broadcast_to(row, (128, row.shape[1])).T[:, 0:1]


def project(idx, xt_ref, cos_ref, sin_ref, *rest):
    weight, gain_ref, n1t_ref, qx_ref, kx_ref, kt_ref, vt_ref, gains, sems = rest[10:]
    run_copies(idx[8], copies(idx, rest[0:10], by_plane_halved, sems, rows_target(weight, gains)))
    length = xt_ref.shape[1]
    first = idx[9]
    gain_one = jnp.concatenate([gains[b, 0:1, 0:DB] for b in range(QUAD)], axis=1).astype(F32)
    gain_two = jnp.concatenate([gains[b, 0:1, 256 : 256 + DB] for b in range(QUAD)], axis=1).astype(F32)
    gain_ref[0:1, :] = gain_one
    gain_ref[1:2, :] = gain_two
    gain_column = column(gain_one)

    place = lax.broadcasted_iota(jnp.int32, (HEAD_DIM, length), 1)
    row = lax.broadcasted_iota(jnp.int32, (HEAD_DIM, length), 0)
    extra_q = jnp.where((row == 0) & (place >= first), NEG, 0.0).astype(BF16)
    extra_k = jnp.where((row == 0) & (place < first), 1.0, 0.0)
    for h in range(HEADS):
        qx_ref[h, HEAD_DIM:, :] = extra_q

    def tile(i, carry):
        at = pl.ds(pl.multiple_of(i * TILE, TILE), TILE)
        x = xt_ref[:, at].astype(F32)
        n1t = (x * norm_columns(x, 0) * gain_column).astype(BF16)
        n1t_ref[:, at] = n1t
        n1 = n1t.T
        cosine, sine = cos_ref[:, at], sin_ref[:, at]
        flat = [nn(n1, weight[z, :, LEAD:]).T for z in range(QUAD)]
        queries = jnp.concatenate([f[SKIP : SKIP + QB] for f in flat], axis=0)
        keys = jnp.concatenate([f[SKIP + QB : SKIP + QB + KB] for f in flat], axis=0)
        values = jnp.concatenate([f[SKIP + QB + KB :] for f in flat], axis=0)

        def turn(u):
            u1, u2 = u[:HALF], u[HALF:]
            return jnp.concatenate([u1 * cosine - u2 * sine, u2 * cosine + u1 * sine], axis=0).astype(BF16)

        for h in range(HEADS):
            qx_ref[h, 0:HEAD_DIM, at] = turn(queries[h * HEAD_DIM : (h + 1) * HEAD_DIM]) * jnp.asarray(0.125, BF16)
        for h in range(KV_HEADS):
            kt_ref[h, :, at] = turn(keys[h * HEAD_DIM : (h + 1) * HEAD_DIM])
        vt_ref[:, :, at] = values.astype(BF16).reshape(KV_HEADS, HEAD_DIM, TILE)
        return carry

    lax.fori_loop(0, length // TILE, tile, 0)
    for j in range(KV_HEADS):
        wide = jnp.concatenate([kt_ref[j].astype(F32), extra_k], axis=0)
        kx_ref[j] = wide.T.astype(BF16)


def call_project(idx, xt, cosine, sine, pieces):
    length = xt.shape[1]
    s = jax.ShapeDtypeStruct
    vm = pl.BlockSpec(memory_space=pltpu.VMEM)
    return pl.pallas_call(
        project,
        out_shape=(
            s((QUAD, D, FB), BF16),
            s((8, D), F32),
            s((D, length), BF16),
            s((HEADS, 2 * HEAD_DIM, length), BF16),
            s((KV_HEADS, length, 2 * HEAD_DIM), BF16),
            s((KV_HEADS, HEAD_DIM, length), BF16),
            s((KV_HEADS, HEAD_DIM, length), BF16),
        ),
        in_specs=[pl.BlockSpec(memory_space=pltpu.SMEM)] + [vm] * 3 + [any_spec()] * 10,
        out_specs=(vm,) * 7,
        scratch_shapes=[
            pltpu.VMEM((QUAD, SPARE, FB), BF16),
            pltpu.SemaphoreType.DMA((64,)),
        ],
        compiler_params=params(),
        name="project",
        cost_estimate=pl.CostEstimate(flops=600000000, bytes_accessed=2000000, transcendentals=0),
    )(idx, xt, cosine, sine, *pieces)


def causal_mask():
    return lax.broadcasted_iota(jnp.int32, (TILE, GROUP * TILE), 0) > (
        lax.broadcasted_iota(jnp.int32, (TILE, GROUP * TILE), 1) % TILE
    )


def attend(qx_ref, kx_ref, vt_ref, ot_ref, lse_ref):
    tiles = qx_ref.shape[2] // TILE
    causal = causal_mask()
    for b in range(tiles):
        at = slice(b * TILE, (b + 1) * TILE)
        qx = jnp.concatenate([qx_ref[g, :, at] for g in range(GROUP)], axis=1)
        scores = []
        for s in range(b + 1):
            raw = nn(kx_ref[0, s * TILE : (s + 1) * TILE, :], qx)
            scores.append(jnp.where(causal, NEG, raw) if s == b else raw)
        highest = functools.reduce(jnp.maximum, [jnp.max(s, axis=0, keepdims=True) for s in scores])
        total = 0.0
        out = 0.0
        for s in range(b + 1):
            weights = jnp.exp(scores[s] - highest)
            total = total + jnp.sum(weights, axis=0, keepdims=True)
            out = out + nn(vt_ref[0, :, s * TILE : (s + 1) * TILE], weights.astype(BF16))
        out = out / total
        lse_ref[0, b] = highest + jnp.log(total)
        for g in range(GROUP):
            ot_ref[g, :, at] = out[:, g * TILE : (g + 1) * TILE].astype(BF16)


def heads_spec(count, rows, length):
    return pl.BlockSpec((count, rows, length), lambda j: (j, 0, 0))


def call_attend(qx, kx, vt):
    length = qx.shape[2]
    tiles = length // TILE
    s = jax.ShapeDtypeStruct
    return pl.pallas_call(
        attend,
        out_shape=(
            s((HEADS, HEAD_DIM, length), BF16),
            s((KV_HEADS, tiles, 1, GROUP * TILE), F32),
        ),
        grid=(KV_HEADS,),
        in_specs=[
            heads_spec(GROUP, 2 * HEAD_DIM, length),
            heads_spec(1, length, 2 * HEAD_DIM),
            heads_spec(1, HEAD_DIM, length),
        ],
        out_specs=[
            heads_spec(GROUP, HEAD_DIM, length),
            pl.BlockSpec((1, tiles, 1, GROUP * TILE), lambda j: (j, 0, 0, 0)),
        ],
        compiler_params=params(),
        name="attend",
        cost_estimate=pl.CostEstimate(flops=2000000000, bytes_accessed=800000, transcendentals=0),
    )(qx, kx, vt)


def leave(xt_ref, gain_ref, weight, ot_ref, y_ref, n2_ref, n2t_ref):
    o = ot_ref[...].reshape(D, ot_ref.shape[2]).T
    added = jnp.concatenate([nn(o, weight[z, :, 0:256])[:, 0:DB] for z in range(QUAD)], axis=1)
    y = xt_ref[...].T.astype(F32) + added
    y_ref[...] = y
    n2 = (y * norm_columns(y, -1) * gain_ref[1:2, :]).astype(BF16)
    n2_ref[...] = n2
    n2t_ref[...] = n2.T


def call_leave(xt, gains, weight, ot):
    length = xt.shape[1]
    s = jax.ShapeDtypeStruct
    tall = pl.BlockSpec((D, TILE), lambda i: (0, i))
    wide = pl.BlockSpec((TILE, D), lambda i: (i, 0))
    return pl.pallas_call(
        leave,
        out_shape=(s((length, D), F32), s((length, D), BF16), s((D, length), BF16)),
        grid=(length // TILE,),
        in_specs=[
            tall,
            pl.BlockSpec((8, D), lambda i: (0, 0)),
            pl.BlockSpec((QUAD, D, FB), lambda i: (0, 0, 0)),
            pl.BlockSpec((HEADS, HEAD_DIM, TILE), lambda i: (0, 0, i)),
        ],
        out_specs=[wide, wide, tall],
        compiler_params=params(),
        name="leave",
        cost_estimate=pl.CostEstimate(flops=300000000, bytes_accessed=1500000, transcendentals=0),
    )(xt, gains, weight, ot)


def feed(idx, n2_ref, y_ref, ct_ref, gain_ref, *rest):
    pairs, downs = rest[0:10], rest[10:18]
    mixed_ref, h_ref, dgu_ref, dyt_ref, dat_ref, gg_ref, weight, down, sems = rest[18:]

    @pl.when(pl.program_id(0) == 0)
    def _():
        first = copies(idx, pairs, by_plane_halved, sems.at[0], pair_target(weight))
        second = copies(idx, downs, by_z, sems.at[1], down_target(down))
        run_copies(idx[8], [a + b for a, b in zip(first, second)])
        gg_ref[...] = jnp.zeros_like(gg_ref)

    n2 = n2_ref[...]
    chunks = [slice(b, b + FEED_CHUNK) for b in range(0, FF, FEED_CHUNK)]
    for at in chunks:
        g = nn(n2, weight[0, :, at])
        u = nn(n2, weight[1, :, at])
        sig = 1.0 / (1.0 + jnp.exp(-g))
        silu = g * sig
        h_ref[:, at] = (silu * u).astype(BF16)
        dgu_ref[0, :, at] = (u * (sig + silu * (1.0 - sig))).astype(BF16)
        dgu_ref[1, :, at] = silu.astype(BF16)
    y = y_ref[...]
    mixed_ref[...] = (y + nt(h_ref[...], down[...])).astype(BF16).T
    c = ct_ref[...].T
    for at in chunks:
        dh = nn(c, down[:, at])
        dgu_ref[0, :, at] = (dh * dgu_ref[0, :, at].astype(F32)).astype(BF16)
        dgu_ref[1, :, at] = (dh * dgu_ref[1, :, at].astype(F32)).astype(BF16)
    dn2 = nt(dgu_ref[0], weight[0]) + nt(dgu_ref[1], weight[1])
    r = norm_columns(y, -1)
    yr = y * r
    gg_ref[0:1, :] += jnp.sum(dn2 * yr, axis=0, keepdims=True)
    t = dn2 * gain_ref[1:2, :]
    dy = c.astype(F32) + r * (t - yr * jnp.mean(t * yr, axis=-1, keepdims=True))
    dyt = dy.T
    dyt_ref[...] = dyt
    dat_ref[...] = dyt.astype(BF16)


FEED_TILE = 512
FEED_CHUNK = 512


def call_feed(idx, n2, y, ct, gains, pairs, downs):
    length = n2.shape[0]
    s = jax.ShapeDtypeStruct
    wide = pl.BlockSpec((FEED_TILE, D), lambda i, p: (i, 0))
    tall = pl.BlockSpec((D, FEED_TILE), lambda i, p: (0, i))
    whole = pl.BlockSpec((8, D), lambda i, p: (0, 0))
    return pl.pallas_call(
        feed,
        out_shape=(
            s((D, length), BF16),
            s((length, FF), BF16),
            s((2, length, FF), BF16),
            s((D, length), F32),
            s((D, length), BF16),
            s((8, D), F32),
        ),
        grid_spec=pltpu.PrefetchScalarGridSpec(
            num_scalar_prefetch=1,
            grid=(length // FEED_TILE,),
            in_specs=[wide, wide, tall, whole] + [any_spec()] * 18,
            out_specs=[
                tall,
                pl.BlockSpec((FEED_TILE, FF), lambda i, p: (i, 0)),
                pl.BlockSpec((2, FEED_TILE, FF), lambda i, p: (0, i, 0)),
                tall,
                tall,
                whole,
            ],
            scratch_shapes=[
                pltpu.VMEM((2, D, FF), BF16),
                pltpu.VMEM((D, FF), BF16),
                pltpu.SemaphoreType.DMA((2, 64)),
            ],
        ),
        compiler_params=params(),
        name="feed_forward_backward",
        cost_estimate=pl.CostEstimate(flops=3000000000, bytes_accessed=5000000, transcendentals=0),
    )(idx, n2, y, ct, gains, *pairs, *downs)


def pair_grads(target, idx, n2t_ref, d_ref, *rest):
    full = rest[-1]
    received, outs = (rest[0:1], rest[1:-1]) if target == 0 else ((), rest[:-1])
    full[...] = nn(n2t_ref[...], d_ref[...])
    for k in range(QUAD):
        got = full[pl.ds(pl.multiple_of(idx[k] * DB, 16), DB), :]
        if received:
            got = got + received[0][k, 0].astype(F32)
        if len(outs) == 1:
            outs[0][k, 0] = got.astype(BF16)
        else:
            outs[k][0] = got.astype(BF16)


def call_pair_grads(idx, n2t, dgu, received=None):
    length = n2t.shape[1]
    s = jax.ShapeDtypeStruct
    block = pl.BlockSpec((QUAD, 1, DB, FB), lambda i, p: (0, i, 0, 0))
    matrix = 10 if received is None else 8
    specs = [
        pl.BlockSpec((D, length), lambda i, p: (0, 0)),
        pl.BlockSpec((None, length, FB), lambda i, p: (p[matrix], 0, p[4 + i])),
    ]
    if received is None:
        out_shape = [s((QUAD, QUAD, DB, FB), BF16)]
        out_specs = [block]
        extra = ()
    else:
        specs.append(block)
        extra = (received,)
        out_shape = [s((QUAD, DB, FB), BF16)] * QUAD
        out_specs = [pl.BlockSpec((1, DB, FB), lambda i, p: (i, 0, 0))] * QUAD
    return pl.pallas_call(
        functools.partial(pair_grads, 1 if received is None else 0),
        out_shape=out_shape,
        grid_spec=pltpu.PrefetchScalarGridSpec(
            num_scalar_prefetch=1,
            grid=(QUAD,),
            in_specs=specs,
            out_specs=out_specs,
            scratch_shapes=[pltpu.VMEM((D, FB), F32)],
        ),
        compiler_params=params(),
        name="pair_grads",
        cost_estimate=pl.CostEstimate(flops=500000000, bytes_accessed=1500000, transcendentals=0),
    )(idx, n2t, dgu, *extra)


WIDE = FB + 256


def down_grads(which, idx, ct_ref, h_ref, ot_ref, dat_ref, gg_ref, *rest):
    right, also = rest[-2:]
    received, outs = (rest[0:1], rest[1:-2]) if which == 8 else ((), rest[:-2])
    core = idx[which]
    k = pl.program_id(0)
    yx = idx[k]
    offset = core * (DB - ROWS)

    def rows(ref, block, size, shift):
        return ref[pl.ds(pl.multiple_of(block * DB + shift, 16), size), :]

    @pl.when(k == 0)
    def _():
        for kz in range(QUAD):
            right[kz * DB : (kz + 1) * DB, :] = rows(dat_ref, idx[4 + kz], DB, 0)
        left = jnp.concatenate([rows(ot_ref, idx[i], ROWS, offset) for i in range(QUAD)], axis=0)
        also[...] = nt(left, right[...]).reshape(QUAD, ROWS, D)

    left = jnp.concatenate([rows(ct_ref, idx[4 + kz], ROWS, offset) for kz in range(QUAD)], axis=0)
    full = nn(left, h_ref[...])
    spare = jnp.broadcast_to(gg_ref[yx, 0:1, :], (SPARE, FB))

    def put(ref, kz):
        got = full[kz * ROWS : (kz + 1) * ROWS]
        out = also[k, :, kz * DB : (kz + 1) * DB]
        head = jnp.where(core == 1, spare, got[0:SPARE])
        if received:
            got = got + received[0][0, kz, :, 0:FB].astype(F32)
            out = out + received[0][0, kz, :, FB : FB + DB].astype(F32)
            head = head + received[0][0, kz, 0:SPARE, 0:FB].astype(F32)
        ref[:, 0:FB] = got.astype(BF16)
        ref[:, FB : FB + DB] = out.astype(BF16)
        ref[:, FB + DB :] = jnp.zeros((ROWS, 256 - DB), BF16)
        ref[0:SPARE, 0:FB] = head.astype(BF16)

    if len(outs) == 1:
        for kz in range(QUAD):
            put(outs[0].at[0, kz], kz)
    else:
        for i in range(QUAD):

            @pl.when(k == i)
            def _():
                for kz in range(QUAD):
                    put(outs[i].at[kz], kz)


def call_down_grads(idx, ct, h, ot, dat, gg, received=None):
    length = ct.shape[1]
    s = jax.ShapeDtypeStruct
    block = pl.BlockSpec((1, QUAD, ROWS, WIDE), lambda i, p: (i, 0, 0, 0))
    vm = pl.BlockSpec((D, length), lambda i, p: (0, 0))
    specs = [
        vm,
        pl.BlockSpec((length, FB), lambda i, p: (0, p[i])),
        vm,
        vm,
        pl.BlockSpec((QUAD, 8, FB), lambda i, p: (0, 0, 0)),
    ]
    if received is None:
        out_shape, out_specs, extra = [s((QUAD, QUAD, ROWS, WIDE), BF16)], [block], ()
    else:
        specs.append(block)
        extra = (received,)
        out_shape = [s((QUAD, ROWS, WIDE), BF16)] * QUAD
        out_specs = [pl.BlockSpec((QUAD, ROWS, WIDE), lambda i, p: (0, 0, 0))] * QUAD
    return pl.pallas_call(
        functools.partial(down_grads, 10 if received is None else 8),
        out_shape=out_shape,
        grid_spec=pltpu.PrefetchScalarGridSpec(
            num_scalar_prefetch=1,
            grid=(QUAD,),
            in_specs=specs,
            out_specs=out_specs,
            scratch_shapes=[pltpu.VMEM((D, length), BF16), pltpu.VMEM((QUAD, ROWS, D), F32)],
        ),
        compiler_params=params(),
        name="down_grads",
        cost_estimate=pl.CostEstimate(flops=400000000, bytes_accessed=1500000, transcendentals=0),
    )(idx, ct, h, ot, dat, gg, *extra)


def give(weight, dat_ref, do_ref):
    total = 0.0
    for z in range(QUAD):
        total = total + nn(weight[z, :, 0:DB], dat_ref[z * DB : (z + 1) * DB, :])
    do_ref[...] = total.astype(BF16).reshape(do_ref.shape)


def call_give(weight, dat):
    length = dat.shape[1]
    return pl.pallas_call(
        give,
        out_shape=jax.ShapeDtypeStruct((HEADS, HEAD_DIM, length), BF16),
        grid=(length // FEED_TILE,),
        in_specs=[
            pl.BlockSpec((QUAD, D, 256), lambda i: (0, 0, 0)),
            pl.BlockSpec((D, FEED_TILE), lambda i: (0, i)),
        ],
        out_specs=pl.BlockSpec((HEADS, HEAD_DIM, FEED_TILE), lambda i: (0, 0, i)),
        compiler_params=params(),
        name="give",
        cost_estimate=pl.CostEstimate(flops=200000000, bytes_accessed=600000, transcendentals=0),
    )(weight, dat)


def unrotate(grads, cosine, sine):
    u1, u2 = grads[:HALF], grads[HALF:]
    return jnp.concatenate([u1 * cosine + u2 * sine, u2 * cosine - u1 * sine], axis=0)


def attend_backward(qx_ref, kx_ref, kt_ref, vt_ref, ot_ref, do_ref, lse_ref, cos_ref, sin_ref, zq, zk, zv, dk_s, dv_s):
    tiles = qx_ref.shape[2] // TILE
    causal = causal_mask()
    values = vt_ref[0].astype(F32).T.astype(BF16)
    for b in range(tiles):
        at = slice(b * TILE, (b + 1) * TILE)
        qx = jnp.concatenate([qx_ref[g, :, at] for g in range(GROUP)], axis=1)
        do = jnp.concatenate([do_ref[g, :, at] for g in range(GROUP)], axis=1)
        o = jnp.concatenate([ot_ref[g, :, at] for g in range(GROUP)], axis=1)
        inner = jnp.sum(do.astype(F32) * o.astype(F32), axis=0, keepdims=True)
        log_total = lse_ref[0, b]
        dq = 0.0
        for s in range(b + 1):
            keys = slice(s * TILE, (s + 1) * TILE)
            raw = nn(kx_ref[0, keys, :], qx)
            if s == b:
                raw = jnp.where(causal, NEG, raw)
            probs = jnp.exp(raw - log_total)
            dp = nn(values[keys, :], do)
            ds = (probs * (dp - inner)).astype(BF16)
            dq = dq + nn(kt_ref[0, :, keys], ds)
            dk = nt(ds, qx[0:HEAD_DIM, :])
            dv = nt(probs.astype(BF16), do)
            if s == b:
                dk_s[keys, :] = dk
                dv_s[keys, :] = dv
            else:
                dk_s[keys, :] += dk
                dv_s[keys, :] += dv
        cosine, sine = cos_ref[:, at], sin_ref[:, at]
        for g in range(GROUP):
            part = unrotate(dq[:, g * TILE : (g + 1) * TILE] * 0.125, cosine, sine)
            zq[g, :, at] = part.astype(BF16)
    zk[0] = unrotate(dk_s[...].T, cos_ref[...], sin_ref[...]).astype(BF16)
    zv[0] = dv_s[...].T.astype(BF16)


def call_attend_backward(start, count, qx, kx, kt, vt, ot, do, lse, cosine, sine):
    length = qx.shape[2]
    tiles = length // TILE
    s = jax.ShapeDtypeStruct

    def spec(heads, rows, lanes):
        return pl.BlockSpec((heads, rows, lanes), lambda j: (j + start, 0, 0))

    table = pl.BlockSpec((HALF, length), lambda j: (0, 0))
    return pl.pallas_call(
        attend_backward,
        out_shape=(
            s((GROUP * count, HEAD_DIM, length), BF16),
            s((count, HEAD_DIM, length), BF16),
            s((count, HEAD_DIM, length), BF16),
        ),
        grid=(count,),
        in_specs=[
            spec(GROUP, 2 * HEAD_DIM, length),
            spec(1, length, 2 * HEAD_DIM),
            spec(1, HEAD_DIM, length),
            spec(1, HEAD_DIM, length),
            spec(GROUP, HEAD_DIM, length),
            spec(GROUP, HEAD_DIM, length),
            pl.BlockSpec((1, tiles, 1, GROUP * TILE), lambda j: (j + start, 0, 0, 0)),
            table,
            table,
        ],
        out_specs=[
            heads_spec(GROUP, HEAD_DIM, length),
            heads_spec(1, HEAD_DIM, length),
            heads_spec(1, HEAD_DIM, length),
        ],
        scratch_shapes=[pltpu.VMEM((length, HEAD_DIM), F32), pltpu.VMEM((length, HEAD_DIM), F32)],
        compiler_params=params(),
        name="attend_backward",
        cost_estimate=pl.CostEstimate(flops=1000000000, bytes_accessed=1000000, transcendentals=0),
    )(qx, kx, kt, vt, ot, do, lse, cosine, sine)


def enter_backward(xt_ref, dyt_ref, gain_ref, weight, *rest):
    parts, (gx_ref, z_ref, gg_ref, sums) = rest[:-4], rest[-4:]
    i = pl.program_id(0)

    @pl.when(i == 0)
    def _():
        sums[...] = jnp.zeros_like(sums)

    def flat(found):
        return jnp.concatenate([ref[...].reshape(-1, TILE) for ref in found], axis=0)

    zq, zk, zv = flat(parts[0::3]), flat(parts[1::3]), flat(parts[2::3])
    dn1 = 0.0
    for z in range(QUAD):
        z_ref[z, 0:SKIP, :] = jnp.zeros((SKIP, TILE), BF16)
        z_ref[z, SKIP : SKIP + QB, :] = zq[z * QB : (z + 1) * QB]
        z_ref[z, SKIP + QB : SKIP + QB + KB, :] = zk[z * KB : (z + 1) * KB]
        z_ref[z, SKIP + QB + KB :, :] = zv[z * KB : (z + 1) * KB]
        dn1 = dn1 + nn(weight[z, :, LEAD:], z_ref[z])
    x = xt_ref[...].astype(F32)
    r = norm_columns(x, 0)
    xr = x * r
    found = dn1 * xr
    sums[...] += found[:, 0:128] + found[:, 128:256]
    t = dn1 * column(gain_ref[0:1, :])
    gx = dyt_ref[...] + r * (t - xr * jnp.mean(t * xr, axis=0, keepdims=True))
    gx_ref[...] = gx.astype(BF16)

    @pl.when(i == pl.num_programs(0) - 1)
    def _():
        gg_ref[...] = jnp.broadcast_to(jnp.sum(sums[...].T, axis=0, keepdims=True), gg_ref.shape)


def call_enter_backward(xt, dyt, gains, weight, *parts):
    length = xt.shape[1]
    s = jax.ShapeDtypeStruct
    tall = pl.BlockSpec((D, TILE), lambda i: (0, i))
    whole = pl.BlockSpec((8, D), lambda i: (0, 0))
    return pl.pallas_call(
        enter_backward,
        out_shape=(s((D, length), BF16), s((QUAD, 512, length), BF16), s((8, D), F32)),
        grid=(length // TILE,),
        in_specs=[tall, tall, whole, pl.BlockSpec((QUAD, D, FB), lambda i: (0, 0, 0))]
        + [pl.BlockSpec((part.shape[0], HEAD_DIM, TILE), lambda i: (0, 0, i)) for part in parts],
        out_specs=[tall, pl.BlockSpec((QUAD, 512, TILE), lambda i: (0, 0, i)), whole],
        scratch_shapes=[pltpu.VMEM((D, 128), F32)],
        compiler_params=params(),
        name="enter_backward",
        cost_estimate=pl.CostEstimate(flops=400000000, bytes_accessed=1500000, transcendentals=0),
    )(xt, dyt, gains, weight, *parts)


def qkv_grads(idx, z_ref, n1t_ref, gg_ref, theirs, *rest):
    mine, (right, full) = rest[0:QUAD], rest[QUAD:]

    @pl.when(pl.program_id(0) == 0)
    def _():
        for k in range(QUAD):
            right[k * DB : (k + 1) * DB, :] = n1t_ref[pl.ds(pl.multiple_of(idx[k] * DB, 16), DB), :]

    full[...] = nt(z_ref[SKIP:, :], right[...])
    for which in (10, 8):
        core = idx[which]
        part = full[pl.ds(pl.multiple_of(core * (QKV - QKV_ROWS), 16), QKV_ROWS), :]
        for k in range(QUAD):
            got = part[:, k * DB : (k + 1) * DB]
            spare = jnp.broadcast_to(gg_ref[idx[k], 0:1, :], (SPARE, DB))
            ref = theirs.at[k, 0] if which == 10 else mine[k].at[0]
            ref[...] = got.astype(BF16)
            ref[0:SPARE, :] = jnp.where(core == 1, spare, got[0:SPARE]).astype(BF16)


def call_qkv_grads(idx, z, n1t, gg):
    length = n1t.shape[1]
    s = jax.ShapeDtypeStruct
    return pl.pallas_call(
        qkv_grads,
        out_shape=[s((QUAD, QUAD, QKV_ROWS, DB), BF16)] + [s((QUAD, QKV_ROWS, DB), BF16)] * QUAD,
        grid_spec=pltpu.PrefetchScalarGridSpec(
            num_scalar_prefetch=1,
            grid=(QUAD,),
            in_specs=[
                pl.BlockSpec((None, 512, length), lambda i, p: (p[4 + i], 0, 0)),
                pl.BlockSpec((D, length), lambda i, p: (0, 0)),
                pl.BlockSpec((QUAD, 8, DB), lambda i, p: (0, 0, 0)),
            ],
            out_specs=[pl.BlockSpec((QUAD, 1, QKV_ROWS, DB), lambda i, p: (0, i, 0, 0))]
            + [pl.BlockSpec((1, QKV_ROWS, DB), lambda i, p: (i, 0, 0))] * QUAD,
            scratch_shapes=[pltpu.VMEM((D, length), BF16), pltpu.VMEM((QKV, D), F32)],
        ),
        compiler_params=params(),
        name="qkv_grads",
        cost_estimate=pl.CostEstimate(flops=300000000, bytes_accessed=1000000, transcendentals=0),
    )(idx, z, n1t, gg)


CORE = [(i, i ^ 1) for i in range(8)]
ALONG_X = [(i, i ^ 2) for i in range(8)]
ALONG_Y = [(i, i ^ 4) for i in range(8)]
ACROSS = [(i, i ^ 6) for i in range(8)]


def swap(values):
    return lax.ppermute(values, "fsdp", CORE)


def from_z(values, k):
    return lax.ppermute(values, "dp", [(j, (j - k) % QUAD) for j in range(QUAD)])


def to_z(values, k):
    return lax.ppermute(values, "dp", [(j, (j + k) % QUAD) for j in range(QUAD)])


def spread_z(piece):
    return (piece,) + tuple(from_z(piece, k) for k in range(1, QUAD))


def spread_sides(own):
    return (own, lax.ppermute(own, "fsdp", ALONG_X), lax.ppermute(own, "fsdp", ALONG_Y))


def spread_across(own, by_x, by_y):
    return (lax.ppermute(by_y[:2], "fsdp", ALONG_X), lax.ppermute(by_x[2:], "fsdp", ALONG_Y))


def spread_core(pieces):
    return tuple(swap(piece) for piece in pieces)


def add(parts):
    return functools.reduce(jnp.add, [part.astype(F32) for part in parts])


def swap_plane(blocks):
    return (
        blocks[0],
        lax.ppermute(blocks[1], "fsdp", ALONG_X),
        lax.ppermute(blocks[2], "fsdp", ALONG_Y),
        lax.ppermute(blocks[3], "fsdp", ACROSS),
    )


def swap_corner(block):
    half = block.shape[0] // 2
    return (lax.ppermute(block[:half], "fsdp", ALONG_X), lax.ppermute(block[half:], "fsdp", ALONG_Y))


def swap_sides(blocks, corner):
    half = blocks[1].shape[0] // 2
    to_x = jnp.concatenate([blocks[1][:half], add([blocks[1][half:], corner[1]]).astype(BF16)], axis=0)
    to_y = jnp.concatenate([add([blocks[2][:half], corner[0]]).astype(BF16), blocks[2][half:]], axis=0)
    return (blocks[0], lax.ppermute(to_x, "fsdp", ALONG_X), lax.ppermute(to_y, "fsdp", ALONG_Y))


def swap_z(blocks):
    return (blocks[0],) + tuple(to_z(blocks[k], k) for k in range(1, QUAD))


def slab(values, start, size, axis):
    return lax.dynamic_slice_in_dim(values, start, size, axis)


def tables(yx, z, core, first):
    entries = [yx ^ k for k in range(QUAD)] + [(z + k) % QUAD for k in range(QUAD)]
    entries += [core, first, 1 - core, 0, 0, 0, 0, 0]
    return jnp.stack([jnp.asarray(e, jnp.int32) for e in entries])


def gather_near(core, early, gain_attn, w_query, w_key, w_value, w_out, gain_mlp, w_gate, w_up, w_down):
    zero = core == 0
    rows = jnp.concatenate([w_out, w_query, w_key, w_value], axis=1)
    share = rows.shape[0]
    extra = ROWS - share
    pad = jnp.zeros((1, 256 - DB), BF16)
    gains = jnp.concatenate(
        [gain_attn[None], jnp.zeros((1, 256 - share), BF16), gain_mlp[None], jnp.zeros((1, FB - 256 - share), BF16)], axis=1
    )
    sent = jnp.concatenate([rows[0:extra], gains, jnp.zeros((SPARE - extra - 1, FB), BF16)], axis=0)
    taken = swap(sent)
    theirs = taken[extra : extra + 1]
    line = jnp.concatenate(
        [theirs[:, 0:share], gain_attn[None], pad, theirs[:, 256 : 256 + share], gain_mlp[None], jnp.zeros((1, FB - 256 - DB), BF16)],
        axis=1,
    )
    attn = jnp.where(
        zero,
        jnp.concatenate([rows, taken[0:extra]], axis=0),
        jnp.concatenate([jnp.broadcast_to(line, (SPARE, FB)), rows[extra:]], axis=0),
    )
    turned = w_down.T
    taken = swap(slab(turned, (1 - core) * (DB - ROWS), ROWS, 0))
    kept = slab(turned, core * (DB - ROWS), ROWS, 0)
    down = jnp.where(zero, jnp.concatenate([kept, taken], axis=1), jnp.concatenate([taken, kept], axis=1))
    taken = swap(jnp.where(zero, w_up, w_gate))
    pair = jnp.where(zero, jnp.concatenate([w_gate, taken], axis=0), jnp.concatenate([taken, w_up], axis=0))
    pair = spread_z(pair)
    attn = jnp.stack(spread_z(attn) + (down,))
    attn, early = lax.optimization_barrier((attn, early))
    sides = spread_sides(attn)
    return sides + spread_across(*sides), pair, early


def after(values, *others):
    return lax.optimization_barrier((values, others))[0]


def in_pieces(blocks):
    return (blocks[0], blocks[1], blocks[2], blocks[3, 0:2], blocks[3, 2:4])


def gather_any(gain_attn, w_query, w_key, w_value, w_out, gain_mlp, w_gate, w_up, w_down):
    def whole(weight):
        return lax.all_gather(lax.all_gather(weight, "dp", axis=1, tiled=True), "fsdp", axis=0, tiled=True)

    def blocks(weight):
        return weight.reshape(QUAD, weight.shape[0] // QUAD, QUAD, weight.shape[1] // QUAD).transpose(0, 2, 1, 3)

    attn = jnp.concatenate([blocks(whole(w)) for w in (w_out, w_query, w_key, w_value)], axis=3)
    gains = [lax.all_gather(g, "fsdp", axis=0, tiled=True).reshape(QUAD, 1, 1, DB) for g in (gain_attn, gain_mlp)]
    line = jnp.concatenate(
        [gains[0], jnp.zeros((QUAD, 1, 1, 256 - DB), BF16), gains[1], jnp.zeros((QUAD, 1, 1, FB - 256 - DB), BF16)], axis=3
    )
    line = jnp.broadcast_to(line, (QUAD, QUAD, SPARE, FB))
    attn_two = jnp.concatenate([line, attn[:, :, ROWS:]], axis=2)
    down = blocks(whole(w_down).T).transpose(1, 0, 2, 3)
    pair = [in_pieces(blocks(whole(w))) for w in (w_gate, w_up)]
    return (
        in_pieces(attn[:, :, 0:ROWS]) + in_pieces(attn_two),
        pair[0] + pair[1],
        tuple(down[:, z, 0:ROWS] for z in range(QUAD)) + tuple(down[:, z, DB - ROWS :] for z in range(QUAD)),
    )


def on_device(
    near,
    tokens,
    first_len,
    gain_attn,
    w_query,
    w_key,
    w_value,
    w_out,
    gain_mlp,
    w_gate,
    w_up,
    w_down,
    cotangent,
):
    length = tokens.shape[0]
    first = first_len[0]
    weights = (gain_attn, w_query, w_key, w_value, w_out, gain_mlp, w_gate, w_up, w_down)
    if near:
        place = lax.axis_index("fsdp")
        core = place & 1
        idx = tables(place >> 1, lax.axis_index("dp"), core, first)
        attn, pair, (idx, cosine, sine) = gather_near(core, (idx, *rope_tables(first, length)), *weights)
    else:
        core = 0
        idx = tables(0, 0, 0, first)
        attn, pair, down = gather_any(*weights)
        cosine, sine = rope_tables(first, length)
    xt, ct = tokens.T, cotangent.T
    if near:
        down = jnp.stack([attn[0][QUAD], attn[1][QUAD], attn[2][QUAD], attn[4][2]])
        attn = attn + spread_core(attn)
        pair = jnp.stack(pair)
        attn, pair, down = lax.optimization_barrier((attn, pair, down))
        pair = spread_sides(pair)
        down = spread_z(down)
    weight, gains, n1t, qx, kx, kt, vt = call_project(idx, xt, cosine, sine, attn)
    ot, lse = call_attend(qx, kx, vt)
    if near:
        pair, ot = lax.optimization_barrier((pair, ot))
        pair = pair + spread_across(*pair)
    y, n2, n2t = call_leave(xt, gains, weight, ot)
    if near:
        pair, down, n2 = lax.optimization_barrier((pair, down, n2))
        pair = pair + spread_core(pair)
        down = down + spread_core(down)
    mixed, h, dgu, dyt, dat, gain_two = call_feed(idx, n2, y, ct, gains, pair, down)

    halves = gain_two[0].reshape(QUAD, 1, 2, DB // 2)
    row = jnp.pad(halves, ((0, 0), (0, 7), (0, 0), (0, FB // 2 - DB // 2))).reshape(QUAD, 8, FB)
    args_down = (ct, h, ot.reshape(D, length), dat, row)
    pair_theirs = call_pair_grads(idx, n2t, dgu)[0]
    if near:
        came = swap(pair_theirs)
        args_down = after(args_down, pair_theirs)
    else:
        came = jnp.zeros_like(pair_theirs)
    down_theirs = call_down_grads(idx, *args_down)[0]
    if near:
        came_down = swap(down_theirs)
        came = after(came, down_theirs)
    else:
        came_down = jnp.zeros_like(down_theirs)
    pair_mine = call_pair_grads(idx, n2t, dgu, received=came)
    if near:
        pair_corner = swap_corner(pair_mine[3])
        came_down = after(came_down, pair_mine)
    down_mine = call_down_grads(idx, *args_down, received=came_down)
    if near:
        pair_corner, down_mine, dat = lax.optimization_barrier((pair_corner, down_mine, dat))
        pair_got = swap_sides(pair_mine, pair_corner)
        down_corner = swap_corner(down_mine[3])
    do = call_give(weight, dat)
    heads = (qx, kx, kt, vt, ot, do, lse, cosine, sine)
    first_part = call_attend_backward(0, 2, *heads)
    if near:
        heads = after(heads, first_part)
    second_part = call_attend_backward(2, 3, *heads)
    if near:
        pair_got, down_corner, second_part = lax.optimization_barrier((pair_got, down_corner, second_part))
        pair_got = swap_z(add(pair_got).astype(BF16))
        down_got = swap_sides(down_mine, down_corner)
    grad_tokens, turned, gain_one = call_enter_backward(xt, dyt, gains, weight, *first_part, *second_part)
    row = jnp.pad(gain_one[0].reshape(QUAD, 1, DB), ((0, 0), (0, 7), (0, 0)))
    qkv_theirs, *qkv_mine = call_qkv_grads(idx, turned, n1t, row)
    if near:
        pair_got, down_got, qkv_theirs = lax.optimization_barrier((pair_got, down_got, qkv_theirs))
        came = swap(qkv_theirs)
        qkv_got = swap_plane([add([part, came[k]]).astype(BF16) for k, part in enumerate(qkv_mine)])
        down_got = swap_z(add(down_got).astype(BF16))
        pair_sum = add(pair_got)
        qkv_got, down_got, pair_sum = lax.optimization_barrier((qkv_got, down_got, pair_sum))
        qkv_got = swap_z(add(qkv_got).astype(BF16))
        down_sum, qkv_sum = add(down_got), add(qkv_got)
        outs = settle_near(core, down_sum, pair_sum, qkv_sum)
    else:
        outs = settle_any(down_mine, down_theirs, pair_mine, pair_theirs, qkv_mine, qkv_theirs, gain_one[0], gain_two[0])
    return (mixed.T, grad_tokens.T) + outs


def settle_near(core, down_sum, pair_sum, qkv_sum):
    zero = core == 0
    share = DB // 2

    kept = slab(pair_sum, core * share, share, 0)
    taken = swap(slab(pair_sum, (1 - core) * share, share, 0).astype(BF16)).astype(F32)
    grad_gate, grad_up = jnp.where(zero, kept, taken), jnp.where(zero, taken, kept)

    grad_out = jnp.where(zero, down_sum[0:share, FB : FB + DB], down_sum[ROWS - share :, FB : FB + DB])
    half = FB // 2
    kept = slab(down_sum, core * half, half, 1)
    taken = swap(slab(down_sum, (1 - core) * half, half, 1).astype(BF16)).astype(F32)
    upper, lower = jnp.where(zero, kept, taken), jnp.where(zero, taken, kept)
    grad_down = jnp.concatenate([upper, lower[SPARE:]], axis=0).T
    grad_gain_mlp = lower[0, 0:share]

    kept = slab(qkv_sum, core * share, share, 1)
    taken = swap(slab(qkv_sum, (1 - core) * share, share, 1).astype(BF16)).astype(F32)
    upper, lower = jnp.where(zero, kept, taken), jnp.where(zero, taken, kept)
    grad_gain_attn = lower[0]
    rows = jnp.concatenate([upper, lower[SPARE:]], axis=0).T
    return (
        grad_gain_attn, rows[:, 0:QB], rows[:, QB : QB + KB], rows[:, QB + KB :], grad_out,
        grad_gain_mlp, grad_gate, grad_up, grad_down,
    )


def settle_any(down_mine, down_theirs, pair_mine, pair_theirs, qkv_mine, qkv_theirs, gain_one, gain_two):
    def whole(blocks):
        return blocks.transpose(0, 2, 1, 3).reshape(blocks.shape[0] * blocks.shape[2], -1)

    def shard(values):
        values = lax.psum_scatter(values, "fsdp", scatter_dimension=0, tiled=True)
        return lax.psum_scatter(values, "dp", scatter_dimension=1, tiled=True).astype(F32)

    def gain(values):
        values = lax.psum(values, "dp")
        return lax.psum_scatter(values, "fsdp", scatter_dimension=0, tiled=True)

    both = jnp.concatenate([jnp.stack(down_mine), down_theirs[:, :, SPARE:]], axis=2)
    grad_down = shard(whole(both[..., 0:FB].transpose(1, 0, 2, 3)).T)
    grad_out = shard(whole(both[..., FB : FB + DB]))
    grad_gate, grad_up = shard(whole(jnp.stack(pair_mine))), shard(whole(pair_theirs))
    both = jnp.concatenate([jnp.stack(qkv_mine), qkv_theirs[:, :, SPARE:]], axis=2).transpose(0, 1, 3, 2)
    grad_query = shard(whole(both[..., 0:QB]))
    grad_key = shard(whole(both[..., QB : QB + KB]))
    grad_value = shard(whole(both[..., QB + KB :]))
    return (
        gain(gain_one), grad_query, grad_key, grad_value, grad_out, gain(gain_two), grad_gate, grad_up, grad_down,
    )


def solution(mesh):
    sizes = dict(mesh.shape)
    near = sizes["fsdp"] == 8 and sizes["dp"] == QUAD
    in_specs = (
        P(("fsdp", "dp"), None),
        P(("fsdp", "dp")),
        P("fsdp"),
        P("fsdp", "dp"),
        P("fsdp", "dp"),
        P("fsdp", "dp"),
        P("fsdp", "dp"),
        P("fsdp"),
        P("fsdp", "dp"),
        P("fsdp", "dp"),
        P("fsdp", "dp"),
        P(("fsdp", "dp"), None),
    )
    out_specs = (
        P(("fsdp", "dp"), None),
        P(("fsdp", "dp"), None),
        P("fsdp"),
        P("fsdp", "dp"),
        P("fsdp", "dp"),
        P("fsdp", "dp"),
        P("fsdp", "dp"),
        P("fsdp"),
        P("fsdp", "dp"),
        P("fsdp", "dp"),
        P("fsdp", "dp"),
    )
    return jax.shard_map(
        functools.partial(on_device, near), mesh=mesh, in_specs=in_specs, out_specs=out_specs, check_vma=False
    )
```

time: 516 us -> 396 us (0.77)
  waiting for transfers between devices: 188 us -> 85 us
  starting transfers between devices: 68.2 us -> 52.5 us
  other arithmetic: 14.8 us -> 22.7 us
  local copies, waits for them, and re-layouts: 32 us -> 25.7 us
    ppermute x21 -> x19, waiting for transfers between devices: 93.3 us -> 19 us  [the longest x2 11.2 us: spread_sides(): lax.ppermute(own, 'fsdp', ALONG_X)]
    ppermute x9, waiting for transfers between devices: 44.4 us -> 26.1 us  [to_z(): lax.ppermute(values, 'dp', [(j, (j + k) % QUAD) for j in range(QUAD)])]
    ppermute x9, waiting for transfers between devices: 42.3 us -> 28.6 us  [from_z(): lax.ppermute(values, 'dp', [(j, (j - k) % QUAD) for j in range(QUAD)])]
    unnamed x68 -> x97, local copies, waits for them, and re-layouts: 19.9 us -> 8.47 us
    ppermute x24 -> x23, starting transfers between devices: 21.8 us -> 11.4 us  [swap(): return lax.ppermute(values, 'fsdp', CORE)]
    ppermute x21 -> x19, starting transfers between devices: 22.1 us -> 15.2 us  [the longest x2 2.53 us: spread_across(): lax.ppermute(by_x[2:], 'fsdp', ALONG_Y)]
    ppermute x24 -> x23, waiting for transfers between devices: 8.5 us -> 11.3 us  [swap(): return lax.ppermute(values, 'fsdp', CORE)]
    pallas_call x5 -> x9, Pallas kernels: 156 us -> 156 us  [the longest x1 50.1 us: call_feed(): pl.pallas_call(feed, out_shape=(s((D, length), BF16), s((length, FF), BF1...]
  transfers between devices with their start and end apart: 63 -> 60, of which waited for: 29 -> 22; matrix products, arithmetic and copies ran while one was open for 7% -> 8% of each run, Pallas kernels for 27% -> 36%
where the time goes in v2:
time: 396 us; the launch traced here: 391 us
  Pallas kernels  203 us (51%)
  waiting for transfers between devices  85 us (21%)
  starting transfers between devices  52.5 us (13%)
  local copies, waits for them, and re-layouts  25.7 us (6%)
  other arithmetic  22.7 us (6%)
    pallas_call x1, Pallas kernels, call_feed(): pl.pallas_call(feed, out_shape=(s((D, length), BF16), s((length, FF), BF1...  50.1 us
    pallas_call x2, Pallas kernels, call_attend_backward(): pl.pallas_call(attend_backward, out_shape=(s((GROUP * count, HEAD_DIM, le...  35.1 us
    ppermute x9, waiting for transfers between devices, from_z(): lax.ppermute(values, 'dp', [(j, (j - k) % QUAD) for j in range(QUAD)])  28.6 us
    ppermute x9, waiting for transfers between devices, to_z(): lax.ppermute(values, 'dp', [(j, (j + k) % QUAD) for j in range(QUAD)])  26.1 us
    pallas_call x2, Pallas kernels, call_down_grads(): pl.pallas_call(functools.partial(down_grads, 10 if received is None else...  24 us
    pallas_call x2, Pallas kernels, call_pair_grads(): pl.pallas_call(functools.partial(pair_grads, 1 if received is None else 0...  23.2 us
    pallas_call x1, Pallas kernels, call_attend(): pl.pallas_call(attend, out_shape=(s((HEADS, HEAD_DIM, length), BF16), s((...  18 us
    pallas_call x1, Pallas kernels, call_project(): pl.pallas_call(project, out_shape=(s((QUAD, D, FB), BF16), s((8, D), F32)...  16.2 us
  transfers between devices with their start and end apart: 60, of which 22 were waited for; matrix products, arithmetic and copies ran while one was open for 8% of the time, Pallas kernels for 36%

profile of v2, /device:TPU:9, one launch (start us, length us, event | category | flops | bytes accessed | tf_op | source)
XLA Modules:
  0.0 391.1 jit_solution(13252994286026457983)
XLA Ops:
  9.7 2.5 collective-permute-start.2
  14.5 8.4 %collective-permute-done.2 = bf16[128,640]{1,0:T(8,128)(2,1)S(1)} collective-permute-done((bf16[128,640]{1,0:T(8,128)(2,1)S(1)}, bf16[128,640]{1,0:T(8,128)(2,1)S(1)}, u32[]{:S(2)}, u32[]{:S(2)}) %collective-permute-start.2) | collective-permute-done | bytes 163872 | tf_op jit(solution)/shard_map/ppermute | solution.py:736
  22.9 3.5 collective-permute-done.3
  32.0 2.8 collective-permute-start.16
  34.8 11.2 %collective-permute-done.5.rest_1_ = bf16[5,128,640]{2,1,0:T(8,128)(2,1)S(1)} collective-permute-done((bf16[5,128,640]{2,1,0:T(8,128)(2,1)S(1)}, bf16[5,128,640]{2,1,0:T(8,128)(2,1)S(1)}, u32[]{:S(2)}, u32[]{:S(2)}) %collective-permute-start.5) | collective-permute-done | bytes 819232 | tf_op jit(solution)/shard_map/ppermute | solution.py:748
  48.9 3.3 collective-permute-done.16
  52.9 5.9 %collective-permute-done.17 = bf16[240,640]{1,0:T(8,128)(2,1)S(1)} collective-permute-done((bf16[240,640]{1,0:T(8,128)(2,1)S(1)}, bf16[240,640]{1,0:T(8,128)(2,1)S(1)}, u32[]{:S(2)}, u32[]{:S(2)}) %collective-permute-start.17) | collective-permute-done | bytes 307232 | tf_op jit(solution)/shard_map/ppermute | solution.py:736
  59.8 7.8 %collective-permute-done.7.rest_3_ = bf16[2,128,640]{2,1,0:T(8,128)(2,1)S(1)} collective-permute-done((bf16[2,128,640]{2,1,0:T(8,128)(2,1)S(1)}, bf16[2,128,640]{2,1,0:T(8,128)(2,1)S(1)}, u32[]{:S(2)}, u32[]{:S(2)}) %collective-permute-start.7) | collective-permute-done | bytes 327712 | tf_op jit(solution)/shard_map/ppermute | solution.py:752
  72.1 4.1 %collective-permute-start.22 = (bf16[4,128,640]{2,1,0:T(8,128)(2,1)}, bf16[4,128,640]{2,1,0:T(8,128)(2,1)}, u32[]{:S(2)}, u32[]{:S(2)}) collective-permute-start(bf16[4,128,640]{2,1,0:T(8,128)(2,1)} %pad_maximum_fusion.5.rest_10_), channel_id=1, source_target_pairs={{0,3},{1,0},{2,1},{3,2},{4,7},{5,4},{6,5},{7,6},{8,11},{9,8},{10,9... | collective-permute-start | bytes 1966088 | tf_op jit(solution)/shard_map/ppermute | solution.py:736
  77.6 16.2 %project.1 = (bf16[4,960,640]{2,1,0:T(8,128)(2,1)}, f32[8,960]{1,0:T(8,128)}, bf16[960,1024]{1,0:T(8,128)(2,1)}, bf16[15,128,1024]{2,1,0:T(8,128)(2,1)}, bf16[5,...) custom-call(s32[16]{0:T(128)} %stack.77.idx, bf16[960,1024]{1,0:T(8,128)(2,1)} %bitcast.100, ...), custom_call_target="tpu_custom_call" | custom-call | flops 600000000 | bytes 2000000 | tf_op jit(solution)/shard_map/project/pallas_call | solution.py:193
  93.8 18.0 %attend.1 = (bf16[15,64,1024]{2,1,0:T(8,128)(2,1)}, f32[5,4,1,768]{3,2,1,0:T(1,128)}) custom-call(bf16[15,128,1024]{2,1,0:T(8,128)(2,1)} %get-tuple-element.198.qx_ref, bf16[5,1024,128]{2,1,0:T(8,128)(2,1)} %get-tuple-element.199.kx_ref, bf16[5,64,1024]{2,1,0:T(8,128)(2,1)} %get-tuple-element.201.vt_ref), custom_call_target="tpu_custom_call" | custom-call | flops 2000000000 | bytes 800000 | tf_op jit(solution)/shard_map/attend/pallas_call | solution.py:253
  115.9 9.3 %leave.1 = (f32[1024,960]{1,0:T(8,128)}, bf16[1024,960]{1,0:T(8,128)(2,1)}, bf16[960,1024]{1,0:T(8,128)(2,1)}) custom-call(bf16[960,1024]{1,0:T(8,128)(2,1)} %bitcast.101, f32[8,960]{1,0:T(8,128)} %get-tuple-element.152.gain_ref, bf16[4,960,640]{2,1,0:T(8,128)(2,1)} %get-tuple-element.153.weight, bf16[15,64,1024]{2,1,0:T(8,128)(2,1)} %get-tuple-element.202.ot_ref), custom_call_target="tpu_custom_call" | custom-call | flops 300000000 | bytes 1500000 | tf_op jit(solution)/shard_map/leave/pallas_call | solution.py:290
  125.3 7.6 %collective-permute-done.24.rest_13_ = bf16[4,128,640]{2,1,0:T(8,128)(2,1)} collective-permute-done((bf16[4,128,640]{2,1,0:T(8,128)(2,1)}, bf16[4,128,640]{2,1,0:T(8,128)(2,1)}, u32[]{:S(2)}, u32[]{:S(2)}) %collective-permute-start.24) | collective-permute-done | bytes 655392 | tf_op jit(solution)/shard_map/ppermute | solution.py:736
  146.0 50.1 %feed_forward_backward.1 = (bf16[960,1024]{1,0:T(8,128)(2,1)}, bf16[1024,2560]{1,0:T(8,128)(2,1)}, bf16[2,1024,2560]{2,1,0:T(8,128)(2,1)}, f32[960,1024]{1,0:T(8...) custom-call(s32[16]{0:T(128)} %stack.77.idx, bf16[1024,960]{1,0:T(8,128)(2,1)} %get-tuple-element.156.n2_ref, ...), custom_call_target="tpu_custom_call" | custom-call | flops 3000000000 | bytes 5000000 | tf_op jit(solution)/shard_map/feed_forward_backward/pallas_call | solution.py:356
  196.1 11.1 %pair_grads.2 = bf16[4,4,240,640]{3,2,1,0:T(8,128)(2,1)} custom-call(s32[16]{0:T(128)} %stack.77.idx, bf16[960,1024]{1,0:T(8,128)(2,1)} %get-tuple-element.170.n2t_ref, bf16[2,1024,2560]{2,1,0:T(8,128)(2,1)} %get-tuple-element.171.d_ref), custom_call_target="tpu_custom_call" | custom-call | flops 500000000 | bytes 1500000 | tf_op jit(solution)/shard_map/pair_grads/pallas_call | solution.py:422
  209.2 10.8 %down_grads.2 = bf16[4,4,128,896]{3,2,1,0:T(8,128)(2,1)} custom-call(s32[16]{0:T(128)} %stack.77.idx, bf16[960,1024]{1,0:T(8,128)(2,1)} %bitcast.104, bf16[1024,2560]{1,0:T(8,128)(2,1)} %get-tuple-element.176.h_ref, bf16[960,1024]{1,0:T(8,128)(2,1)} %bitcast.98, bf16[960,1024]{1,0:T(8,128)(2,1)} %get-tuple-element.190.dat_ref, f32[4,8,640]{2,1,0:T(8,128)} %reshape.234.gg_ref), custom_call_target="tpu_custom_call" | custom-call | flops 400000000 | bytes 1500000 | tf_op jit(solution)/shard_map/down_grads/pallas_call | solution.py:507
  220.1 12.2 %pair_grads.3 = (bf16[4,240,640]{2,1,0:T(8,128)(2,1)}, bf16[4,240,640]{2,1,0:T(8,128)(2,1)}, bf16[4,240,640]{2,1,0:T(8,128)(2,1)}, bf16[4,240,640]{2,1,0:T(8,128)(2,1)}) custom-call(s32[16]{0:T(128)} %stack.77.idx, bf16[960,1024]{1,0:T(8,128)(2,1)} %get-tuple-element.170.n2t_ref, bf16[2,1024,2560]{2,1,0:T(8,128)(2,1)} %get-tuple-element.171.d_ref, ...), custom_call_target="tpu_custom_call" | custom-call | flops 500000000 | bytes 1500000 | tf_op jit(solution)/shard_map/pair_grads/pallas_call | solution.py:422
  232.3 2.5 fusion.8
  240.7 13.2 %down_grads.3 = (bf16[4,128,896]{2,1,0:T(8,128)(2,1)}, bf16[4,128,896]{2,1,0:T(8,128)(2,1)}, bf16[4,128,896]{2,1,0:T(8,128)(2,1)}, bf16[4,128,896]{2,1,0:T(8,128)(2,1)}) custom-call(s32[16]{0:T(128)} %stack.77.idx, bf16[960,1024]{1,0:T(8,128)(2,1)} %bitcast.105, bf16[1024,2560]{1,0:T(8,128)(2,1)} %get-tuple-element.176.h_ref, bf16[960,1024]{1,0:T(8,128)(2,1)} %bitcast.99, ...), custom_call_target="tpu_custom_call" | custom-call | flops 400000000 | bytes 1500000 | tf_op jit(solution)/shard_map/down_grads/pallas_call | solution.py:507
  262.9 5.2 %give.1.do_ref = bf16[15,64,1024]{2,1,0:T(8,128)(2,1)} custom-call(bf16[4,960,640]{2,1,0:T(8,128)(2,1)} %get-tuple-element.153.weight, bf16[960,1024]{1,0:T(8,128)(2,1)} %get-tuple-element.190.dat_ref), custom_call_target="tpu_custom_call" | custom-call | flops 200000000 | bytes 600000 | tf_op jit(solution)/shard_map/give/pallas_call | solution.py:532
  268.1 14.6 %attend_backward.2 = (bf16[6,64,1024]{2,1,0:T(8,128)(2,1)}, bf16[2,64,1024]{2,1,0:T(8,128)(2,1)}, bf16[2,64,1024]{2,1,0:T(8,128)(2,1)}) custom-call(bf16[15,128,1024]{2,1,0:T(8,128)(2,1)} %get-tuple-element.198.qx_ref, bf16[5,1024,128]{2,1,0:T(8,128)(2,1)} %get-tuple-element.199.kx_ref, bf16[5,64,1024]{2,1,0:T(8,128)(2,1)} %get-tuple-element.200.kt_ref, ...), custom_call_target="tpu_custom_call" | custom-call | flops 1000000000 | bytes 1000000 | tf_op jit(solution)/shard_map/attend_backward/pallas_call | solution.py:598
  284.1 20.5 %attend_backward.3 = (bf16[9,64,1024]{2,1,0:T(8,128)(2,1)}, bf16[3,64,1024]{2,1,0:T(8,128)(2,1)}, bf16[3,64,1024]{2,1,0:T(8,128)(2,1)}) custom-call(bf16[15,128,1024]{2,1,0:T(8,128)(2,1)} %get-tuple-element.198.qx_ref, bf16[5,1024,128]{2,1,0:T(8,128)(2,1)} %get-tuple-element.199.kx_ref, bf16[5,64,1024]{2,1,0:T(8,128)(2,1)} %get-tuple-element.200.kt_ref, ...), custom_call_target="tpu_custom_call" | custom-call | flops 1000000000 | bytes 1000000 | tf_op jit(solution)/shard_map/attend_backward/pallas_call | solution.py:598
  311.7 2.4 collective-permute-start.42
  315.4 12.0 %enter_backward.1 = (bf16[960,1024]{1,0:T(8,128)(2,1)}, bf16[4,512,1024]{2,1,0:T(8,128)(2,1)}, f32[8,960]{1,0:T(8,128)}) custom-call(bf16[960,1024]{1,0:T(8,128)(2,1)} %bitcast.102, f32[960,1024]{1,0:T(8,128)} %get-tuple-element.168.dyt_ref, f32[8,960]{1,0:T(8,128)} %get-tuple-element.152.gain_ref, bf16[4,960,640]{2,1,0:T(8,128)(2,1)} %get-tuple-element.153.weight, ...), custom_call_target="tpu_custom_call" | custom-call | flops 400000000 | bytes 1500000 | tf_op jit(solution)/shard_map/enter_backward/pallas_call | solution.py:667
  328.9 9.7 %qkv_grads.1 = (bf16[4,4,208,240]{3,2,1,0:T(8,128)(2,1)}, bf16[4,208,240]{2,1,0:T(8,128)(2,1)}, bf16[4,208,240]{2,1,0:T(8,128)(2,1)}, bf16[4,208,240]{2,1,0:T(8,128)(2,1)}, bf16[4,208,240]{2,1,0:T(8,128)(2,1)}) custom-call(s32[16]{0:T(128)} %stack.77.idx, bf16[4,512,1024]{2,1,0:T(8,128)(2,1)} %get-tuple-element.214.z_ref, ...), custom_call_target="tpu_custom_call" | custom-call | flops 300000000 | bytes 1000000 | tf_op jit(solution)/shard_map/qkv_grads/pallas_call | solution.py:704
  338.6 3.4 collective-permute-done.44
  349.2 2.6 collective-permute-start.52
  352.2 2.9 collective-permute-start.53
  356.4 10.7 %collective-permute-done.52 = bf16[128,896]{1,0:T(8,128)(2,1)S(1)} collective-permute-done((bf16[128,896]{1,0:T(8,128)(2,1)}, bf16[128,896]{1,0:T(8,128)(2,1)S(1)}, u32[]{:S(2)}, u32[]{:S(2)}) %collective-permute-start.52) | collective-permute-done | bytes 229408 | tf_op jit(solution)/shard_map/ppermute | solution.py:740
  367.1 2.6 collective-permute-done.53
  377.7 5.0 %collective-permute-done.55 = bf16[208,240]{1,0:T(8,128)(2,1)S(1)} collective-permute-done((bf16[208,240]{1,0:T(8,128)(2,1)S(1)}, bf16[208,240]{1,0:T(8,128)(2,1)S(1)}, u32[]{:S(2)}, u32[]{:S(2)}) %collective-permute-start.55) | collective-permute-done | bytes 99872 | tf_op jit(solution)/shard_map/ppermute | solution.py:740
  382.7 3.6 collective-permute-done.56
  (283 shorter events, 93.1 us)
Async XLA Ops:
  6.2 20.2 %collective-permute-start.4 = (bf16[128,320]{1,0:T(8,128)(2,1)S(1)}, bf16[128,320]{1,0:T(8,128)(2,1)S(1)}, u32[]{:S(2)}, u32[]{:S(2)}) collective-permute-start(bf16[128,320]{1,0:T(8,128)(2,1)S(1)} %bitcast.113), channel_id=1, source_target_pairs={{0,4},{4,0},{8,12},{12,8},{16,20},{20,16},{24,28},{28,24},{1,5},{5... | collective-permute-start | bytes 245768 | tf_op jit(solution)/shard_map/ppermute | solution.py:732
  26.6 19.4 %collective-permute-start.5 = (bf16[5,128,640]{2,1,0:T(8,128)(2,1)S(1)}, bf16[5,128,640]{2,1,0:T(8,128)(2,1)S(1)}, u32[]{:S(2)}, u32[]{:S(2)}) collective-permute-start(bf16[5,128,640]{2,1,0:T(8,128)(2,1)S(1)} %fusion.7.rest_0_), channel_id=1, source_target_pairs={{0,8},{4,12},{8,0},{12,4},{16,24},{20,28},{24,16},{28,20},{1,9},{5... | collective-permute-start | bytes 2457608 | tf_op jit(solution)/shard_map/ppermute | solution.py:748
  27.8 24.9 %collective-permute-start.6 = (bf16[5,128,640]{2,1,0:T(8,128)(2,1)S(1)}, bf16[5,128,640]{2,1,0:T(8,128)(2,1)S(1)}, u32[]{:S(2)}, u32[]{:S(2)}) collective-permute-start(bf16[5,128,640]{2,1,0:T(8,128)(2,1)S(1)} %fusion.7.rest_0_), channel_id=1, source_target_pairs={{0,16},{4,20},{8,24},{12,28},{16,0},{20,4},{24,8},{28,12},{1,17},{... | collective-permute-start | bytes 2457608 | tf_op jit(solution)/shard_map/ppermute | solution.py:748
  32.0 20.2 %collective-permute-start.16 = (bf16[240,640]{1,0:T(8,128)(2,1)S(1)}, bf16[240,640]{1,0:T(8,128)(2,1)S(1)}, u32[]{:S(2)}, u32[]{:S(2)}) collective-permute-start(bf16[240,640]{1,0:T(8,128)(2,1)S(1)} %maximum_select_fusion.1), channel_id=1, source_target_pairs={{0,2},{1,3},{2,0},{3,1},{4,6},{5,7},{6,4},{7,5},{8,10},{9,11},{10,... | collective-permute-start | bytes 921608 | tf_op jit(solution)/shard_map/ppermute | solution.py:736
  34.7 24.0 %collective-permute-start.17 = (bf16[240,640]{1,0:T(8,128)(2,1)S(1)}, bf16[240,640]{1,0:T(8,128)(2,1)S(1)}, u32[]{:S(2)}, u32[]{:S(2)}) collective-permute-start(bf16[240,640]{1,0:T(8,128)(2,1)S(1)} %maximum_select_fusion.1), channel_id=1, source_target_pairs={{0,1},{1,2},{2,3},{3,0},{4,5},{5,6},{6,7},{7,4},{8,9},{9,10},{10,1... | collective-permute-start | bytes 921608 | tf_op jit(solution)/shard_map/ppermute | solution.py:736
  47.3 23.2 %collective-permute-start.9 = (bf16[5,128,640]{2,1,0:T(8,128)(2,1)S(1)}, bf16[5,128,640]{2,1,0:T(8,128)(2,1)S(1)}, u32[]{:S(2)}, u32[]{:S(2)}) collective-permute-start(bf16[5,128,640]{2,1,0:T(8,128)(2,1)S(1)} %fusion.7.rest_0_), channel_id=1, source_target_pairs={{0,4},{4,0},{8,12},{12,8},{16,20},{20,16},{24,28},{28,24},{1,5},{5... | collective-permute-start | bytes 2457608 | tf_op jit(solution)/shard_map/ppermute | solution.py:732
  52.2 18.3 %collective-permute-start.10 = (bf16[5,128,640]{2,1,0:T(8,128)(2,1)S(1)}, bf16[5,128,640]{2,1,0:T(8,128)(2,1)S(1)}, u32[]{:S(2)}, u32[]{:S(2)}) collective-permute-start(bf16[5,128,640]{2,1,0:T(8,128)(2,1)S(1)} %collective-permute-done.5.rest_1_), channel_id=1, source_target_pairs={{0,4},{4,0},{8,12},{12,8},{16,20},{20,16},{24,28},{28,24},{1,5},{5... | collective-permute-start | bytes 2457608 | tf_op jit(solution)/shard_map/ppermute | solution.py:732
  52.8 17.7 %collective-permute-start.11 = (bf16[5,128,640]{2,1,0:T(8,128)(2,1)S(1)}, bf16[5,128,640]{2,1,0:T(8,128)(2,1)S(1)}, u32[]{:S(2)}, u32[]{:S(2)}) collective-permute-start(bf16[5,128,640]{2,1,0:T(8,128)(2,1)S(1)} %collective-permute-done.6.rest_2_), channel_id=1, source_target_pairs={{0,4},{4,0},{8,12},{12,8},{16,20},{20,16},{24,28},{28,24},{1,5},{5... | collective-permute-start | bytes 2457608 | tf_op jit(solution)/shard_map/ppermute | solution.py:732
  71.5 40.4 %collective-permute-start.18 = (bf16[4,240,640]{2,1,0:T(8,128)(2,1)S(1)}, bf16[4,240,640]{2,1,0:T(8,128)(2,1)S(1)}, u32[]{:S(2)}, u32[]{:S(2)}) collective-permute-start(bf16[4,240,640]{2,1,0:T(8,128)(2,1)S(1)} %pad_maximum_fusion.rest_0_), channel_id=1, source_target_pairs={{0,8},{4,12},{8,0},{12,4},{16,24},{20,28},{24,16},{28,20},{1,9},{5... | collective-permute-start | bytes 3686408 | tf_op jit(solution)/shard_map/ppermute | solution.py:748
  71.8 40.1 %collective-permute-start.19 = (bf16[4,240,640]{2,1,0:T(8,128)(2,1)S(1)}, bf16[4,240,640]{2,1,0:T(8,128)(2,1)S(1)}, u32[]{:S(2)}, u32[]{:S(2)}) collective-permute-start(bf16[4,240,640]{2,1,0:T(8,128)(2,1)S(1)} %pad_maximum_fusion.rest_0_), channel_id=1, source_target_pairs={{0,16},{4,20},{8,24},{12,28},{16,0},{20,4},{24,8},{28,12},{1,17},{... | collective-permute-start | bytes 3686408 | tf_op jit(solution)/shard_map/ppermute | solution.py:748
  72.1 53.2 %collective-permute-start.22 = (bf16[4,128,640]{2,1,0:T(8,128)(2,1)}, bf16[4,128,640]{2,1,0:T(8,128)(2,1)}, u32[]{:S(2)}, u32[]{:S(2)}) collective-permute-start(bf16[4,128,640]{2,1,0:T(8,128)(2,1)} %pad_maximum_fusion.5.rest_10_), channel_id=1, source_target_pairs={{0,3},{1,0},{2,1},{3,2},{4,7},{5,4},{6,5},{7,6},{8,11},{9,8},{10,9... | collective-permute-start | bytes 1966088 | tf_op jit(solution)/shard_map/ppermute | solution.py:736
  76.3 49.0 %collective-permute-start.23 = (bf16[4,128,640]{2,1,0:T(8,128)(2,1)}, bf16[4,128,640]{2,1,0:T(8,128)(2,1)}, u32[]{:S(2)}, u32[]{:S(2)}) collective-permute-start(bf16[4,128,640]{2,1,0:T(8,128)(2,1)} %pad_maximum_fusion.5.rest_10_), channel_id=1, source_target_pairs={{0,2},{1,3},{2,0},{3,1},{4,6},{5,7},{6,4},{7,5},{8,10},{9,11},{10,... | collective-permute-start | bytes 1966088 | tf_op jit(solution)/shard_map/ppermute | solution.py:736
  76.3 56.7 %collective-permute-start.24 = (bf16[4,128,640]{2,1,0:T(8,128)(2,1)}, bf16[4,128,640]{2,1,0:T(8,128)(2,1)}, u32[]{:S(2)}, u32[]{:S(2)}) collective-permute-start(bf16[4,128,640]{2,1,0:T(8,128)(2,1)} %pad_maximum_fusion.5.rest_10_), channel_id=1, source_target_pairs={{0,1},{1,2},{2,3},{3,0},{4,5},{5,6},{6,7},{7,4},{8,9},{9,10},{10,1... | collective-permute-start | bytes 1966088 | tf_op jit(solution)/shard_map/ppermute | solution.py:736
  112.9 20.1 %collective-permute-start.20 = (bf16[2,240,640]{2,1,0:T(8,128)(2,1)}, bf16[2,240,640]{2,1,0:T(8,128)(2,1)}, u32[]{:S(2)}, u32[]{:S(2)}) collective-permute-start(bf16[2,240,640]{2,1,0:T(8,128)(2,1)} %slice.170), channel_id=1, source_target_pairs={{0,8},{4,12},{8,0},{12,4},{16,24},{20,28},{24,16},{28,20},{1,9},{5... | collective-permute-start | bytes 1843208 | tf_op jit(solution)/shard_map/ppermute | solution.py:752
  114.7 18.2 %collective-permute-start.21 = (bf16[2,240,640]{2,1,0:T(8,128)(2,1)}, bf16[2,240,640]{2,1,0:T(8,128)(2,1)}, u32[]{:S(2)}, u32[]{:S(2)}) collective-permute-start(bf16[2,240,640]{2,1,0:T(8,128)(2,1)} %slice.171), channel_id=1, source_target_pairs={{0,16},{4,20},{8,24},{12,28},{16,0},{20,4},{24,8},{28,12},{1,17},{... | collective-permute-start | bytes 1843208 | tf_op jit(solution)/shard_map/ppermute | solution.py:752
  220.0 18.9 %collective-permute-start.37 = (bf16[4,4,128,896]{3,2,1,0:T(8,128)(2,1)}, bf16[4,4,128,896]{3,2,1,0:T(8,128)(2,1)S(1)}, u32[]{:S(2)}, u32[]{:S(2)}) collective-permute-start(bf16[4,4,128,896]{3,2,1,0:T(8,128)(2,1)} %down_grads.2), channel_id=1, source_target_pairs={{0,4},{4,0},{8,12},{12,8},{16,20},{20,16},{24,28},{28,24},{1,5},{5... | collective-permute-start | bytes 11010056 | tf_op jit(solution)/shard_map/ppermute | solution.py:732
  234.8 19.1 %collective-permute-start.35 = (bf16[2,240,640]{2,1,0:T(8,128)(2,1)}, bf16[2,240,640]{2,1,0:T(8,128)(2,1)}, u32[]{:S(2)}, u32[]{:S(2)}) collective-permute-start(bf16[2,240,640]{2,1,0:T(8,128)(2,1)} %get-tuple-element.267), channel_id=1, source_target_pairs={{0,8},{4,12},{8,0},{12,4},{16,24},{20,28},{24,16},{28,20},{1,9},{5... | collective-permute-start | bytes 1843208 | tf_op jit(solution)/shard_map/ppermute | solution.py:774
  235.9 18.0 %collective-permute-start.36 = (bf16[2,240,640]{2,1,0:T(8,128)(2,1)}, bf16[2,240,640]{2,1,0:T(8,128)(2,1)}, u32[]{:S(2)}, u32[]{:S(2)}) collective-permute-start(bf16[2,240,640]{2,1,0:T(8,128)(2,1)} %get-tuple-element.266), channel_id=1, source_target_pairs={{0,16},{4,20},{8,24},{12,28},{16,0},{20,4},{24,8},{28,12},{1,17},{... | collective-permute-start | bytes 1843208 | tf_op jit(solution)/shard_map/ppermute | solution.py:774
  256.7 48.0 %collective-permute-start.39 = (bf16[4,240,640]{2,1,0:T(8,128)(2,1)}, bf16[4,240,640]{2,1,0:T(8,128)(2,1)S(1)}, u32[]{:S(2)}, u32[]{:S(2)}) collective-permute-start(bf16[4,240,640]{2,1,0:T(8,128)(2,1)} %pad_maximum_fusion.2), channel_id=1, source_target_pairs={{0,16},{4,20},{8,24},{12,28},{16,0},{20,4},{24,8},{28,12},{1,17},{... | collective-permute-start | bytes 3686408 | tf_op jit(solution)/shard_map/ppermute | solution.py:781
  259.6 45.0 %collective-permute-start.38 = (bf16[4,240,640]{2,1,0:T(8,128)(2,1)}, bf16[4,240,640]{2,1,0:T(8,128)(2,1)S(1)}, u32[]{:S(2)}, u32[]{:S(2)}) collective-permute-start(bf16[4,240,640]{2,1,0:T(8,128)(2,1)} %pad_maximum_fusion.1), channel_id=1, source_target_pairs={{0,8},{4,12},{8,0},{12,4},{16,24},{20,28},{24,16},{28,20},{1,9},{5... | collective-permute-start | bytes 3686408 | tf_op jit(solution)/shard_map/ppermute | solution.py:781
  260.7 43.9 %collective-permute-start.40 = (bf16[2,128,896]{2,1,0:T(8,128)(2,1)}, bf16[2,128,896]{2,1,0:T(8,128)(2,1)}, u32[]{:S(2)}, u32[]{:S(2)}) collective-permute-start(bf16[2,128,896]{2,1,0:T(8,128)(2,1)} %get-tuple-element.273), channel_id=1, source_target_pairs={{0,8},{4,12},{8,0},{12,4},{16,24},{20,28},{24,16},{28,20},{1,9},{5... | collective-permute-start | bytes 1376264 | tf_op jit(solution)/shard_map/ppermute | solution.py:774
  261.9 42.7 %collective-permute-start.41 = (bf16[2,128,896]{2,1,0:T(8,128)(2,1)S(1)}, bf16[2,128,896]{2,1,0:T(8,128)(2,1)}, u32[]{:S(2)}, u32[]{:S(2)}) collective-permute-start(bf16[2,128,896]{2,1,0:T(8,128)(2,1)S(1)} %get-tuple-element.272), channel_id=1, source_target_pairs={{0,16},{4,20},{8,24},{12,28},{16,0},{20,4},{24,8},{28,12},{1,17},{... | collective-permute-start | bytes 1376264 | tf_op jit(solution)/shard_map/ppermute | solution.py:774
  307.0 35.0 %collective-permute-start.46 = (bf16[4,128,896]{2,1,0:T(8,128)(2,1)}, bf16[4,128,896]{2,1,0:T(8,128)(2,1)S(1)}, u32[]{:S(2)}, u32[]{:S(2)}) collective-permute-start(bf16[4,128,896]{2,1,0:T(8,128)(2,1)} %pad_maximum_fusion.4), channel_id=1, source_target_pairs={{0,16},{4,20},{8,24},{12,28},{16,0},{20,4},{24,8},{28,12},{1,17},{... | collective-permute-start | bytes 2752520 | tf_op jit(solution)/shard_map/ppermute | solution.py:781
  309.7 32.3 %collective-permute-start.45 = (bf16[4,128,896]{2,1,0:T(8,128)(2,1)}, bf16[4,128,896]{2,1,0:T(8,128)(2,1)}, u32[]{:S(2)}, u32[]{:S(2)}) collective-permute-start(bf16[4,128,896]{2,1,0:T(8,128)(2,1)} %pad_maximum_fusion.3), channel_id=1, source_target_pairs={{0,8},{4,12},{8,0},{12,4},{16,24},{20,28},{24,16},{28,20},{1,9},{5... | collective-permute-start | bytes 2752520 | tf_op jit(solution)/shard_map/ppermute | solution.py:781
  311.7 26.9 %collective-permute-start.42 = (bf16[240,640]{1,0:T(8,128)(2,1)}, bf16[240,640]{1,0:T(8,128)(2,1)S(1)}, u32[]{:S(2)}, u32[]{:S(2)}) collective-permute-start(bf16[240,640]{1,0:T(8,128)(2,1)} %get-tuple-element.264), channel_id=1, source_target_pairs={{0,1},{1,2},{2,3},{3,0},{4,5},{5,6},{6,7},{7,4},{8,9},{9,10},{10,1... | collective-permute-start | bytes 921608 | tf_op jit(solution)/shard_map/ppermute | solution.py:740
  314.1 24.5 %collective-permute-start.43 = (bf16[240,640]{1,0:T(8,128)(2,1)}, bf16[240,640]{1,0:T(8,128)(2,1)S(1)}, u32[]{:S(2)}, u32[]{:S(2)}) collective-permute-start(bf16[240,640]{1,0:T(8,128)(2,1)} %get-tuple-element.263), channel_id=1, source_target_pairs={{0,2},{1,3},{2,0},{3,1},{4,6},{5,7},{6,4},{7,5},{8,10},{9,11},{10,... | collective-permute-start | bytes 921608 | tf_op jit(solution)/shard_map/ppermute | solution.py:740
  314.3 27.7 %collective-permute-start.44 = (bf16[240,640]{1,0:T(8,128)(2,1)}, bf16[240,640]{1,0:T(8,128)(2,1)S(1)}, u32[]{:S(2)}, u32[]{:S(2)}) collective-permute-start(bf16[240,640]{1,0:T(8,128)(2,1)} %get-tuple-element.262), channel_id=1, source_target_pairs={{0,3},{1,0},{2,1},{3,2},{4,7},{5,4},{6,5},{7,6},{8,11},{9,8},{10,9... | collective-permute-start | bytes 921608 | tf_op jit(solution)/shard_map/ppermute | solution.py:740
  346.5 23.2 %collective-permute-start.48 = (bf16[4,208,240]{2,1,0:T(8,128)(2,1)S(1)}, bf16[4,208,240]{2,1,0:T(8,128)(2,1)S(1)}, u32[]{:S(2)}, u32[]{:S(2)}) collective-permute-start(bf16[4,208,240]{2,1,0:T(8,128)(2,1)S(1)} %get-tuple-element.260), channel_id=1, source_target_pairs={{0,8},{4,12},{8,0},{12,4},{16,24},{20,28},{24,16},{28,20},{1,9},{5... | collective-permute-start | bytes 1198088 | tf_op jit(solution)/shard_map/ppermute | solution.py:766
  347.4 22.2 %collective-permute-start.49 = (bf16[4,208,240]{2,1,0:T(8,128)(2,1)S(1)}, bf16[4,208,240]{2,1,0:T(8,128)(2,1)}, u32[]{:S(2)}, u32[]{:S(2)}) collective-permute-start(bf16[4,208,240]{2,1,0:T(8,128)(2,1)S(1)} %get-tuple-element.259), channel_id=1, source_target_pairs={{0,16},{4,20},{8,24},{12,28},{16,0},{20,4},{24,8},{28,12},{1,17},{... | collective-permute-start | bytes 1198088 | tf_op jit(solution)/shard_map/ppermute | solution.py:767
  348.4 21.2 %collective-permute-start.50 = (bf16[4,208,240]{2,1,0:T(8,128)(2,1)S(1)}, bf16[4,208,240]{2,1,0:T(8,128)(2,1)}, u32[]{:S(2)}, u32[]{:S(2)}) collective-permute-start(bf16[4,208,240]{2,1,0:T(8,128)(2,1)S(1)} %get-tuple-element.258), channel_id=1, source_target_pairs={{0,24},{4,28},{8,16},{12,20},{16,8},{20,12},{24,0},{28,4},{1,25},{... | collective-permute-start | bytes 1198088 | tf_op jit(solution)/shard_map/ppermute | solution.py:768
  349.2 17.9 %collective-permute-start.52 = (bf16[128,896]{1,0:T(8,128)(2,1)}, bf16[128,896]{1,0:T(8,128)(2,1)S(1)}, u32[]{:S(2)}, u32[]{:S(2)}) collective-permute-start(bf16[128,896]{1,0:T(8,128)(2,1)} %get-tuple-element.269), channel_id=1, source_target_pairs={{0,2},{1,3},{2,0},{3,1},{4,6},{5,7},{6,4},{7,5},{8,10},{9,11},{10,... | collective-permute-start | bytes 688136 | tf_op jit(solution)/shard_map/ppermute | solution.py:740
  372.1 18.0 %collective-permute-start.59 = (bf16[120,640]{1,0:T(8,128)(2,1)S(1)}, bf16[120,640]{1,0:T(8,128)(2,1)S(1)}, u32[]{:S(2)}, u32[]{:S(2)}) collective-permute-start(bf16[120,640]{1,0:T(8,128)(2,1)S(1)} %dynamic-slice_convert_fusion), channel_id=1, source_target_pairs={{0,4},{4,0},{8,12},{12,8},{16,20},{20,16},{24,28},{28,24},{1,5},{5... | collective-permute-start | bytes 460808 | tf_op jit(solution)/shard_map/ppermute | solution.py:732
  (72 other events, 575.8 us)
